TPU v7x, 32 devices: a whole 2x2x4 slice. The times are simulated.
32 devices in a mesh: batch: 8 (over y, x, core), seq: 4 (over z).
Axes of the slice: x: 2, y: 2, z: 4, core: 2. Of those that a mesh axis runs over, the one named last changes fastest.
Arguments:
- inputs: bfloat16 [16, 1728, 1024], P('batch', 'seq'), may hold values from -6 to 6
- timesteps: int32 [16], P('batch'), may hold values from 0 to 4999
- segments: int32 [16, 1728], P('batch'), may hold values from 0 to 13, as said below
- cotangent: bfloat16 [16, 1728, 1024], P('batch', 'seq'), may hold values from -6 to 6
- w_qkv: bfloat16 [1024, 3072], replicated, may hold values from -0.1875 to 0.1875
- b_query: bfloat16 [1024], replicated, may hold values from -3 to 3
- b_value: bfloat16 [1024], replicated, may hold values from -3 to 3
- w_out: bfloat16 [1024, 1024], replicated, may hold values from -1.5 to 1.5
- b_out: bfloat16 [1024], replicated, may hold values from -3 to 3
- ln1_gain: bfloat16 [1024], replicated, may hold values from 0.25 to 1.75
- ln1_bias: bfloat16 [1024], replicated, may hold values from -3 to 3
- w_up: bfloat16 [1024, 4096], replicated, may hold values from -0.1875 to 0.1875
- b_up: bfloat16 [4096], replicated, may hold values from -3 to 3
- w_down: bfloat16 [4096, 1024], replicated, may hold values from -0.09375 to 0.09375
- b_down: bfloat16 [1024], replicated, may hold values from -3 to 3
- ln2_gain: bfloat16 [1024], replicated, may hold values from 0.25 to 1.75
- ln2_bias: bfloat16 [1024], replicated, may hold values from -3 to 3
- w_time: bfloat16 [1024], replicated, may hold values from -4 to 4
- b_time: bfloat16 [1024], replicated, may hold values from -3 to 3
Outputs:
- output: bfloat16 [16, 1728, 1024], P('batch', 'seq')
- grad_inputs: bfloat16 [16, 1728, 1024], P('batch', 'seq')
- grad_w_qkv: float32 [1024, 3072], P(('batch', 'seq'))
- grad_b_query: float32 [1024], P(('batch', 'seq'))
- grad_b_value: float32 [1024], P(('batch', 'seq'))
- grad_w_out: float32 [1024, 1024], P(('batch', 'seq'))
- grad_b_out: float32 [1024], P(('batch', 'seq'))
- grad_ln1_gain: float32 [1024], P(('batch', 'seq'))
- grad_ln1_bias: float32 [1024], P(('batch', 'seq'))
- grad_w_up: float32 [1024, 4096], P(('batch', 'seq'))
- grad_b_up: float32 [4096], P(('batch', 'seq'))
- grad_w_down: float32 [4096, 1024], P(('batch', 'seq'))
- grad_b_down: float32 [1024], P(('batch', 'seq'))
- grad_ln2_gain: float32 [1024], P(('batch', 'seq'))
- grad_ln2_bias: float32 [1024], P(('batch', 'seq'))
- grad_w_time: float32 [1024], P(('batch', 'seq'))
- grad_b_time: float32 [1024], P(('batch', 'seq'))
Inputs may be any that keep to these rules, and one draw needn't show every extreme that they name: `segments`: in each sequence the ids rise by one from item to item, starting at 1 at position 0, over the first 1664 positions; the last 64 positions carry 0. Items are 512 or 128 positions long, except that in each index of batch one sequence is a single item. Padding positions attend only to padding.
All inputs are finite; a program needn't handle non-finite values.
Results may differ from a plain program's by a relative error of at most 0.014.
Values may be sent and summed in bfloat16 or wider, within the bound.
No kernel may reach another device: no remote copies, remote signals or barrier semaphores. Data moves between devices by JAX's collectives and lax.ppermute only.
A program may use at most 256 MiB of HBM per device.

v0:
```python
import functools

import jax
import jax.numpy as jnp
from jax import lax
from jax.experimental import pallas as pl
from jax.experimental.pallas import tpu as pltpu
from jax.sharding import PartitionSpec as P

D = 1024
HEADS = 16
TSTEPS = 5000
AXES = ("batch", "seq")


BF=jnp.bfloat16; F32=jnp.float32
NT=(((1,),(1,)),((),())); NN=(((1,),(0,)),((),())); TN=(((0,),(0,)),((),()))
def dot(a,b,d): return lax.dot_general(a,b,d,preferred_element_type=F32)
PHASE=1
FILLED=1664; PAD=64
def lanes(rows):
    return lax.broadcasted_iota(jnp.int32,(rows,128),1)
def parts3(x):
    a=x.astype(BF).astype(F32); r=x-a; b=r.astype(BF).astype(F32); c=r-b
    return a,b,c
def augment(base,h,x,lane):
    a,b,c=parts3(x)
    o=(1-h)*64
    f=base.astype(F32)
    f=jnp.where((lane>=o)&(lane<o+64),jnp.where(lane==o,a,jnp.where(lane==o+1,b,jnp.where(lane==o+2,c,0.0))),f)
    return f.astype(BF)
def ones3(base,h,lane,n=3):
    o=(1-h)*64
    f=base.astype(F32)
    f=jnp.where((lane>=o)&(lane<o+64),jnp.where(lane<o+n,1.0,0.0),f)
    return f.astype(BF)
def spread(base,h,x,lane):
    a=x.astype(BF).astype(F32); r=x-a; b=r.astype(BF).astype(F32); c=r-b
    o=(1-h)*64
    f=jnp.where(lane==o,a,jnp.where(lane==o+1,b,jnp.where(lane==o+2,c,0.0)))
    return jnp.where((lane//64)==h,base.astype(F32),f).astype(BF)
def fwd_tiles(tasks,lane):
    scores=[]
    for q,k,vs,keep in tasks:
        for h in (0,1):
            qh=jnp.where((lane//64)==h,q.astype(F32),0.0).astype(BF)
            s=dot(qh,k,NT)
            scores.append(s if keep is None else jnp.where(keep,s,-1e30))
    tops=[];outs=[]
    depth=PHASE
    n=len(scores)
    def soft(i):
        m=jnp.max(scores[i],axis=1,keepdims=True)
        tops.append(m)
        return jnp.exp2(scores[i]-m).astype(BF)
    ps=[]
    for i in range(n+depth):
        if i<n: ps.append(soft(i))
        if i>=depth: outs.append(dot(ps[i-depth],tasks[(i-depth)//2][2][(i-depth)%2],NN))
    done=[]
    for t,(q,_,_,_) in enumerate(tasks):
        os=[];augs=[]
        for h in (0,1):
            o=outs[2*t+h]
            os.append(o/pltpu.roll(o,64,1))
            augs.append(spread(q,h,-(tops[2*t+h]+jnp.log2(o)),lane))
        done.append((jnp.where(lane<64,os[0],os[1]),augs))
    return done
def fwd_store(refs,rows,o,augs):
    o_ref,ol_ref,qa_ref=refs
    o_ref[rows,:]=o.astype(BF)
    ol_ref[rows,:]=(o-o.astype(BF).astype(F32)).astype(BF)
    for h in (0,1): qa_ref[h,rows,:]=augs[h]
def fwd_kernel(bq,info,q_ref,k_ref,v_ref,*refs):
    *refs,vs_ref=refs
    single=info[0]==1
    @pl.when(single)
    def _():
        v=v_ref[0:FILLED,:]
        for h in (0,1): vs_ref[h,...]=ones3(v,h,lanes(FILLED),64)
        lq=lanes(bq)
        @pl.loop(0,FILLED//bq)
        def _(r):
            rows=pl.ds(pl.multiple_of(r*bq,bq),bq)
            (o,augs),=fwd_tiles([(q_ref[rows,:],k_ref[0:FILLED,:],(vs_ref[0],vs_ref[1]),None)],lq)
            fwd_store(refs,rows,o,augs)
    @pl.when(info[0]==2)
    def _():
        lq=lanes(128)
        each=[slice(i*128,i*128+128) for i in range(13)]
        tasks=[(q_ref[r,:],k_ref[r,:],[ones3(v_ref[r,:],h,lq,64) for h in (0,1)],None) for r in each]
        for r,(o,augs) in zip(each,fwd_tiles(tasks,lq)): fwd_store(refs,r,o,augs)
    @pl.when(info[0]==0)
    def _():
        col=lax.broadcasted_iota(jnp.int32,(128,512),1)
        lw=lanes(512); lq=lanes(128)
        @pl.loop(0,13)
        def _(i):
            lo=info[1+i]; hi=info[14+i]
            at=jnp.minimum(lo,9)
            window=pl.ds(pl.multiple_of(at*128,128),512)
            k=k_ref[window,:]; v=v_ref[window,:]
            vs=[ones3(v,h,lw,64) for h in (0,1)]
            keep=(col>=(lo-at)*128)&(col<(hi-at)*128)
            rows=pl.ds(pl.multiple_of(i*128,128),128)
            (o,augs),=fwd_tiles([(q_ref[rows,:],k,vs,keep)],lq)
            fwd_store(refs,rows,o,augs)
    rows=slice(FILLED,FILLED+PAD)
    lp=lanes(PAD)
    v=v_ref[rows,:]
    (o,augs),=fwd_tiles([(q_ref[rows,:],k_ref[rows,:],[ones3(v,h,lp,64) for h in (0,1)],None)],lp)
    fwd_store(refs,rows,o,augs)
def attn_fwd(info,qkv,first,count,bq=832):
    L,W3=qkv.shape; n=W3//384
    spec=lambda j: pl.BlockSpec((L,128),lambda p,s,j=j:(0,p+first+j*n))
    one=pl.BlockSpec((L,128),lambda p,s:(0,p))
    return pl.pallas_call(functools.partial(fwd_kernel,bq),
        out_shape=(jax.ShapeDtypeStruct((L,count*128),BF),)*2+(jax.ShapeDtypeStruct((2*count,L,128),BF),),
        grid_spec=pltpu.PrefetchScalarGridSpec(num_scalar_prefetch=1,grid=(count,),
            in_specs=[spec(0),spec(1),spec(2)],
            out_specs=(one,one,pl.BlockSpec((2,L,128),lambda p,s:(p,0,0))),
            scratch_shapes=[pltpu.VMEM((2,FILLED,128),BF)]),
        compiler_params=pltpu.CompilerParams(vmem_limit_bytes=50<<20),name="attn_forward",
        cost_estimate=pl.CostEstimate(flops=8*count*L*L*256,bytes_accessed=10*L*count*128,transcendentals=2*count*L*L))(info,qkv,qkv,qkv)
def deltas(g,o,ol,lane):
    prod=g.astype(F32)*(o.astype(F32)+ol.astype(F32))
    return [augment(g,h,-jnp.sum(jnp.where((lane//64)==h,prod,0.0),axis=1,keepdims=True),lane) for h in (0,1)]
def bwd_tiles(tasks,lane,turned=None):
    khs=[ones3(t[1],t[4],lane) for t in tasks]
    ps=[dot(kh,t[0],NT) for kh,t in zip(khs,tasks)]
    ds=[dot(ones3(t[2],t[4],lane),t[3],NT) for t in tasks]
    done=[]
    for kh,p,d,(qa,_,_,ga,h,keep) in zip(khs,ps,ds,tasks):
        p=jnp.exp2(p)
        if keep is not None: p=jnp.where(keep,p,0.0)
        d=(p*d).astype(BF)
        done.append((kh,p.astype(BF),d,qa,ga))
    back=lambda i,kh,d: dot(d,kh,TN) if turned is None else dot(turned[i*64:i*64+64,:],d,NN)
    return [(back(i,kh,d),dot(d,qa,NN),dot(p,ga,NN)) for i,(kh,p,d,qa,ga) in enumerate(done)]
LN2=0.6931471805599453
def both(a,lane): return jnp.where(lane<64,a[0],a[1])
def bwd_alone(each,lane,qa_ref,k_ref,v_ref,o_ref,ol_ref,g_ref,dq_ref,dk_ref,dv_ref):
    tasks=[]
    for r in each:
        gas=deltas(g_ref[r,:],o_ref[r,:],ol_ref[r,:],lane)
        tasks+=[(qa_ref[h,r,:],k_ref[r,:],v_ref[r,:],gas[h],h,None) for h in (0,1)]
    got=bwd_tiles(tasks,lane)
    for i,r in enumerate(each):
        x,y=got[2*i],got[2*i+1]
        dq_ref[r,:]=(both((x[0],y[0]),lane)*0.125).astype(BF)
        dk_ref[r,:]=(both((x[1],y[1]),lane)*LN2).astype(BF)
        dv_ref[r,:]=both((x[2],y[2]),lane).astype(BF)
def bwd_kernel(bk,joined,info,qa_ref,k_ref,v_ref,o_ref,ol_ref,g_ref,*rest):
    d_ref,sum_ref,acc,acc_k,acc_v,ga_ref=rest[1:] if joined else rest
    dq_ref,dk_ref,dv_ref=d_ref.at[0],d_ref.at[1],d_ref.at[2]
    tile_refs=(qa_ref,k_ref,v_ref,o_ref,ol_ref,g_ref,dq_ref,dk_ref,dv_ref)
    single=info[0]==1
    @pl.when(single)
    def _():
        lf=lanes(FILLED)
        gas=deltas(g_ref[0:FILLED,:],o_ref[0:FILLED,:],ol_ref[0:FILLED,:],lf)
        acc[...]=jnp.zeros_like(acc)
        lb=lanes(bk)
        ga_ref[0,...]=gas[0]; ga_ref[1,...]=gas[1]
        @pl.loop(0,FILLED//bk)
        def _(r):
            rows=pl.ds(pl.multiple_of(r*bk,bk),bk)
            k=k_ref[rows,:]; v=v_ref[rows,:]
            dks=[];dvs=[]
            got=bwd_tiles([(qa_ref[h,0:FILLED,:],k,v,ga_ref[h],h,None) for h in (0,1)],lb,k.astype(F32).T.astype(BF))
            for h in (0,1):
                dq,dk,dv=got[h]
                acc[h*64:h*64+64,:]+=dq
                dks.append(dk); dvs.append(dv)
            dk_ref[rows,:]=(both(dks,lb)*LN2).astype(BF)
            dv_ref[rows,:]=both(dvs,lb).astype(BF)
        dq_ref[0:FILLED,:]=(acc[...].T*0.125).astype(BF)
    @pl.when(info[0]==2)
    def _():
        lq=lanes(128)
        bwd_alone([slice(i*128,i*128+128) for i in range(13)],lq,*tile_refs)
    @pl.when(info[0]==0)
    def _():
        row=lax.broadcasted_iota(jnp.int32,(512,128),0)
        lw=lanes(512); lq=lanes(128)
        acc_k[...]=jnp.zeros_like(acc_k); acc_v[...]=jnp.zeros_like(acc_v)
        @pl.loop(0,13)
        def _(i):
            lo=info[1+i]; hi=info[14+i]
            at=jnp.minimum(lo,9)
            window=pl.ds(pl.multiple_of(at*128,128),512)
            k=k_ref[window,:]; v=v_ref[window,:]
            keep=(row>=(lo-at)*128)&(row<(hi-at)*128)
            rows=pl.ds(pl.multiple_of(i*128,128),128)
            gas=deltas(g_ref[rows,:],o_ref[rows,:],ol_ref[rows,:],lq)
            dqs=[]
            got=bwd_tiles([(qa_ref[h,rows,:],k,v,gas[h],h,keep) for h in (0,1)],lw)
            for h in (0,1):
                dq,dk,dv=got[h]
                dqs.append(dq)
                acc_k[h,window,:]+=dk
                acc_v[h,window,:]+=dv
            dq_ref[rows,:]=(both(dqs,lq)*0.125).astype(BF)
        lf=lanes(FILLED)
        dk_ref[0:FILLED,:]=(jnp.where(lf<64,acc_k[0],acc_k[1])*LN2).astype(BF)
        dv_ref[0:FILLED,:]=jnp.where(lf<64,acc_v[0],acc_v[1]).astype(BF)
    bwd_alone([slice(FILLED,FILLED+PAD)],lanes(PAD),*tile_refs)
    sum_ref[0:1,:]=jnp.sum(dq_ref[...].astype(F32),axis=0,keepdims=True)
    sum_ref[1:2,:]=jnp.sum(dv_ref[...].astype(F32),axis=0,keepdims=True)
def attn_bwd(info,qa,qkv,o,ol,g,first,count,inner,wide,at,into=None,bk=416):
    L,W3=qkv.shape; n=W3//384
    spec=lambda j: pl.BlockSpec((L,128),lambda p,s,j=j:(0,p+first+j*n))
    one=pl.BlockSpec((L,128),lambda p,s:(0,p))
    part=pl.BlockSpec((L,128),lambda p,s:(0,p+inner))
    every=pl.BlockSpec((L,128),lambda p,s:(0,p+first))
    return pl.pallas_call(functools.partial(bwd_kernel,bk,into is not None),
        input_output_aliases={} if into is None else {7:0},
        out_shape=(jax.ShapeDtypeStruct((3,L,wide*128),BF),jax.ShapeDtypeStruct((2,count*128),F32)),
        grid_spec=pltpu.PrefetchScalarGridSpec(num_scalar_prefetch=1,grid=(count,),
            in_specs=[pl.BlockSpec((2,L,128),lambda p,s:(p+inner,0,0)),spec(1),spec(2),part,part,every]+([] if into is None else [pl.BlockSpec(memory_space=pl.ANY)]),
            out_specs=(pl.BlockSpec((3,L,128),lambda p,s:(0,0,p+at)),pl.BlockSpec((2,128),lambda p,s:(0,p))),
            scratch_shapes=[pltpu.VMEM((128,FILLED),F32)]+[pltpu.VMEM((2,FILLED,128),F32)]*2+[pltpu.VMEM((2,FILLED,128),BF)]),
        compiler_params=pltpu.CompilerParams(vmem_limit_bytes=56<<20),name="attn_backward",
        cost_estimate=pl.CostEstimate(flops=20*count*L*L*256,bytes_accessed=16*L*count*128,transcendentals=2*count*L*L))(*((info,qa,qkv,qkv,o,ol,g) if into is None else (info,qa,qkv,qkv,o,ol,g,into)))


def gelu_exact(values):
    return jax.nn.gelu(values, approximate=False)


def norm_forward(values, gain, shift):
    centered = values - jnp.mean(values, axis=-1, keepdims=True)
    inverse = lax.rsqrt(jnp.mean(centered * centered, axis=-1, keepdims=True) + 1e-05)
    unit_part = centered * inverse
    return (unit_part * gain + shift, unit_part, inverse)


def norm_backward(grad_out, unit_part, inverse, gain):
    scaled = grad_out * gain
    centered = scaled - jnp.mean(scaled, axis=-1, keepdims=True)
    grad_in = inverse * (
        centered - unit_part * jnp.mean(scaled * unit_part, axis=-1, keepdims=True)
    )
    return (grad_in, jnp.sum(grad_out * unit_part, axis=0), jnp.sum(grad_out, axis=0))


def attention_forward(query_all, key_all, value_all, segments, head_dim):
    length, local_width = (query_all.shape[1], query_all.shape[2])
    head_count = local_width // head_dim
    block_len = length // 3
    score_scale = head_dim ** (-0.5)

    def per_sequence(pieces):
        queries, key_rows, value_rows, seq_ids = pieces
        key_heads = key_rows.reshape(length, head_count, head_dim)
        value_heads = value_rows.reshape(length, head_count, head_dim)

        def per_block(block_pieces):
            query_part, id_part = block_pieces
            query_heads = query_part.reshape(block_len, head_count, head_dim)
            scores = (
                jnp.einsum(
                    "qhd,khd->hqk", query_heads, key_heads, preferred_element_type=jnp.float32
                )
                * score_scale
            )
            masked = jnp.where(id_part[None, :, None] == seq_ids[None, None, :], scores, -1e30)
            maxima = jnp.max(masked, axis=-1, keepdims=True)
            exp_scores = jnp.exp(masked - maxima)
            totals = jnp.sum(exp_scores, axis=-1, keepdims=True)
            weights_low = (exp_scores / totals).astype(jnp.bfloat16)
            context = jnp.einsum(
                "hqk,khd->qhd", weights_low, value_heads, preferred_element_type=jnp.float32
            )
            return (
                context.astype(jnp.bfloat16).reshape(block_len, local_width),
                (maxima + jnp.log(totals))[..., 0],
            )

        contexts, logsums = lax.map(
            per_block, (queries.reshape(3, block_len, local_width), seq_ids.reshape(3, block_len))
        )
        return (contexts.reshape(length, local_width), logsums)

    return lax.map(per_sequence, (query_all, key_all, value_all, segments))


def attention_backward(query_all, key_all, value_all, segments, logsums, grad_all, head_dim):
    length, local_width = (query_all.shape[1], query_all.shape[2])
    head_count = local_width // head_dim
    block_len = length // 3
    score_scale = head_dim ** (-0.5)

    def per_sequence(pieces):
        queries, key_rows, value_rows, seq_ids, sum_rows, grad_rows = pieces
        key_heads = key_rows.reshape(length, head_count, head_dim)
        value_heads = value_rows.reshape(length, head_count, head_dim)

        def per_block(carry, block_pieces):
            key_total, value_total = carry
            query_part, id_part, sum_part, grad_part = block_pieces
            query_heads = query_part.reshape(block_len, head_count, head_dim)
            grad_heads = grad_part.reshape(block_len, head_count, head_dim)
            scores = (
                jnp.einsum(
                    "qhd,khd->hqk", query_heads, key_heads, preferred_element_type=jnp.float32
                )
                * score_scale
            )
            allowed = id_part[None, :, None] == seq_ids[None, None, :]
            prob_weights = jnp.where(allowed, jnp.exp(scores - sum_part[:, :, None]), 0.0)
            grad_probs = jnp.einsum(
                "qhd,khd->hqk", grad_heads, value_heads, preferred_element_type=jnp.float32
            )
            delta = jnp.sum(prob_weights * grad_probs, axis=-1, keepdims=True)
            grad_scores = (prob_weights * (grad_probs - delta)).astype(jnp.bfloat16)
            query_grad = (
                jnp.einsum(
                    "hqk,khd->qhd", grad_scores, key_heads, preferred_element_type=jnp.float32
                )
                * score_scale
            )
            key_total = (
                key_total
                + jnp.einsum(
                    "hqk,qhd->khd", grad_scores, query_heads, preferred_element_type=jnp.float32
                )
                * score_scale
            )
            value_total = value_total + jnp.einsum(
                "hqk,qhd->khd",
                prob_weights.astype(jnp.bfloat16),
                grad_heads,
                preferred_element_type=jnp.float32,
            )
            return (
                (key_total, value_total),
                query_grad.astype(jnp.bfloat16).reshape(block_len, local_width),
            )

        zero_heads = jnp.zeros((length, head_count, head_dim), jnp.float32)
        (key_total, value_total), query_grads = lax.scan(
            per_block,
            (zero_heads, zero_heads),
            (
                queries.reshape(3, block_len, local_width),
                seq_ids.reshape(3, block_len),
                sum_rows,
                grad_rows.reshape(3, block_len, local_width),
            ),
        )
        return (
            query_grads.reshape(length, local_width),
            key_total.astype(jnp.bfloat16).reshape(length, local_width),
            value_total.astype(jnp.bfloat16).reshape(length, local_width),
        )

    return lax.map(per_sequence, (query_all, key_all, value_all, segments, logsums, grad_all))


def per_device(
    inputs,
    timesteps,
    segments,
    cotangent,
    w_qkv,
    b_query,
    b_value,
    w_out,
    b_out,
    ln1_gain,
    ln1_bias,
    w_up,
    b_up,
    w_down,
    b_down,
    ln2_gain,
    ln2_bias,
    w_time,
    b_time,
):
    groups, local_len, model_width = inputs.shape
    row_count = groups * local_len
    head_dim = D // HEADS
    fraction = timesteps.astype(jnp.float32) / TSTEPS
    start_sum = (
        inputs.astype(jnp.float32)
        + fraction[:, None, None] * w_time.astype(jnp.float32)
        + b_time.astype(jnp.float32)
    )
    start_low = start_sum.astype(jnp.bfloat16)
    projected = jnp.einsum("bld,de->ble", start_low, w_qkv, preferred_element_type=jnp.float32)
    query_low = (projected[..., :model_width] + b_query.astype(jnp.float32)).astype(jnp.bfloat16)
    key_low = projected[..., model_width : 2 * model_width].astype(jnp.bfloat16)
    value_low = (projected[..., 2 * model_width :] + b_value.astype(jnp.float32)).astype(
        jnp.bfloat16
    )
    query_all, key_all, value_all = (
        lax.all_to_all(query_low, "seq", split_axis=2, concat_axis=1, tiled=True),
        lax.all_to_all(key_low, "seq", split_axis=2, concat_axis=1, tiled=True),
        lax.all_to_all(value_low, "seq", split_axis=2, concat_axis=1, tiled=True),
    )
    context_heads, logsums = attention_forward(query_all, key_all, value_all, segments, head_dim)
    context = lax.all_to_all(context_heads, "seq", split_axis=1, concat_axis=2, tiled=True)
    context_rows = context.reshape(row_count, model_width)
    start_rows = start_sum.reshape(row_count, model_width)
    residual_one = (
        start_rows
        + jnp.dot(context_rows, w_out, preferred_element_type=jnp.float32)
        + b_out.astype(jnp.float32)
    )
    normed, unit_one, inverse_one = norm_forward(
        residual_one, ln1_gain.astype(jnp.float32), ln1_bias.astype(jnp.float32)
    )
    normed_low = normed.astype(jnp.bfloat16)
    hidden_pre = jnp.dot(normed_low, w_up, preferred_element_type=jnp.float32) + b_up.astype(
        jnp.float32
    )
    activated, gelu_pull = jax.vjp(gelu_exact, hidden_pre)
    activated_low = activated.astype(jnp.bfloat16)
    residual_two = (
        normed
        + jnp.dot(activated_low, w_down, preferred_element_type=jnp.float32)
        + b_down.astype(jnp.float32)
    )
    result, unit_two, inverse_two = norm_forward(
        residual_two, ln2_gain.astype(jnp.float32), ln2_bias.astype(jnp.float32)
    )
    output = result.astype(jnp.bfloat16).reshape(groups, local_len, model_width)
    grad_result = cotangent.reshape(row_count, model_width).astype(jnp.float32)
    grad_two, grad_ln2_gain, grad_ln2_bias = norm_backward(
        grad_result, unit_two, inverse_two, ln2_gain.astype(jnp.float32)
    )
    grad_b_down = jnp.sum(grad_two, axis=0)
    grad_two_low = grad_two.astype(jnp.bfloat16)
    grad_w_down = jnp.einsum(
        "rf,rd->fd", activated_low, grad_two_low, preferred_element_type=jnp.float32
    )
    grad_activated = jnp.einsum(
        "rd,fd->rf", grad_two_low, w_down, preferred_element_type=jnp.float32
    )
    grad_hidden = gelu_pull(grad_activated)[0]
    grad_b_up = jnp.sum(grad_hidden, axis=0)
    grad_hidden_low = grad_hidden.astype(jnp.bfloat16)
    grad_w_up = jnp.einsum(
        "rd,rf->df", normed_low, grad_hidden_low, preferred_element_type=jnp.float32
    )
    grad_normed = grad_two + jnp.einsum(
        "rf,df->rd", grad_hidden_low, w_up, preferred_element_type=jnp.float32
    )
    grad_one, grad_ln1_gain, grad_ln1_bias = norm_backward(
        grad_normed, unit_one, inverse_one, ln1_gain.astype(jnp.float32)
    )
    grad_b_out = jnp.sum(grad_one, axis=0)
    grad_one_low = grad_one.astype(jnp.bfloat16)
    grad_w_out = jnp.einsum(
        "rd,re->de", context_rows, grad_one_low, preferred_element_type=jnp.float32
    )
    grad_context = (
        jnp.einsum("re,de->rd", grad_one_low, w_out, preferred_element_type=jnp.float32)
        .astype(jnp.bfloat16)
        .reshape(groups, local_len, model_width)
    )
    grad_context_heads = lax.all_to_all(
        grad_context, "seq", split_axis=2, concat_axis=1, tiled=True
    )
    query_grads, key_grads, value_grads = attention_backward(
        query_all, key_all, value_all, segments, logsums, grad_context_heads, head_dim
    )
    grad_query, grad_key, grad_value = (
        lax.all_to_all(query_grads, "seq", split_axis=1, concat_axis=2, tiled=True),
        lax.all_to_all(key_grads, "seq", split_axis=1, concat_axis=2, tiled=True),
        lax.all_to_all(value_grads, "seq", split_axis=1, concat_axis=2, tiled=True),
    )
    grad_projected = jnp.concatenate((grad_query, grad_key, grad_value), axis=2).reshape(
        row_count, 3 * model_width
    )
    grad_w_qkv = jnp.einsum(
        "rd,re->de",
        start_low.reshape(row_count, model_width),
        grad_projected,
        preferred_element_type=jnp.float32,
    )
    grad_b_query = jnp.sum(grad_query.astype(jnp.float32), axis=(0, 1))
    grad_b_value = jnp.sum(grad_value.astype(jnp.float32), axis=(0, 1))
    grad_start = grad_one + jnp.einsum(
        "re,de->rd", grad_projected, w_qkv, preferred_element_type=jnp.float32
    )
    grad_inputs = grad_start.astype(jnp.bfloat16).reshape(groups, local_len, model_width)
    per_sequence_grad = jnp.sum(grad_start.reshape(groups, local_len, model_width), axis=1)
    grad_w_time = jnp.einsum("g,gd->d", fraction, per_sequence_grad)
    grad_b_time = jnp.sum(per_sequence_grad, axis=0)
    (
        sum_w_qkv,
        sum_b_query,
        sum_b_value,
        sum_w_out,
        sum_b_out,
        sum_ln1_gain,
        sum_ln1_bias,
        sum_w_up,
        sum_b_up,
        sum_w_down,
        sum_b_down,
        sum_ln2_gain,
        sum_ln2_bias,
        sum_w_time,
        sum_b_time,
    ) = (
        lax.psum_scatter(grad_w_qkv, ("batch", "seq"), scatter_dimension=0, tiled=True),
        lax.psum_scatter(grad_b_query, ("batch", "seq"), scatter_dimension=0, tiled=True),
        lax.psum_scatter(grad_b_value, ("batch", "seq"), scatter_dimension=0, tiled=True),
        lax.psum_scatter(grad_w_out, ("batch", "seq"), scatter_dimension=0, tiled=True),
        lax.psum_scatter(grad_b_out, ("batch", "seq"), scatter_dimension=0, tiled=True),
        lax.psum_scatter(grad_ln1_gain, ("batch", "seq"), scatter_dimension=0, tiled=True),
        lax.psum_scatter(grad_ln1_bias, ("batch", "seq"), scatter_dimension=0, tiled=True),
        lax.psum_scatter(grad_w_up, ("batch", "seq"), scatter_dimension=0, tiled=True),
        lax.psum_scatter(grad_b_up, ("batch", "seq"), scatter_dimension=0, tiled=True),
        lax.psum_scatter(grad_w_down, ("batch", "seq"), scatter_dimension=0, tiled=True),
        lax.psum_scatter(grad_b_down, ("batch", "seq"), scatter_dimension=0, tiled=True),
        lax.psum_scatter(grad_ln2_gain, ("batch", "seq"), scatter_dimension=0, tiled=True),
        lax.psum_scatter(grad_ln2_bias, ("batch", "seq"), scatter_dimension=0, tiled=True),
        lax.psum_scatter(grad_w_time, ("batch", "seq"), scatter_dimension=0, tiled=True),
        lax.psum_scatter(grad_b_time, ("batch", "seq"), scatter_dimension=0, tiled=True),
    )
    return (
        output,
        grad_inputs,
        sum_w_qkv,
        sum_b_query,
        sum_b_value,
        sum_w_out,
        sum_b_out,
        sum_ln1_gain,
        sum_ln1_bias,
        sum_w_up,
        sum_b_up,
        sum_w_down,
        sum_b_down,
        sum_ln2_gain,
        sum_ln2_bias,
        sum_w_time,
        sum_b_time,
    )


SLOPE = F32
PIECES = 8
LOG2E = 1.4426950408889634


def layer_norm(values):
    centered = values - jnp.mean(values, axis=1, keepdims=True)
    inverse = lax.rsqrt(jnp.mean(centered * centered, axis=1, keepdims=True) + 1e-05)
    return centered * inverse, inverse


def layer_norm_back(scaled, unit_part, inverse):
    return inverse * (
        scaled
        - jnp.mean(scaled, axis=1, keepdims=True)
        - unit_part * jnp.mean(scaled * unit_part, axis=1, keepdims=True)
    )


def gelu_pair(v):
    bell = jnp.exp2(v * v * (-0.5 * LOG2E))
    base = 1.0 + 0.2316418882663604 * jnp.abs(v)
    t = pltpu.reciprocal(base, approx=True)
    t = t * (2.0 - base * t)
    tail = t * (
        0.127414796
        + t * (-0.142248368 + t * (0.7107068705 + t * (-0.7265760135 + t * 0.5307027145)))
    )
    tail = tail * bell
    cover = jnp.where(v >= 0, 1.0 - tail, tail)
    return v * cover, cover + v * bell * 0.3989422804014327


def middle_kernel(
    fc,
    sel_ref,
    frac_ref,
    inp_ref,
    ctx_a0_ref,
    ctx_a1_ref,
    ctx_b0_ref,
    ctx_b1_ref,
    cot_ref,
    vec_ref,
    b_up_ref,
    wo_a_ref,
    wo_b_ref,
    w_up_hbm,
    w_down_hbm,
    out_ref,
    norm_ref,
    act_ref,
    two_ref,
    hid_ref,
    one_ref,
    onel_ref,
    small_ref,
    smallup_ref,
    w_up,
    w_down,
    slope,
    sems,
):
    step = pl.program_id(0)
    def pieces(i, source, target):
        size = source.shape[0] // PIECES
        return [
            pltpu.make_async_copy(
                source.at[pl.ds(j * size, size)],
                target.at[pl.ds(j * size, size)],
                sems.at[i * PIECES + j],
            )
            for j in range(PIECES)
        ]

    copies = pieces(0, w_up_hbm, w_up) + pieces(1, w_down_hbm, w_down)

    @pl.when(step == 0)
    def _():
        for copy in copies:
            copy.start()
        small_ref[...] = jnp.zeros_like(small_ref)
        smallup_ref[...] = jnp.zeros_like(smallup_ref)

    vec = lambda i: vec_ref[i : i + 1, :]
    start = inp_ref[...].astype(F32) + (frac_ref[0] * vec(0) + vec(1))
    residual = (
        start
        + dot(jnp.concatenate([ctx_a0_ref[...], ctx_a1_ref[...]], axis=1), wo_a_ref[...].reshape(-1, wo_a_ref.shape[-1]), NN)
        + dot(jnp.concatenate([ctx_b0_ref[...], ctx_b1_ref[...]], axis=1), wo_b_ref[...].reshape(-1, wo_b_ref.shape[-1]), NN)
        + vec(2)
    )
    unit_one, inverse_one = layer_norm(residual)
    normed = unit_one * vec(3) + vec(4)
    low = normed.astype(BF)
    norm_ref[...] = low

    @pl.when(step == 0)
    def _():
        for copy in copies:
            copy.wait()

    width = w_up.shape[1]
    total = normed + vec(5)
    for f in range(0, width, fc):
        cols = slice(f, f + fc)
        v = dot(low, w_up[:, cols], NN) + b_up_ref[:, cols]
        a, g = gelu_pair(v)
        a = a.astype(BF)
        act_ref[:, cols] = a
        slope[:, cols] = g.astype(slope.dtype)
        total = total + dot(a, w_down[cols, :], NN)
    unit_two, inverse_two = layer_norm(total)
    out_ref[...] = (unit_two * vec(6) + vec(7)).astype(BF)
    cot = cot_ref[...].astype(F32)
    two = layer_norm_back(cot * vec(6), unit_two, inverse_two)
    add = lambda v: jnp.sum(v, axis=0, keepdims=True)
    small_ref[3:4, :] += add(two)
    small_ref[4:5, :] += add(cot * unit_two)
    small_ref[5:6, :] += add(cot)
    two_low = two.astype(BF)
    two_ref[...] = two_low
    total = two
    for f in range(0, width, fc):
        cols = slice(f, f + fc)
        d = dot(two_low, w_down[cols, :], NT) * slope[:, cols].astype(F32)
        smallup_ref[:, cols] += add(d)
        d = d.astype(BF)
        hid_ref[:, cols] = d
        total = total + dot(d, w_up[:, cols], NT)
    small_ref[1:2, :] += add(total * unit_one)
    small_ref[2:3, :] += add(total)
    one = layer_norm_back(total * vec(3), unit_one, inverse_one)
    small_ref[0:1, :] += add(one)
    one_ref[...] = one
    onel_ref[...] = one.astype(BF)


def middle(core, fraction, inp, ctx_a, ctx_b, cot, vecs, b_up, w_out, w_up, w_down, br=288, fc=2048):
    rows, model = inp.shape
    width = w_up.shape[1]
    half = model // 2
    quads = w_out.shape[0]
    row = lambda w: pl.BlockSpec((br, w), lambda i, s: (i, 0))
    fixed = lambda shape: pl.BlockSpec(shape, lambda i, s: (0,) * len(shape))
    here = pl.BlockSpec((br, half // 2), lambda i, s: (s[0] * (rows // br) + i, 0))
    wo = lambda flip: pl.BlockSpec(
        (quads, 1, model // quads // 2, model),
        (lambda i, s: (0, s[0], 0, 0)) if not flip else (lambda i, s: (0, 1 - s[0], 0, 0)),
    )
    out = lambda w, t: jax.ShapeDtypeStruct((rows, w), t)
    return pl.pallas_call(
        functools.partial(middle_kernel, fc),
        out_shape=(
            out(model, BF),
            out(model, BF),
            out(width, BF),
            out(model, BF),
            out(width, BF),
            out(model, F32),
            out(model, BF),
            jax.ShapeDtypeStruct((8, model), F32),
            jax.ShapeDtypeStruct((1, width), F32),
        ),
        grid_spec=pltpu.PrefetchScalarGridSpec(
            num_scalar_prefetch=1,
            grid=(rows // br,),
            in_specs=[
                pl.BlockSpec(memory_space=pltpu.SMEM),
                row(model),
                here,
                here,
                row(half // 2),
                row(half // 2),
                row(model),
                fixed((8, model)),
                fixed((1, width)),
                wo(False),
                wo(True),
                pl.BlockSpec(memory_space=pl.ANY),
                pl.BlockSpec(memory_space=pl.ANY),
            ],
            out_specs=(
                row(model),
                row(model),
                row(width),
                row(model),
                row(width),
                row(model),
                row(model),
                fixed((8, model)),
                fixed((1, width)),
            ),
            scratch_shapes=[
                pltpu.VMEM(w_up.shape, BF),
                pltpu.VMEM(w_down.shape, BF),
                pltpu.VMEM((br, width), SLOPE),
                pltpu.SemaphoreType.DMA((2 * PIECES,)),
            ],
        ),
        compiler_params=pltpu.CompilerParams(vmem_limit_bytes=60 << 20),
        cost_estimate=pl.CostEstimate(
            flops=4 * rows * model * (model // 2 + 2 * width),
            bytes_accessed=4 * model * width + rows * (16 * model + 4 * width),
            transcendentals=rows * width * 2,
        ),
        name="middle",
    )(core, fraction, inp, *ctx_a, *ctx_b, cot, vecs, b_up, w_out, w_out, w_up, w_down)


def grad_kernel(count, extra, *refs):
    lhs = [r[...] for r in refs[1 : 1 + count]]
    rhs_ref = refs[1 + count]
    out_ref = refs[-1]
    left = lhs[0] if count == 1 else jnp.concatenate(lhs, axis=1)
    right = rhs_ref[0] if len(rhs_ref.shape) == 3 else rhs_ref[...]
    total = dot(left, right, TN)
    if extra:
        total = total + refs[2 + count][...].astype(F32)
    out_ref[...] = total.astype(BF)


def weight_grad(sel, lhs, rhs, add=None, cols=1024, quads=4, pairs=2):
    depth, width = lhs.shape
    three = rhs.ndim == 3
    n = rhs.shape[0] * rhs.shape[2] if three else rhs.shape[1]
    cols = rhs.shape[2] if three else cols
    w = width // (quads * pairs)
    extra = add is not None
    if w >= 512:
        grid, count = (quads,), 1
        ins = [
            pl.BlockSpec((depth, w), lambda i, s: (0, pairs * i + s[0])),
            pl.BlockSpec((depth, n), lambda i, s: (0, 0)),
        ]
        out = pl.BlockSpec((w, n), lambda i, s: (i, 0))
        args = [lhs, rhs]
    else:
        grid, count = (n // cols,), quads
        ins = [
            pl.BlockSpec((depth, w), lambda i, s, q=q: (0, pairs * q + s[0])) for q in range(quads)
        ] + [
            pl.BlockSpec((1, depth, cols), lambda i, s: (i, 0, 0))
            if three
            else pl.BlockSpec((depth, cols), lambda i, s: (0, i))
        ]
        out = pl.BlockSpec((quads * w, cols), lambda i, s: (0, i))
        args = [lhs] * quads + [rhs]
    if extra:
        ins.append(out)
        args.append(add)
    total = quads * w
    return pl.pallas_call(
        functools.partial(grad_kernel, count, extra),
        out_shape=jax.ShapeDtypeStruct((total, n), BF),
        grid_spec=pltpu.PrefetchScalarGridSpec(
            num_scalar_prefetch=1, grid=grid, in_specs=ins, out_specs=out
        ),
        compiler_params=pltpu.CompilerParams(vmem_limit_bytes=48 << 20),
        cost_estimate=pl.CostEstimate(
            flops=2 * depth * total * n,
            bytes_accessed=2 * depth * (total + n) + (4 if extra else 2) * total * n,
            transcendentals=0,
        ),
        name="weight_grad",
    )(sel, *args)


def columns_kernel(sel_ref, a_ref, b_ref, own_ref, oth_ref):
    own_ref[...] = a_ref[...]
    oth_ref[...] = b_ref[...]


def split_columns(core, w, quads):
    model, wide = w.shape
    width = wide // 6 // quads
    at = lambda flip: lambda i, s: (
        0,
        (i // quads) * 2 * quads + 2 * (i % quads) + (1 - s[0] if flip else s[0]),
    )
    out = pl.BlockSpec((model, width), lambda i, s: (0, i))
    return pl.pallas_call(
        columns_kernel,
        out_shape=(jax.ShapeDtypeStruct((model, wide // 2), BF),) * 2,
        grid_spec=pltpu.PrefetchScalarGridSpec(
            num_scalar_prefetch=1,
            grid=(3 * quads,),
            in_specs=[pl.BlockSpec((model, width), at(False)), pl.BlockSpec((model, width), at(True))],
            out_specs=(out, out),
        ),
        compiler_params=pltpu.CompilerParams(vmem_limit_bytes=8 << 20),
        cost_estimate=pl.CostEstimate(flops=0, bytes_accessed=4 * model * wide, transcendentals=0),
        name="split_columns",
    )(core, w, w)


def chosen(sel_ref, own_ref, oth_ref):
    mine = pl.program_id(0) // 2 == sel_ref[0]
    return jnp.where(mine, own_ref[...].astype(F32), oth_ref[...].astype(F32))


def project_kernel(sel_ref, frac_ref, own_ref, oth_ref, vec_ref, w_ref, bias_ref, qkv_ref, start_ref):
    start = chosen(sel_ref, own_ref, oth_ref) + (frac_ref[0] * vec_ref[0:1, :] + vec_ref[1:2, :])
    start = start.astype(BF)
    start_ref[...] = start
    half = w_ref.shape[1] // 3
    out = dot(start, w_ref[...], NN) + bias_ref[...]
    qkv_ref[:, :half] = (out[:, :half] * (0.125 * LOG2E)).astype(BF)
    qkv_ref[:, half:] = out[:, half:].astype(BF)


def project(core, fraction, own, oth, vecs, w, bias):
    rows, model = own.shape
    br = rows // 2
    fixed = lambda shape: pl.BlockSpec(shape, lambda i, s: (0, 0))
    part = pl.BlockSpec((br, model), lambda i, s: (i % 2, 0))
    out = lambda w: pl.BlockSpec((br, w), lambda i, s: (i, 0))
    return pl.pallas_call(
        project_kernel,
        out_shape=(
            jax.ShapeDtypeStruct((2 * rows, w.shape[1]), BF),
            jax.ShapeDtypeStruct((2 * rows, model), BF),
        ),
        grid_spec=pltpu.PrefetchScalarGridSpec(
            num_scalar_prefetch=1,
            grid=(4,),
            in_specs=[
                pl.BlockSpec(memory_space=pltpu.SMEM),
                part,
                part,
                fixed(vecs.shape),
                fixed(w.shape),
                fixed(bias.shape),
            ],
            out_specs=(out(w.shape[1]), out(model)),
        ),
        compiler_params=pltpu.CompilerParams(vmem_limit_bytes=40 << 20),
        cost_estimate=pl.CostEstimate(
            flops=4 * rows * model * w.shape[1],
            bytes_accessed=4 * rows * (2 * model + w.shape[1]) + 2 * model * w.shape[1],
            transcendentals=0,
        ),
        name="project",
    )(core, fraction, own, oth, vecs, w, bias)


def context_grad_kernel(sel_ref, own_ref, oth_ref, w_ref, out_ref):
    rows = chosen(sel_ref, own_ref, oth_ref).astype(BF)
    out_ref[...] = dot(rows, w_ref[...].reshape(-1, w_ref.shape[-1]), NT).astype(BF)


def context_grad(core, own, oth, w_out):
    rows, model = own.shape
    br = rows // 2
    quads, _, w, _ = w_out.shape
    part = pl.BlockSpec((br, model), lambda i, s: (i % 2, 0))
    return pl.pallas_call(
        context_grad_kernel,
        out_shape=jax.ShapeDtypeStruct((2 * rows, quads * w), BF),
        grid_spec=pltpu.PrefetchScalarGridSpec(
            num_scalar_prefetch=1,
            grid=(4,),
            in_specs=[
                part,
                part,
                pl.BlockSpec((quads, 1, w, model), lambda i, s: (0, s[0], 0, 0)),
            ],
            out_specs=pl.BlockSpec((br, quads * w), lambda i, s: (i, 0)),
        ),
        compiler_params=pltpu.CompilerParams(vmem_limit_bytes=32 << 20),
        cost_estimate=pl.CostEstimate(
            flops=4 * rows * model * quads * w,
            bytes_accessed=4 * rows * (model + quads * w) + 2 * quads * w * model,
            transcendentals=0,
        ),
        name="context_grad",
    )(core, own, oth, w_out)


def out_grad_kernel(sel_ref, a0, b0, a1, b1, own_ref, oth_ref, out_ref):
    w = a0.shape[1]
    out_ref[:w, :] = (dot(a0[...], own_ref[...], TN) + dot(b0[...], oth_ref[...], TN)).astype(BF)
    out_ref[w:, :] = (dot(a1[...], own_ref[...], TN) + dot(b1[...], oth_ref[...], TN)).astype(BF)


def out_grad(core, contexts, own, oth):
    rows, model = own.shape
    w = contexts[0].shape[1]
    here = pl.BlockSpec((rows, w), lambda i, s: (s[0], 0))
    there = pl.BlockSpec((rows, w), lambda i, s: (1 - s[0], 0))
    full = pl.BlockSpec((rows, model), lambda i, s: (0, 0))
    return pl.pallas_call(
        out_grad_kernel,
        out_shape=jax.ShapeDtypeStruct((2 * w, model), BF),
        grid_spec=pltpu.PrefetchScalarGridSpec(
            num_scalar_prefetch=1,
            grid=(1,),
            in_specs=[here, there, here, there, full, full],
            out_specs=pl.BlockSpec((2 * w, model), lambda i, s: (0, 0)),
        ),
        compiler_params=pltpu.CompilerParams(vmem_limit_bytes=40 << 20),
        cost_estimate=pl.CostEstimate(
            flops=8 * rows * model * w, bytes_accessed=8 * rows * (model + w), transcendentals=0
        ),
        name="out_grad",
    )(core, contexts[0], contexts[0], contexts[1], contexts[1], own, oth)


def finish_kernel(sel_ref, base_ref, mine_ref, got_ref, wm0, wm1, wm2, wg0, wg1, wg2, out_ref, *rest):
    total = base_ref[...]
    for t, (wm, wg) in enumerate(((wm0, wg0), (wm1, wg1), (wm2, wg2))):
        total = total + dot(mine_ref[t], wm[...], NT)
        total = total + dot(got_ref[t], wg[...], NT)
    out_ref[...] = total.astype(out_ref.dtype)
    if rest:
        step = pl.program_id(0)

        @pl.when(step == 0)
        def _():
            rest[0][...] = jnp.zeros_like(rest[0])

        rest[0][...] += jnp.sum(total, axis=0, keepdims=True)


def add_start(core, base, grads, got, w_mine, w_got, group, last, br=288):
    rows, model = base.shape
    n = got.shape[2]
    steps = rows // br
    every = w_mine.shape[1] // (3 * n)
    cols = [pl.BlockSpec((model, n), lambda i, s, t=t: (0, t * every + group)) for t in range(3)]
    row = pl.BlockSpec((br, model), lambda i, s: (i, 0))
    outs = [jax.ShapeDtypeStruct((rows, model), BF if last else F32)]
    specs = [row]
    if last:
        outs.append(jax.ShapeDtypeStruct((1, model), F32))
        specs.append(pl.BlockSpec((1, model), lambda i, s: (0, 0)))
    return pl.pallas_call(
        finish_kernel,
        out_shape=tuple(outs),
        grid_spec=pltpu.PrefetchScalarGridSpec(
            num_scalar_prefetch=1,
            grid=(steps,),
            in_specs=[
                row,
                pl.BlockSpec((3, br, n), lambda i, s: (0, s[0] * steps + i, 0)),
                pl.BlockSpec((3, br, n), lambda i, s: (0, i, 0)),
                *cols,
                *cols,
            ],
            out_specs=tuple(specs),
        ),
        compiler_params=pltpu.CompilerParams(vmem_limit_bytes=40 << 20),
        cost_estimate=pl.CostEstimate(
            flops=12 * rows * n * model,
            bytes_accessed=8 * rows * model + 12 * n * (rows + model),
            transcendentals=0,
        ),
        name="add_start",
    )(core, base, grads, got, *(w_mine,) * 3, *(w_got,) * 3)


class Plan:
    def __init__(self, mesh):
        sizes = dict(mesh.shape)
        self.batch, self.depth = sizes["batch"], sizes["seq"]
        chips = self.batch // 2
        side = 1
        while side * side < chips:
            side *= 2
        self.nx, self.ny = side, chips // side

    def perm(self, target):
        pairs = []
        for y in range(self.ny):
            for x in range(self.nx):
                for c in range(2):
                    for z in range(self.depth):
                        to = target(y, x, c, z)
                        if to != (y, x, c, z):
                            pairs.append((self.index(y, x, c, z), self.index(*to)))
        return pairs

    def index(self, y, x, c, z):
        return ((y * self.nx + x) * 2 + c) * self.depth + z

    def send(self, value, target):
        return lax.ppermute(value, AXES, self.perm(target))

    def sibling(self, value):
        return self.send(value, lambda y, x, c, z: (y, x, 1 - c, z))


def pick(array, index, axis):
    return lax.dynamic_index_in_dim(array, index, axis, keepdims=False)


def tie(*values):
    return lax.optimization_barrier(values)


class Sum:
    def __init__(self, plan, terms, where, axes="yxhl"):
        self.plan, self.terms, self.axes = plan, terms, axes
        y, x, z = where
        self.where = {"y": y, "x": x, "h": z // 2, "l": z % 2}

    def send(self, axis):
        plan, terms = self.plan, self.terms
        self.axis, self.at = axis, self.axes.index(axis)
        self.axes = self.axes.replace(axis, "")
        size = {"x": plan.nx, "y": plan.ny}.get(axis, 2)
        here = self.where[axis]
        self.got = []
        for r in range(1, size):

            def target(y, x, c, z, r=r):
                at = {"y": y, "x": x, "h": z // 2, "l": z % 2}
                at[axis] = (at[axis] + r) % size
                return at["y"], at["x"], c, 2 * at["h"] + at["l"]

            self.got.append(plan.send(pick(terms, (here + r) % size, self.at), target))
        return self

    def add(self):
        total = pick(self.terms, self.where[self.axis], self.at).astype(F32)
        for got in self.got:
            total = total + got.astype(F32)
        self.terms = total.astype(self.terms.dtype) if self.axes else total
        return self.terms

    def hold(self, *others):
        self.terms, *rest = tie(self.terms, *others)
        return rest


def per_chip(
    plan,
    inputs,
    timesteps,
    segments,
    cotangent,
    w_qkv,
    b_query,
    b_value,
    w_out,
    b_out,
    ln1_gain,
    ln1_bias,
    w_up,
    b_up,
    w_down,
    b_down,
    ln2_gain,
    ln2_bias,
    w_time,
    b_time,
):
    local_len = inputs.shape[1]
    rows = 2 * local_len
    length = segments.shape[1]
    b = lax.axis_index("batch")
    z = lax.axis_index("seq")
    c, x, y = b % 2, (b // 2) % plan.nx, b // 2 // plan.nx
    part = z % 2
    where = (y, x, z)
    first = (segments[1, 0] == segments[1, 128 * 12]).astype(jnp.int32)
    which = lambda s: (first + s) % 2
    facts = jnp.concatenate(
        [segments[:, : 128 * 13 : 128], timesteps[:, None], jnp.zeros((2, 2), jnp.int32)], axis=1
    )
    facts = jnp.stack([pick(facts, which(0), 0), pick(facts, which(1), 0)])
    other_facts = plan.sibling(facts)
    facts = jnp.where(z // 2 == c, facts, other_facts)
    mine = pick(facts, z % 2, 0)
    marks = mine[:13]
    info = jnp.concatenate(
        [
            jnp.where(marks[:1] == marks[12:], 1, jnp.where(marks[12:] == marks[:1] + 12, 2, 0)),
            jnp.sum((marks[None, :] < marks[:, None]).astype(jnp.int32), axis=1),
            jnp.sum((marks[None, :] <= marks[:, None]).astype(jnp.int32), axis=1),
        ]
    )
    fraction = mine[13].astype(F32) / TSTEPS

    stays = z // 2 == c

    def exchange(parts):
        got = [
            plan.send(v, lambda y, x, c, z, j=j: (y, x, z // 2, 2 * c + (z + j) % 2))
            for j, v in enumerate(parts)
        ]
        return [(got[0], parts[0]), (got[1], None)]

    def arrived(got):
        return [jnp.where(stays, got[0][1], got[0][0]), got[1][0]]

    def gather_parts(array):
        return [pick(array, which((part + j) % 2), 0) for j in (0, 1)]

    def gather_end(got):
        got = arrived(got)
        return jnp.concatenate(
            [jnp.where(part == 0, got[0], got[1]), jnp.where(part == 0, got[1], got[0])], axis=0
        )

    def spread_parts(array):
        array = array.reshape(2, local_len, array.shape[-1])
        return [pick(array, (part + j) % 2, 0) for j in (0, 1)]

    def spread_end(got):
        got = arrived(got)
        swap = (part + first) % 2
        return jnp.stack(
            [jnp.where(swap == 0, got[0], got[1]), jnp.where(swap == 0, got[1], got[0])], axis=0
        )

    def whole(own, other):
        return jnp.where(c == 0, jnp.concatenate([own, other]), jnp.concatenate([other, own]))

    def halves(array, axis):
        shape = array.shape
        cut = shape[:axis] + (plan.ny * plan.nx, 2, -1) + shape[axis + 1 :]
        flat = shape[:axis] + (-1,) + shape[axis + 1 :]
        split = array.reshape(cut)
        return (
            pick(split, c, axis + 1).reshape(flat),
            pick(split, 1 - c, axis + 1).reshape(flat),
        )

    def blocks(array):
        return array.reshape(plan.ny, plan.nx, 2, 2, -1, array.shape[-1])

    model = inputs.shape[-1]
    half = model // 2
    quads = plan.ny * plan.nx
    core = jnp.stack([c]).astype(jnp.int32)
    away = 1 - core
    w_own, w_oth = split_columns(core, w_qkv, quads)
    bias = jnp.concatenate(
        [
            halves(b_query.astype(F32), 0)[0],
            jnp.zeros((half,), F32),
            halves(b_value.astype(F32), 0)[0],
        ]
    )
    w_out_four = w_out.reshape(quads, 2, -1, model)
    ahead = [range(0, quads // 2), range(quads // 2, quads)]
    groups = ahead
    own_inputs = gather_end(exchange(gather_parts(inputs)))
    vecs = jnp.stack(
        [v.astype(F32) for v in (w_time, b_time, b_out, ln1_gain, ln1_bias, b_down, ln2_gain, ln2_bias)]
    )
    cot_parts = gather_parts(cotangent)
    bias = bias[None]
    own_inputs, w_own, w_oth, vecs, info, bias, cot_parts = tie(
        own_inputs, w_own, w_oth, vecs, info, bias, cot_parts
    )
    sib_inputs = plan.sibling(own_inputs)
    cot_parts, sib_inputs = tie(cot_parts, sib_inputs)
    own_cotangent = gather_end(exchange(cot_parts))
    qkv, start_full = project(core, fraction[None], own_inputs, sib_inputs, vecs, w_own, bias)
    fwd = [attn_fwd(info, qkv, g.start, len(g)) for g in ahead]
    away_of = [
        plan.sibling(pick(f[0].reshape(2, rows, -1), 1 - c, 0)) for f in fwd
    ]
    result, normed_low, act, two_low, hid, grad_one, one_low, small_sums, up_sums = middle(
        core,
        fraction[None],
        own_inputs,
        [f[0] for f in fwd],
        away_of,
        own_cotangent,
        vecs,
        b_up.astype(F32)[None],
        w_out_four,
        w_up,
        w_down,
    )
    one_sib = plan.sibling(one_low)
    output_got = exchange(spread_parts(result))
    down_part = weight_grad(away, act, two_low, quads=quads)
    normed_low, down_part = tie(normed_low, down_part)
    down_got = plan.sibling(down_part)
    up_part = weight_grad(away, normed_low, hid, quads=quads)
    act, up_part = tie(act, up_part)
    up_got = plan.sibling(up_part)
    down_sum = weight_grad(core, act, two_low, down_got, quads=quads)
    normed_low, down_sum = tie(normed_low, down_sum)
    down = Sum(plan, blocks(down_sum), where).send("x")
    up_sum = weight_grad(core, normed_low, hid, up_got, quads=quads)
    one_low, one_sib, up_sum = tie(one_low, one_sib, up_sum)
    up = Sum(plan, blocks(up_sum), where).send("y")
    out_sum = out_grad(core, [f[0] for f in fwd], one_low, one_sib)
    one_low, one_sib, out_sum = tie(one_low, one_sib, out_sum)
    out = Sum(plan, blocks(out_sum), where).send("x")
    grad_context = context_grad(core, one_low, one_sib, w_out_four)

    def back(first, count, into=None):
        f = first // (quads // 2)
        start = ahead[f].start
        return attn_bwd(
            info,
            fwd[f][2],
            qkv,
            fwd[f][0],
            fwd[f][1],
            grad_context,
            first,
            count,
            first - start,
            quads // 2,
            first - start,
            into,
        )

    def away_rows(grads):
        return plan.sibling(pick(grads.reshape(3, 2, rows, -1), 1 - c, 1))

    def products(grads):
        cross_part = weight_grad(away, start_full, grads, quads=quads)
        grads, cross_part = tie(grads, cross_part)
        cross = plan.sibling(cross_part)
        keep = weight_grad(core, start_full, grads, quads=quads)
        return Sum(plan, blocks(cross), where), Sum(plan, blocks(keep), where)

    def settle(items, other):
        for item in items:
            item.got, other = tie(item.got, other)
            item.add()
            item.terms, other = tie(item.terms, other)
        return other

    grads, b_sum0 = back(0, quads // 2)
    got = away_rows(grads)
    output_got, grads = tie(output_got, grads)
    grads = settle([down, up, out], grads)
    down.send("y")
    up.send("x")
    out.send("y")
    cross0, keep0 = products(grads)
    got, cross0.terms, keep0.terms = tie(got, cross0.terms, keep0.terms)
    (grad_start,) = add_start(core, grad_one, grads, got, w_own, w_oth, 0, False)
    keep0.send("x")
    cross0.send("y")
    grad_context, grad_start = tie(grad_context, grad_start)
    grads, b_sum1 = back(quads // 2, quads // 4)
    grads = settle([down, up, out, keep0, cross0], grads)
    wide_rows = up.terms.shape[-2]
    slabs = [up.terms[..., i * model : (i + 1) * model] for i in range(up.terms.shape[-1] // model)]
    ffn = jnp.concatenate([down.terms, *slabs, out.terms], axis=2)
    ffn, grads = tie(ffn, grads)
    ffn = Sum(plan, ffn, where, "hl").send("l")
    keep0.send("y")
    cross0.send("x")
    grads, b_sum2 = back(quads // 2 + quads // 4, quads // 4, grads)
    got = away_rows(grads)
    grads = settle([ffn], grads)
    ffn.send("h")
    cross1, keep1 = products(grads)
    got, keep1.terms = tie(got, keep1.terms)
    keep1.send("x")
    cross1.send("y")
    grad_low, b_time_sum = add_start(core, grad_start, grads, got, w_own, w_oth, 1, True)
    in_parts, b_time_sum = tie(spread_parts(grad_low), b_time_sum)
    grad_inputs_got = exchange(in_parts)
    b_time_sum = settle([keep0, cross0, keep1, cross1], b_time_sum)
    ffn.got, b_time_sum = tie(ffn.got, b_time_sum)
    keep1.send("y")
    cross1.send("x")
    small_sums, up_sums, b_time_sum = tie(small_sums, up_sums, b_time_sum)
    b_sum = jnp.concatenate([b_sum0, b_sum1, b_sum2], axis=1)
    zero = jnp.zeros((quads, 2, half // quads), F32)

    def placed(v):
        return lax.dynamic_update_index_in_dim(zero, v.reshape(quads, half // quads), c, 1).reshape(-1)

    vectors = [small_sums[i] for i in range(6)]
    vectors += [placed(b_sum[0]), placed(b_sum[1]), fraction * b_time_sum[0], b_time_sum[0]]
    small = jnp.concatenate([v[:, None] for v in vectors] + [up_sums.reshape(model, -1)], axis=1)
    small_own, small_oth = halves(small, 0)
    small = Sum(plan, blocks(small_own + plan.sibling(small_oth)), where)
    small.send("x").add()
    small.send("y")
    keep1.got, cross1.got, small.got, grad_inputs_got = tie(
        keep1.got, cross1.got, small.got, grad_inputs_got
    )
    keep1.add()
    cross1.add()
    small.add()
    late = jnp.concatenate([i.terms for i in (keep0, cross0, keep1, cross1)], axis=3)
    late = Sum(plan, late, where, "hl").send("l")
    small.send("l")
    late.got, small.got = tie(late.got, small.got)
    late.add()
    small.add()
    late.send("h")
    small.send("h")
    small.add()
    small = small.terms
    late = late.add()
    wide = 3 * half // 2
    keeps = [late[:, :wide], late[:, 2 * wide : 3 * wide]]
    crosses = [late[:, wide : 2 * wide], late[:, 3 * wide : 4 * wide]]
    ffn = ffn.add()
    count = ffn.shape[0] - wide_rows * (len(slabs) + 1)
    sum_w_down, sum_w_out = ffn[:count], ffn[count + wide_rows * len(slabs) :]
    sum_w_up = jnp.concatenate(
        [ffn[count + i * wide_rows : count + (i + 1) * wide_rows] for i in range(len(slabs))], axis=1
    )
    output = spread_end(output_got)
    grad_inputs = spread_end(grad_inputs_got)
    split3 = lambda parts: jnp.concatenate(
        [p.reshape(p.shape[0], 3, len(g), -1) for p, g in zip(parts, groups)], axis=2
    )
    sum_own, sum_oth = split3(keeps), split3(crosses)
    pair = jnp.where(c == 0, jnp.stack([sum_own, sum_oth]), jnp.stack([sum_oth, sum_own]))
    sum_w_qkv = (
        pair.transpose(1, 2, 3, 0, 4).reshape(-1, 3 * model)
    )
    v = [small[:, i] for i in (6, 7, 0, 1, 2, 3, 4, 5, 8, 9)]
    return (
        output,
        grad_inputs,
        sum_w_qkv,
        v[0],
        v[1],
        sum_w_out,
        v[2],
        v[3],
        v[4],
        sum_w_up,
        small[:, 10:].reshape(-1),
        sum_w_down,
        v[5],
        v[6],
        v[7],
        v[8],
        v[9],
    )


def solution(mesh):
    placed = (
        P("batch", "seq", None),
        P("batch"),
        P("batch", None),
        P("batch", "seq", None),
        P(),
        P(),
        P(),
        P(),
        P(),
        P(),
        P(),
        P(),
        P(),
        P(),
        P(),
        P(),
        P(),
        P(),
        P(),
    )
    sizes = dict(mesh.shape)
    body = per_device
    if sizes["seq"] == 4 and sizes["batch"] % 2 == 0:
        body = functools.partial(per_chip, Plan(mesh))
    return jax.shard_map(
        body,
        mesh=mesh,
        in_specs=placed,
        out_specs=(
            P("batch", "seq", None),
            P("batch", "seq", None),
            P(("batch", "seq"), None),
            P(("batch", "seq")),
            P(("batch", "seq")),
            P(("batch", "seq"), None),
            P(("batch", "seq")),
            P(("batch", "seq")),
            P(("batch", "seq")),
            P(("batch", "seq"), None),
            P(("batch", "seq")),
            P(("batch", "seq"), None),
            P(("batch", "seq")),
            P(("batch", "seq")),
            P(("batch", "seq")),
            P(("batch", "seq")),
            P(("batch", "seq")),
        ),
        check_vma=False,
    )
```

profile of v0, /device:TPU:0, one launch (start us, length us, event | category | flops | bytes accessed | tf_op | source)
XLA Modules:
  0.0 457.0 jit_solution(8124278739235987218)
XLA Ops:
  3.4 2.8 dynamic-slice_bitcast_fusion.12
  6.3 1.7 collective-permute-start.1
  8.0 3.0 collective-permute-start.2
  12.1 2.6 collective-permute-start
  16.4 2.8 copy-done.8
  19.2 3.7 split_columns.1
  22.9 1.7 copy-done.4
  28.2 3.2 collective-permute-done.2
  31.4 1.6 broadcast_select_fusion.3
  34.3 11.2 %collective-permute-start.3 = (bf16[864,1024]{1,0:T(8,128)(2,1)}, bf16[864,1024]{1,0:T(8,128)(2,1)}, u32[]{:S(2)}, u32[]{:S(2)}) collective-permute-start(bf16[864,1024]{1,0:T(8,128)(2,1)} %pad_maximum_fusion.own_ref.inp_ref), channel_id=1, source_target_pairs={{0,4},{1,5},{2,6},{3,7},{4,0},{5,1},{6,2},{7,3},{8,12},{9,13},{10,... | collective-permute-start | bytes 5308424 | tf_op jit(solution)/shard_map/ppermute | solution.py:1033
  46.8 2.4 collective-permute-done.3.oth_ref
  49.9 10.2 %collective-permute-start.7 = (bf16[432,1024]{1,0:T(8,128)(2,1)}, bf16[432,1024]{1,0:T(8,128)(2,1)S(1)}, u32[]{:S(2)}, u32[]{:S(2)}) collective-permute-start(bf16[432,1024]{1,0:T(8,128)(2,1)} %get-tuple-element.166), channel_id=1, source_target_pairs={{0,1},{1,0},{2,5},{3,4},{4,3},{5,2},{6,7},{7,6},{8,9},{9,8},{10,13... | collective-permute-start | bytes 2654216 | tf_op jit(solution)/shard_map/ppermute | solution.py:1033
  60.1 9.2 %project.1 = (bf16[1728,1536]{1,0:T(8,128)(2,1)}, bf16[1728,1024]{1,0:T(8,128)(2,1)S(1)}) custom-call(s32[1]{0:T(128)} %bitcast.1.sel_ref.refs_0_, f32[1]{0:T(128)} %bitcast.3.frac_ref, bf16[864,1024]{1,0:T(8,128)(2,1)} %pad_maximum_fusion.own_ref.inp_ref, bf16[864,1024]{1,0:T(8,128)(2,1)} %collective-permute-done.3.oth_ref, f32[8,1024]{1,0:T(8,128)S(1)} %stack.89.vec_ref, ...), custom_call_target="tpu_custom_call" | custom-call | flops 5435817984 | bytes 15532032 | tf_op jit(solution)/shard_map/project/pallas_call | solution.py:864
  69.3 1.7 copy-done
  71.0 17.7 %attn_forward.3 = (bf16[1728,256]{1,0:T(8,128)(2,1)S(1)}, bf16[1728,256]{1,0:T(8,128)(2,1)S(1)}, bf16[4,1728,128]{2,1,0:T(8,128)(2,1)S(1)}) custom-call(s32[27]{0:T(128)S(1)} %pad_add_fusion.1.info, bf16[1728,1536]{1,0:T(8,128)(2,1)} %get-tuple-element.162.q_ref.k_ref.v_ref, bf16[1728,1536]{1,0:T(8,128)(2,1)} %get-tuple-element.162.q_ref.k_ref.v_ref, ...), custom_call_target="tpu_custom_call" | custom-call | flops 12230590464 | bytes 4423680 | tf_op jit(solution)/shard_map/attn_forward/pallas_call | solution.py:117
  90.9 3.7 collective-permute-start.5
  94.6 17.9 %attn_forward.2 = (bf16[1728,256]{1,0:T(8,128)(2,1)S(1)}, bf16[1728,256]{1,0:T(8,128)(2,1)S(1)}, bf16[4,1728,128]{2,1,0:T(8,128)(2,1)S(1)}) custom-call(s32[27]{0:T(128)S(1)} %pad_add_fusion.1.info, bf16[1728,1536]{1,0:T(8,128)(2,1)} %get-tuple-element.162.q_ref.k_ref.v_ref, bf16[1728,1536]{1,0:T(8,128)(2,1)} %get-tuple-element.162.q_ref.k_ref.v_ref, ...), custom_call_target="tpu_custom_call" | custom-call | flops 12230590464 | bytes 4423680 | tf_op jit(solution)/shard_map/attn_forward/pallas_call | solution.py:117
  116.6 54.9 %middle.1 = (bf16[864,1024]{1,0:T(8,128)(2,1)}, bf16[864,1024]{1,0:T(8,128)(2,1)}, bf16[864,4096]{1,0:T(8,128)(2,1)}, bf16[864,1024]{1,0:T(8,128)(2,1)}, bf16[86...) custom-call(s32[1]{0:T(128)} %bitcast.1.sel_ref.refs_0_, ...), custom_call_target="tpu_custom_call" | custom-call | flops 30802968576 | bytes 45088768 | tf_op jit(solution)/shard_map/middle/pallas_call | solution.py:698
  171.5 1.5 copy-done.16
  173.0 7.8 %weight_grad.8 = bf16[2048,1024]{1,0:T(8,128)(2,1)} custom-call(s32[1]{0:T(128)S(6)} %sub.27.refs_0_, bf16[864,4096]{1,0:T(8,128)(2,1)} %get-tuple-element.176.refs_1_, bf16[864,1024]{1,0:T(8,128)(2,1)S(1)} %copy-done.16), custom_call_target="tpu_custom_call" | custom-call | flops 3623878656 | bytes 9502720 | tf_op jit(solution)/shard_map/weight_grad/pallas_call | solution.py:799
  180.8 8.6 %weight_grad.9 = bf16[512,4096]{1,0:T(8,128)(2,1)} custom-call(s32[1]{0:T(128)S(6)} %sub.27.refs_0_, bf16[864,1024]{1,0:T(8,128)(2,1)S(1)} %copy-done.1, bf16[864,1024]{1,0:T(8,128)(2,1)S(1)} %copy-done.1, bf16[864,1024]{1,0:T(8,128)(2,1)S(1)} %copy-done.1, bf16[864,1024]{1,0:T(8,128)(2,1)S(1)} %copy-done.1, bf16[864,4096]{1,0:T(8,128)(2,1)} %get-tuple-element.175.refs_5_), custom_call_target="tpu_custom_call" | custom-call | flops 3623878656 | bytes 12156928 | tf_op jit(solution)/shard_map/weight_grad/pallas_call | solution.py:799
  189.8 2.9 dynamic-slice_bitcast_fusion.7
  192.8 1.6 collective-permute-start.8
  194.4 7.0 %weight_grad.10 = bf16[2048,1024]{1,0:T(8,128)(2,1)S(1)} custom-call(s32[1]{0:T(128)} %bitcast.1.sel_ref.refs_0_, bf16[864,4096]{1,0:T(8,128)(2,1)} %get-tuple-element.176.refs_1_, bf16[864,1024]{1,0:T(8,128)(2,1)S(1)} %copy-done.17, bf16[2048,1024]{1,0:T(8,128)(2,1)} %collective-permute-done.11.refs_3_), custom_call_target="tpu_custom_call" | custom-call | flops 3623878656 | bytes 13697024 | tf_op jit(solution)/shard_map/weight_grad/pallas_call | solution.py:799
  202.0 1.5 copy.237
  203.5 1.5 collective-permute-start.15
  205.0 7.7 %weight_grad.11 = bf16[512,4096]{1,0:T(8,128)(2,1)S(1)} custom-call(s32[1]{0:T(128)} %bitcast.1.sel_ref.refs_0_, bf16[864,1024]{1,0:T(8,128)(2,1)S(1)} %copy-done.1, bf16[864,1024]{1,0:T(8,128)(2,1)S(1)} %copy-done.1, bf16[864,1024]{1,0:T(8,128)(2,1)S(1)} %copy-done.1, bf16[864,1024]{1,0:T(8,128)(2,1)S(1)} %copy-done.1, ...), custom_call_target="tpu_custom_call" | custom-call | flops 3623878656 | bytes 16351232 | tf_op jit(solution)/shard_map/weight_grad/pallas_call | solution.py:799
  212.8 3.8 out_grad.1
  216.6 1.8 constant_dynamic-slice_fusion.9
  218.5 1.6 copy.238
  220.1 1.5 collective-permute-start.14
  221.6 4.4 context_grad.1.g_ref
  227.2 35.0 %attn_backward.3 = (bf16[3,1728,256]{2,1,0:T(8,128)(2,1)}, f32[2,256]{1,0:T(2,128)}) custom-call(s32[27]{0:T(128)} %copy-done.22, bf16[4,1728,128]{2,1,0:T(8,128)(2,1)} %copy-done.24, bf16[1728,1536]{1,0:T(8,128)(2,1)} %get-tuple-element.162.q_ref.k_ref.v_ref, bf16[1728,1536]{1,0:T(8,128)(2,1)} %get-tuple-element.162.q_ref.k_ref.v_ref, ...), custom_call_target="tpu_custom_call" | custom-call | flops 30576476160 | bytes 7077888 | tf_op jit(solution)/shard_map/attn_backward/pallas_call | solution.py:216
  265.5 1.6 select_bitcast_fusion.3
  268.5 2.7 fusion
  271.2 3.2 fusion.1
  274.4 2.3 collective-permute-done.13
  276.9 3.7 weight_grad.12
  285.6 4.2 weight_grad.13
  291.0 1.4 collective-permute-start.22
  293.7 4.8 %add_start.2.base_ref = f32[864,1024]{1,0:T(8,128)S(1)} custom-call(s32[1]{0:T(128)} %bitcast.1.sel_ref.refs_0_, f32[864,1024]{1,0:T(8,128)} %get-tuple-element.190.base_ref, bf16[3,1728,256]{2,1,0:T(8,128)(2,1)S(1)} %copy-done.6, bf16[3,864,256]{2,1,0:T(8,128)(2,1)S(1)} %copy-done.20, bf16[1024,1536]{1,0:T(8,128)(2,1)S(1)} %copy-done.3, ...), custom_call_target="tpu_custom_call" | custom-call | flops 2717908992 | bytes 12877824 | tf_op jit(solution)/shard_map/add_start/pallas_call | solution.py:983
  298.6 1.8 copy-done.9
  300.4 1.8 dynamic-slice_bitcast_fusion.20
  303.2 19.2 %attn_backward.4 = (bf16[3,1728,256]{2,1,0:T(8,128)(2,1)}, f32[2,128]{1,0:T(2,128)}) custom-call(s32[27]{0:T(128)} %copy-done.22, bf16[4,1728,128]{2,1,0:T(8,128)(2,1)} %copy-done.23, bf16[1728,1536]{1,0:T(8,128)(2,1)} %get-tuple-element.162.q_ref.k_ref.v_ref, bf16[1728,1536]{1,0:T(8,128)(2,1)} %get-tuple-element.162.q_ref.k_ref.v_ref, ...), custom_call_target="tpu_custom_call" | custom-call | flops 15288238080 | bytes 3538944 | tf_op jit(solution)/shard_map/attn_backward/pallas_call | solution.py:216
  323.2 1.9 fusion.4
  325.1 1.5 fusion.3
  330.7 19.3 %attn_backward.5 = (bf16[3,1728,256]{2,1,0:T(8,128)(2,1)}, f32[2,128]{1,0:T(2,128)}) custom-call(s32[27]{0:T(128)} %copy-done.22, bf16[4,1728,128]{2,1,0:T(8,128)(2,1)} %copy-done.23, bf16[1728,1536]{1,0:T(8,128)(2,1)} %get-tuple-element.162.q_ref.k_ref.v_ref, ...), custom_call_target="tpu_custom_call", output_to_operand_aliasing={{0}: (7, {})} | custom-call | flops 15288238080 | bytes 3538944 | tf_op jit(solution)/shard_map/attn_backward/pallas_call | solution.py:216
  350.0 1.6 dynamic-slice_bitcast_fusion
  354.8 3.0 collective-permute-done.24
  357.8 1.7 fusion.2
  359.5 3.7 weight_grad.14
  363.3 3.7 weight_grad.15
  368.1 5.0 %add_start.3 = (bf16[864,1024]{1,0:T(8,128)(2,1)S(1)}, f32[1,1024]{1,0:T(1,128)S(1)}) custom-call(s32[1]{0:T(128)} %bitcast.1.sel_ref.refs_0_, f32[864,1024]{1,0:T(8,128)} %copy-done.9, bf16[3,1728,256]{2,1,0:T(8,128)(2,1)S(1)} %copy-done.7, bf16[3,864,256]{2,1,0:T(8,128)(2,1)S(1)} %collective-permute-done.23.got_ref, bf16[1024,1536]{1,0:T(8,128)(2,1)S(1)} %copy-done.3, ...), custom_call_target="tpu_custom_call" | custom-call | flops 2717908992 | bytes 12877824 | tf_op jit(solution)/shard_map/add_start/pallas_call | solution.py:983
  378.5 1.7 fusion.16
  380.1 1.7 collective-permute-start.36
  382.2 3.5 collective-permute-done.25
  389.2 25.9 %collective-permute-done.32 = bf16[288,1024]{1,0:T(8,128)(2,1)} collective-permute-done((bf16[288,1024]{1,0:T(8,128)(2,1)S(1)}, bf16[288,1024]{1,0:T(8,128)(2,1)}, u32[]{:S(2)}, u32[]{:S(2)}) %collective-permute-start.32) | collective-permute-done | bytes 589856 | tf_op jit(solution)/shard_map/ppermute | solution.py:1033
  420.3 1.4 collective-permute-start.31
  421.8 2.6 collective-permute-done.34
  429.7 2.1 collective-permute-start.38
  431.8 1.6 select_bitcast_fusion.1
  434.7 3.7 collective-permute-done.38
  438.5 5.0 %collective-permute-start.41 = (f32[32,14]{0,1:T(8,128)S(1)}, f32[32,14]{0,1:T(8,128)S(1)}, u32[]{:S(2)}, u32[]{:S(2)}) collective-permute-start(f32[32,14]{0,1:T(8,128)S(1)} %bitcast.269), channel_id=1, source_target_pairs={{0,2},{1,3},{2,0},{3,1},{4,6},{5,7},{6,4},{7,5},{8,10},{9,11},{10,... | collective-permute-start | bytes 5384 | tf_op jit(solution)/shard_map/ppermute | solution.py:1033
  446.4 8.2 %collective-permute-done.40 = bf16[32,3072]{1,0:T(8,128)(2,1)S(1)} collective-permute-done((bf16[32,3072]{1,0:T(8,128)(2,1)S(1)}, bf16[32,3072]{1,0:T(8,128)(2,1)S(1)}, u32[]{:S(2)}, u32[]{:S(2)}) %collective-permute-start.40) | collective-permute-done | bytes 196640 | tf_op jit(solution)/shard_map/ppermute | solution.py:1033
  (297 shorter events, 64.5 us)
Async XLA Ops:
  0.7 11.1 %copy-start.53 = (s32[2]{0:T(128)S(1)}, s32[2]{0:T(128)}, u32[]{:S(2)}) copy-start(s32[2]{0:T(128)} %param.20) | copy-start | bytes 28
  0.7 14.0 %copy-start.34 = (bf16[2,432,1024]{2,1,0:T(8,128)(2,1)S(1)}, bf16[2,432,1024]{2,1,0:T(8,128)(2,1)}, u32[]{:S(2)}) copy-start(bf16[2,432,1024]{2,1,0:T(8,128)(2,1)} %param.22) | copy-start | bytes 5308420
  6.2 9.9 %copy-start.39 = (bf16[1024]{0:T(1024)(128)(2,1)S(1)}, bf16[1024]{0:T(1024)(128)(2,1)}, u32[]{:S(2)}) copy-start(bf16[1024]{0:T(1024)(128)(2,1)} %param.24) | copy-start | bytes 6148
  6.2 9.9 %copy-start.40 = (bf16[1024]{0:T(1024)(128)(2,1)S(1)}, bf16[1024]{0:T(1024)(128)(2,1)}, u32[]{:S(2)}) copy-start(bf16[1024]{0:T(1024)(128)(2,1)} %param.25) | copy-start | bytes 6148
  6.2 10.0 %copy-start.41 = (bf16[1024]{0:T(1024)(128)(2,1)S(1)}, bf16[1024]{0:T(1024)(128)(2,1)}, u32[]{:S(2)}) copy-start(bf16[1024]{0:T(1024)(128)(2,1)} %param.36) | copy-start | bytes 6148
  6.2 10.0 %copy-start.42 = (bf16[1024]{0:T(1024)(128)(2,1)S(1)}, bf16[1024]{0:T(1024)(128)(2,1)}, u32[]{:S(2)}) copy-start(bf16[1024]{0:T(1024)(128)(2,1)} %param.37) | copy-start | bytes 6148
  6.2 10.0 %copy-start.43 = (bf16[1024]{0:T(1024)(128)(2,1)S(1)}, bf16[1024]{0:T(1024)(128)(2,1)}, u32[]{:S(2)}) copy-start(bf16[1024]{0:T(1024)(128)(2,1)} %param.27) | copy-start | bytes 6148
  6.2 10.0 %copy-start.44 = (bf16[1024]{0:T(1024)(128)(2,1)S(1)}, bf16[1024]{0:T(1024)(128)(2,1)}, u32[]{:S(2)}) copy-start(bf16[1024]{0:T(1024)(128)(2,1)} %param.28) | copy-start | bytes 6148
  6.2 10.0 %copy-start.45 = (bf16[1024]{0:T(1024)(128)(2,1)S(1)}, bf16[1024]{0:T(1024)(128)(2,1)}, u32[]{:S(2)}) copy-start(bf16[1024]{0:T(1024)(128)(2,1)} %param.29) | copy-start | bytes 6148
  6.2 10.0 %copy-start.46 = (bf16[1024]{0:T(1024)(128)(2,1)S(1)}, bf16[1024]{0:T(1024)(128)(2,1)}, u32[]{:S(2)}) copy-start(bf16[1024]{0:T(1024)(128)(2,1)} %param.33) | copy-start | bytes 6148
  6.2 10.0 %copy-start.47 = (bf16[1024]{0:T(1024)(128)(2,1)S(1)}, bf16[1024]{0:T(1024)(128)(2,1)}, u32[]{:S(2)}) copy-start(bf16[1024]{0:T(1024)(128)(2,1)} %param.34) | copy-start | bytes 6148
  6.3 10.1 %copy-start.48 = (bf16[1024]{0:T(1024)(128)(2,1)S(1)}, bf16[1024]{0:T(1024)(128)(2,1)}, u32[]{:S(2)}) copy-start(bf16[1024]{0:T(1024)(128)(2,1)} %param.35) | copy-start | bytes 6148
  6.3 21.9 %collective-permute-start.1 = (bf16[432,1024]{1,0:T(8,128)(2,1)}, bf16[432,1024]{1,0:T(8,128)(2,1)}, u32[]{:S(2)}, u32[]{:S(2)}) collective-permute-start(bf16[432,1024]{1,0:T(8,128)(2,1)} %get-tuple-element.307), channel_id=1, source_target_pairs={{2,4},{3,5},{4,2},{5,3},{10,12},{11,13},{12,10},{13,11},{18,20},{1... | collective-permute-start | bytes 2654216 | tf_op jit(solution)/shard_map/ppermute | solution.py:1033
  8.0 23.4 %collective-permute-start.2 = (bf16[432,1024]{1,0:T(8,128)(2,1)}, bf16[432,1024]{1,0:T(8,128)(2,1)}, u32[]{:S(2)}, u32[]{:S(2)}) collective-permute-start(bf16[432,1024]{1,0:T(8,128)(2,1)} %get-tuple-element.308), channel_id=1, source_target_pairs={{0,1},{1,0},{2,5},{3,4},{4,3},{5,2},{6,7},{7,6},{8,9},{9,8},{10,13... | collective-permute-start | bytes 2654216 | tf_op jit(solution)/shard_map/ppermute | solution.py:1033
  12.1 12.5 %collective-permute-start = (s32[2,16]{1,0:T(2,128)S(1)}, s32[2,16]{1,0:T(2,128)S(1)}, u32[]{:S(2)}, u32[]{:S(2)}) collective-permute-start(s32[2,16]{1,0:T(2,128)S(1)} %pad_add_fusion), channel_id=1, source_target_pairs={{0,4},{1,5},{2,6},{3,7},{4,0},{5,1},{6,2},{7,3},{8,12},{9,13},{10,... | collective-permute-start | bytes 392 | tf_op jit(solution)/shard_map/ppermute | solution.py:1033
  16.4 43.7 %copy-start.21 = (f32[8,1024]{1,0:T(8,128)}, f32[8,1024]{1,0:T(8,128)S(1)}, u32[]{:S(2)}) copy-start(f32[8,1024]{1,0:T(8,128)S(1)} %stack.89.vec_ref) | copy-start | bytes 98308
  24.6 35.5 %copy-start.2 = (bf16[1024,1536]{1,0:T(8,128)(2,1)}, bf16[1024,1536]{1,0:T(8,128)(2,1)S(1)}, u32[]{:S(2)}) copy-start(bf16[1024,1536]{1,0:T(8,128)(2,1)S(1)} %get-tuple-element.160.w_ref.wm0.wm1.wm2) | copy-start | bytes 9437188
  28.2 66.4 %copy-start.22 = (s32[27]{0:T(128)}, s32[27]{0:T(128)S(1)}, u32[]{:S(2)}) copy-start(s32[27]{0:T(128)S(1)} %pad_add_fusion.1.info) | copy-start | bytes 328
  33.0 12.5 %copy-start.38 = (bf16[4096]{0:T(1024)(128)(2,1)S(1)}, bf16[4096]{0:T(1024)(128)(2,1)}, u32[]{:S(2)}) copy-start(bf16[4096]{0:T(1024)(128)(2,1)} %param.31) | copy-start | bytes 24580
  34.3 14.8 %collective-permute-start.3 = (bf16[864,1024]{1,0:T(8,128)(2,1)}, bf16[864,1024]{1,0:T(8,128)(2,1)}, u32[]{:S(2)}, u32[]{:S(2)}) collective-permute-start(bf16[864,1024]{1,0:T(8,128)(2,1)} %pad_maximum_fusion.own_ref.inp_ref), channel_id=1, source_target_pairs={{0,4},{1,5},{2,6},{3,7},{4,0},{5,1},{6,2},{7,3},{8,12},{9,13},{10,... | collective-permute-start | bytes 5308424 | tf_op jit(solution)/shard_map/ppermute | solution.py:1033
  49.2 63.6 %collective-permute-start.6 = (bf16[432,1024]{1,0:T(8,128)(2,1)}, bf16[432,1024]{1,0:T(8,128)(2,1)S(1)}, u32[]{:S(2)}, u32[]{:S(2)}) collective-permute-start(bf16[432,1024]{1,0:T(8,128)(2,1)} %get-tuple-element.165), channel_id=1, source_target_pairs={{2,4},{3,5},{4,2},{5,3},{10,12},{11,13},{12,10},{13,11},{18,20},{1... | collective-permute-start | bytes 2654216 | tf_op jit(solution)/shard_map/ppermute | solution.py:1033
  49.9 62.8 %collective-permute-start.7 = (bf16[432,1024]{1,0:T(8,128)(2,1)}, bf16[432,1024]{1,0:T(8,128)(2,1)S(1)}, u32[]{:S(2)}, u32[]{:S(2)}) collective-permute-start(bf16[432,1024]{1,0:T(8,128)(2,1)} %get-tuple-element.166), channel_id=1, source_target_pairs={{0,1},{1,0},{2,5},{3,4},{4,3},{5,2},{6,7},{7,6},{8,9},{9,8},{10,13... | collective-permute-start | bytes 2654216 | tf_op jit(solution)/shard_map/ppermute | solution.py:1033
  90.9 21.7 %copy-start.11 = (bf16[1728,256]{1,0:T(8,128)(2,1)}, bf16[1728,256]{1,0:T(8,128)(2,1)S(1)}, u32[]{:S(2)}) copy-start(bf16[1728,256]{1,0:T(8,128)(2,1)S(1)} %get-tuple-element.164.ctx_a1_ref.a1.b1.o_ref) | copy-start | bytes 2654212
  90.9 21.8 %copy-start.33 = (bf16[432,1024]{1,0:T(8,128)(2,1)S(1)}, bf16[432,1024]{1,0:T(8,128)(2,1)}, u32[]{:S(2)}) copy-start(bf16[432,1024]{1,0:T(8,128)(2,1)} %get-tuple-element.165) | copy-start | bytes 2654212
  90.9 24.7 %collective-permute-start.5 = (bf16[864,256]{1,0:T(8,128)(2,1)S(1)}, bf16[864,256]{1,0:T(8,128)(2,1)S(1)}, u32[]{:S(2)}, u32[]{:S(2)}) collective-permute-start(bf16[864,256]{1,0:T(8,128)(2,1)S(1)} %dynamic-slice_bitcast_fusion.14), channel_id=1, source_target_pairs={{0,4},{1,5},{2,6},{3,7},{4,0},{5,1},{6,2},{7,3},{8,12},{9,13},{10,... | collective-permute-start | bytes 1327112 | tf_op jit(solution)/shard_map/ppermute | solution.py:1033
  112.6 3.0 collective-permute-start.4
  180.8 13.6 %collective-permute-start.11 = (bf16[2048,1024]{1,0:T(8,128)(2,1)}, bf16[2048,1024]{1,0:T(8,128)(2,1)}, u32[]{:S(2)}, u32[]{:S(2)}) collective-permute-start(bf16[2048,1024]{1,0:T(8,128)(2,1)} %weight_grad.8), channel_id=1, source_target_pairs={{0,4},{1,5},{2,6},{3,7},{4,0},{5,1},{6,2},{7,3},{8,12},{9,13},{10,... | collective-permute-start | bytes 12582920 | tf_op jit(solution)/shard_map/ppermute | solution.py:1033
  189.3 15.7 %collective-permute-start.12 = (bf16[512,4096]{1,0:T(8,128)(2,1)}, bf16[512,4096]{1,0:T(8,128)(2,1)}, u32[]{:S(2)}, u32[]{:S(2)}) collective-permute-start(bf16[512,4096]{1,0:T(8,128)(2,1)} %weight_grad.9), channel_id=1, source_target_pairs={{0,4},{1,5},{2,6},{3,7},{4,0},{5,1},{6,2},{7,3},{8,12},{9,13},{10,... | collective-permute-start | bytes 12582920 | tf_op jit(solution)/shard_map/ppermute | solution.py:1033
  189.8 23.0 %collective-permute-start.10 = (bf16[864,1024]{1,0:T(8,128)(2,1)S(1)}, bf16[864,1024]{1,0:T(8,128)(2,1)}, u32[]{:S(2)}, u32[]{:S(2)}) collective-permute-start(bf16[864,1024]{1,0:T(8,128)(2,1)S(1)} %copy-done.10), channel_id=1, source_target_pairs={{0,4},{1,5},{2,6},{3,7},{4,0},{5,1},{6,2},{7,3},{8,12},{9,13},{10,... | collective-permute-start | bytes 5308424 | tf_op jit(solution)/shard_map/ppermute | solution.py:1033
  192.8 69.5 %collective-permute-start.8 = (bf16[432,1024]{1,0:T(8,128)(2,1)}, bf16[432,1024]{1,0:T(8,128)(2,1)}, u32[]{:S(2)}, u32[]{:S(2)}) collective-permute-start(bf16[432,1024]{1,0:T(8,128)(2,1)} %get-tuple-element.185), channel_id=1, source_target_pairs={{2,4},{3,5},{4,2},{5,3},{10,12},{11,13},{12,10},{13,11},{18,20},{1... | collective-permute-start | bytes 2654216 | tf_op jit(solution)/shard_map/ppermute | solution.py:1033
  194.4 67.9 %collective-permute-start.9 = (bf16[432,1024]{1,0:T(8,128)(2,1)}, bf16[432,1024]{1,0:T(8,128)(2,1)}, u32[]{:S(2)}, u32[]{:S(2)}) collective-permute-start(bf16[432,1024]{1,0:T(8,128)(2,1)} %get-tuple-element.303), channel_id=1, source_target_pairs={{0,1},{1,0},{2,5},{3,4},{4,3},{5,2},{6,7},{7,6},{8,9},{9,8},{10,13... | collective-permute-start | bytes 2654216 | tf_op jit(solution)/shard_map/ppermute | solution.py:1033
  203.5 64.9 %collective-permute-start.15 = (bf16[2,2,2,128,1024]{4,3,1,2,0:T(8,128)(2,1)}, bf16[2,2,2,128,1024]{4,3,1,2,0:T(8,128)(2,1)}, u32[]{:S(2)}, u32[]{:S(2)}) collective-permute-start(bf16[2,2,2,128,1024]{4,3,1,2,0:T(8,128)(2,1)} %bitcast.227), channel_id=1, source_target_pairs={{0,8},{1,9},{2,10},{3,11},{4,12},{5,13},{6,14},{7,15},{8,0},{9,1},... | collective-permute-start | bytes 6291464 | tf_op jit(solution)/shard_map/ppermute | solution.py:1033
  220.1 51.2 %collective-permute-start.14 = (bf16[2,2,2,32,4096]{4,3,1,2,0:T(8,128)(2,1)}, bf16[2,2,2,32,4096]{4,3,1,2,0:T(8,128)(2,1)}, u32[]{:S(2)}, u32[]{:S(2)}) collective-permute-start(bf16[2,2,2,32,4096]{4,3,1,2,0:T(8,128)(2,1)} %bitcast.228), channel_id=1, source_target_pairs={{0,16},{1,17},{2,18},{3,19},{4,20},{5,21},{6,22},{7,23},{8,24},{9,... | collective-permute-start | bytes 6291464 | tf_op jit(solution)/shard_map/ppermute | solution.py:1033
  262.4 14.2 %collective-permute-start.13 = (bf16[2,2,2,32,1024]{4,3,1,2,0:T(8,128)(2,1)S(1)}, bf16[2,2,2,32,1024]{4,3,1,2,0:T(8,128)(2,1)S(1)}, u32[]{:S(2)}, u32[]{:S(2)}) collective-permute-start(bf16[2,2,2,32,1024]{4,3,1,2,0:T(8,128)(2,1)S(1)} %bitcast.253), channel_id=1, source_target_pairs={{0,8},{1,9},{2,10},{3,11},{4,12},{5,13},{6,14},{7,15},{8,0},{9,1},... | collective-permute-start | bytes 1572872 | tf_op jit(solution)/shard_map/ppermute | solution.py:1033
  265.2 24.6 %collective-permute-start.16 = (bf16[3,864,256]{2,1,0:T(8,128)(2,1)}, bf16[3,864,256]{2,1,0:T(8,128)(2,1)S(1)}, u32[]{:S(2)}, u32[]{:S(2)}) collective-permute-start(bf16[3,864,256]{2,1,0:T(8,128)(2,1)} %dynamic-slice_bitcast_fusion.1), channel_id=1, source_target_pairs={{0,4},{1,5},{2,6},{3,7},{4,0},{5,1},{6,2},{7,3},{8,12},{9,13},{10,... | collective-permute-start | bytes 3981320 | tf_op jit(solution)/shard_map/ppermute | solution.py:1033
  271.2 12.3 %copy-start.27 = (bf16[2,2,2,128,1024]{4,3,1,2,0:T(8,128)(2,1)}, bf16[2,2,2,128,1024]{4,3,1,2,0:T(8,128)(2,1)S(1)}, u32[]{:S(2)}) copy-start(bf16[2,2,2,128,1024]{4,3,1,2,0:T(8,128)(2,1)S(1)} %fusion) | copy-start | bytes 6291460
  280.5 10.4 %collective-permute-start.17 = (bf16[512,768]{1,0:T(8,128)(2,1)S(1)}, bf16[512,768]{1,0:T(8,128)(2,1)}, u32[]{:S(2)}, u32[]{:S(2)}) collective-permute-start(bf16[512,768]{1,0:T(8,128)(2,1)S(1)} %weight_grad.12), channel_id=1, source_target_pairs={{0,4},{1,5},{2,6},{3,7},{4,0},{5,1},{6,2},{7,3},{8,12},{9,13},{10,... | collective-permute-start | bytes 2359304 | tf_op jit(solution)/shard_map/ppermute | solution.py:1033
  280.7 46.0 %collective-permute-start.20 = (bf16[2,2,32,1024]{3,2,0,1:T(8,128)(2,1)S(1)}, bf16[2,2,32,1024]{3,2,0,1:T(8,128)(2,1)}, u32[]{:S(2)}, u32[]{:S(2)}) collective-permute-start(bf16[2,2,32,1024]{3,2,0,1:T(8,128)(2,1)S(1)} %dynamic-slice_bitcast_fusion.21), channel_id=1, source_target_pairs={{0,16},{1,17},{2,18},{3,19},{4,20},{5,21},{6,22},{7,23},{8,24},{9,... | collective-permute-start | bytes 786440 | tf_op jit(solution)/shard_map/ppermute | solution.py:1033
  282.8 42.3 %collective-permute-start.19 = (bf16[2,2,32,4096]{3,2,0,1:T(8,128)(2,1)}, bf16[2,2,32,4096]{3,2,0,1:T(8,128)(2,1)}, u32[]{:S(2)}, u32[]{:S(2)}) collective-permute-start(bf16[2,2,32,4096]{3,2,0,1:T(8,128)(2,1)} %dynamic-slice_bitcast_fusion.3), channel_id=1, source_target_pairs={{0,8},{1,9},{2,10},{3,11},{4,12},{5,13},{6,14},{7,15},{8,0},{9,1},... | collective-permute-start | bytes 3145736 | tf_op jit(solution)/shard_map/ppermute | solution.py:1033
  284.6 38.6 %collective-permute-start.18 = (bf16[2,2,128,1024]{3,2,0,1:T(8,128)(2,1)}, bf16[2,2,128,1024]{3,2,0,1:T(8,128)(2,1)}, u32[]{:S(2)}, u32[]{:S(2)}) collective-permute-start(bf16[2,2,128,1024]{3,2,0,1:T(8,128)(2,1)} %dynamic-slice_bitcast_fusion.4), channel_id=1, source_target_pairs={{0,16},{1,17},{2,18},{3,19},{4,20},{5,21},{6,22},{7,23},{8,24},{9,... | collective-permute-start | bytes 3145736 | tf_op jit(solution)/shard_map/ppermute | solution.py:1033
  291.0 36.9 %collective-permute-start.22 = (bf16[2,2,2,32,768]{4,3,2,1,0:T(8,128)(2,1)S(1)}, bf16[2,2,2,32,768]{4,3,2,1,0:T(8,128)(2,1)}, u32[]{:S(2)}, u32[]{:S(2)}) collective-permute-start(bf16[2,2,2,32,768]{4,3,2,1,0:T(8,128)(2,1)S(1)} %dynamic-slice_bitcast_fusion.19), channel_id=1, source_target_pairs={{0,8},{1,9},{2,10},{3,11},{4,12},{5,13},{6,14},{7,15},{8,0},{9,1},... | collective-permute-start | bytes 1179656 | tf_op jit(solution)/shard_map/ppermute | solution.py:1033
  302.1 27.2 %collective-permute-start.21 = (bf16[2,2,2,32,768]{4,3,2,1,0:T(8,128)(2,1)}, bf16[2,2,2,32,768]{4,3,2,1,0:T(8,128)(2,1)}, u32[]{:S(2)}, u32[]{:S(2)}) collective-permute-start(bf16[2,2,2,32,768]{4,3,2,1,0:T(8,128)(2,1)} %dynamic-slice_bitcast_fusion.20), channel_id=1, source_target_pairs={{0,16},{1,17},{2,18},{3,19},{4,20},{5,21},{6,22},{7,23},{8,24},{9,... | collective-permute-start | bytes 1179656 | tf_op jit(solution)/shard_map/ppermute | solution.py:1033
  330.6 27.1 %collective-permute-start.24 = (bf16[2,288,1024]{2,1,0:T(8,128)(2,1)S(1)}, bf16[2,288,1024]{2,1,0:T(8,128)(2,1)}, u32[]{:S(2)}, u32[]{:S(2)}) collective-permute-start(bf16[2,288,1024]{2,1,0:T(8,128)(2,1)S(1)} %dynamic-slice_bitcast_fusion.2), channel_id=1, source_target_pairs={{0,1},{1,0},{2,3},{3,2},{4,5},{5,4},{6,7},{7,6},{8,9},{9,8},{10,11... | collective-permute-start | bytes 3538952 | tf_op jit(solution)/shard_map/ppermute | solution.py:1033
  351.6 16.5 %collective-permute-start.23 = (bf16[3,864,256]{2,1,0:T(8,128)(2,1)S(1)}, bf16[3,864,256]{2,1,0:T(8,128)(2,1)S(1)}, u32[]{:S(2)}, u32[]{:S(2)}) collective-permute-start(bf16[3,864,256]{2,1,0:T(8,128)(2,1)S(1)} %dynamic-slice_bitcast_fusion), channel_id=1, source_target_pairs={{0,4},{1,5},{2,6},{3,7},{4,0},{5,1},{6,2},{7,3},{8,12},{9,13},{10,... | collective-permute-start | bytes 3981320 | tf_op jit(solution)/shard_map/ppermute | solution.py:1033
  352.4 22.0 %collective-permute-start.27 = (bf16[2,2,32,768]{3,2,1,0:T(8,128)(2,1)}, bf16[2,2,32,768]{3,2,1,0:T(8,128)(2,1)}, u32[]{:S(2)}, u32[]{:S(2)}) collective-permute-start(bf16[2,2,32,768]{3,2,1,0:T(8,128)(2,1)} %dynamic-slice_bitcast_fusion.25), channel_id=1, source_target_pairs={{0,16},{1,17},{2,18},{3,19},{4,20},{5,21},{6,22},{7,23},{8,24},{9,... | collective-permute-start | bytes 589832 | tf_op jit(solution)/shard_map/ppermute | solution.py:1033
  354.1 22.0 %collective-permute-start.26 = (bf16[2,2,32,768]{3,2,1,0:T(8,128)(2,1)}, bf16[2,2,32,768]{3,2,1,0:T(8,128)(2,1)}, u32[]{:S(2)}, u32[]{:S(2)}) collective-permute-start(bf16[2,2,32,768]{3,2,1,0:T(8,128)(2,1)} %dynamic-slice_bitcast_fusion.26), channel_id=1, source_target_pairs={{0,8},{1,9},{2,10},{3,11},{4,12},{5,13},{6,14},{7,15},{8,0},{9,1},... | collective-permute-start | bytes 589832 | tf_op jit(solution)/shard_map/ppermute | solution.py:1033
  363.2 12.9 %collective-permute-start.29 = (bf16[512,768]{1,0:T(8,128)(2,1)S(1)}, bf16[512,768]{1,0:T(8,128)(2,1)}, u32[]{:S(2)}, u32[]{:S(2)}) collective-permute-start(bf16[512,768]{1,0:T(8,128)(2,1)S(1)} %weight_grad.14), channel_id=1, source_target_pairs={{0,4},{1,5},{2,6},{3,7},{4,0},{5,1},{6,2},{7,3},{8,12},{9,13},{10,... | collective-permute-start | bytes 2359304 | tf_op jit(solution)/shard_map/ppermute | solution.py:1033
  367.0 48.1 %collective-permute-start.32 = (bf16[288,1024]{1,0:T(8,128)(2,1)S(1)}, bf16[288,1024]{1,0:T(8,128)(2,1)}, u32[]{:S(2)}, u32[]{:S(2)}) collective-permute-start(bf16[288,1024]{1,0:T(8,128)(2,1)S(1)} %dynamic-slice_bitcast_fusion.13), channel_id=1, source_target_pairs={{0,2},{1,3},{2,0},{3,1},{4,6},{5,7},{6,4},{7,5},{8,10},{9,11},{10,... | collective-permute-start | bytes 1769480 | tf_op jit(solution)/shard_map/ppermute | solution.py:1033
  374.5 11.3 %collective-permute-start.25 = (bf16[2,2,2,32,768]{4,3,2,1,0:T(8,128)(2,1)S(1)}, bf16[2,2,2,32,768]{4,3,2,1,0:T(8,128)(2,1)S(1)}, u32[]{:S(2)}, u32[]{:S(2)}) collective-permute-start(bf16[2,2,2,32,768]{4,3,2,1,0:T(8,128)(2,1)S(1)} %dynamic-slice_bitcast_fusion.18), channel_id=1, source_target_pairs={{0,8},{1,9},{2,10},{3,11},{4,12},{5,13},{6,14},{7,15},{8,0},{9,1},... | collective-permute-start | bytes 1179656 | tf_op jit(solution)/shard_map/ppermute | solution.py:1033
  376.0 39.1 %copy-start.36 = (f32[8,1024]{1,0:T(8,128)S(1)}, f32[8,1024]{1,0:T(8,128)}, u32[]{:S(2)}) copy-start(f32[8,1024]{1,0:T(8,128)} %get-tuple-element.268) | copy-start | bytes 98308
  376.1 39.7 %copy-start.37 = (f32[1,4096]{1,0:T(1,128)S(1)}, f32[1,4096]{1,0:T(1,128)}, u32[]{:S(2)}) copy-start(f32[1,4096]{1,0:T(1,128)} %get-tuple-element.273) | copy-start | bytes 49156
  377.1 11.0 %collective-permute-start.30 = (bf16[2,2,2,32,768]{4,3,2,1,0:T(8,128)(2,1)S(1)}, bf16[2,2,2,32,768]{4,3,2,1,0:T(8,128)(2,1)S(1)}, u32[]{:S(2)}, u32[]{:S(2)}) collective-permute-start(bf16[2,2,2,32,768]{4,3,2,1,0:T(8,128)(2,1)S(1)} %dynamic-slice_bitcast_fusion.17), channel_id=1, source_target_pairs={{0,16},{1,17},{2,18},{3,19},{4,20},{5,21},{6,22},{7,23},{8,24},{9,... | collective-permute-start | bytes 1179656 | tf_op jit(solution)/shard_map/ppermute | solution.py:1033
  380.1 47.0 %collective-permute-start.36 = (bf16[432,1024]{1,0:T(8,128)(2,1)}, bf16[432,1024]{1,0:T(8,128)(2,1)}, u32[]{:S(2)}, u32[]{:S(2)}) collective-permute-start(bf16[432,1024]{1,0:T(8,128)(2,1)} %get-tuple-element.276), channel_id=1, source_target_pairs={{2,4},{3,5},{4,2},{5,3},{10,12},{11,13},{12,10},{13,11},{18,20},{1... | collective-permute-start | bytes 2654216 | tf_op jit(solution)/shard_map/ppermute | solution.py:1033
  381.9 45.3 %collective-permute-start.37 = (bf16[432,1024]{1,0:T(8,128)(2,1)}, bf16[432,1024]{1,0:T(8,128)(2,1)}, u32[]{:S(2)}, u32[]{:S(2)}) collective-permute-start(bf16[432,1024]{1,0:T(8,128)(2,1)} %get-tuple-element.275), channel_id=1, source_target_pairs={{0,1},{1,0},{2,5},{3,4},{4,3},{5,2},{6,7},{7,6},{8,9},{9,8},{10,13... | collective-permute-start | bytes 2654216 | tf_op jit(solution)/shard_map/ppermute | solution.py:1033
  386.5 40.6 %collective-permute-start.28 = (bf16[2,2,32,768]{3,2,1,0:T(8,128)(2,1)}, bf16[2,2,32,768]{3,2,1,0:T(8,128)(2,1)}, u32[]{:S(2)}, u32[]{:S(2)}) collective-permute-start(bf16[2,2,32,768]{3,2,1,0:T(8,128)(2,1)} %dynamic-slice_bitcast_fusion.24), channel_id=1, source_target_pairs={{0,16},{1,17},{2,18},{3,19},{4,20},{5,21},{6,22},{7,23},{8,24},{9,... | collective-permute-start | bytes 589832 | tf_op jit(solution)/shard_map/ppermute | solution.py:1033
  417.2 2.1 collective-permute-start.33
  419.5 10.0 %copy-start.35 = (bf16[2,2,32,768]{3,2,1,0:T(8,128)(2,1)S(1)}, bf16[2,2,32,768]{3,2,1,0:T(8,128)(2,1)}, u32[]{:S(2)}) copy-start(bf16[2,2,32,768]{3,2,1,0:T(8,128)(2,1)} %fusion.16) | copy-start | bytes 589828
  419.6 4.8 %collective-permute-start.34 = (f32[2,2,2,32,14]{3,2,4,1,0:T(2,128)S(1)}, f32[2,2,2,32,14]{3,2,4,1,0:T(2,128)S(1)}, u32[]{:S(2)}, u32[]{:S(2)}) collective-permute-start(f32[2,2,2,32,14]{3,2,4,1,0:T(2,128)S(1)} %bitcast.257), channel_id=1, source_target_pairs={{0,8},{1,9},{2,10},{3,11},{4,12},{5,13},{6,14},{7,15},{8,0},{9,1},... | collective-permute-start | bytes 43016 | tf_op jit(solution)/shard_map/ppermute | solution.py:1033
  420.3 8.0 %collective-permute-start.31 = (bf16[2,2,32,768]{3,2,1,0:T(8,128)(2,1)S(1)}, bf16[2,2,32,768]{3,2,1,0:T(8,128)(2,1)S(1)}, u32[]{:S(2)}, u32[]{:S(2)}) collective-permute-start(bf16[2,2,32,768]{3,2,1,0:T(8,128)(2,1)S(1)} %dynamic-slice_bitcast_fusion.23), channel_id=1, source_target_pairs={{0,8},{1,9},{2,10},{3,11},{4,12},{5,13},{6,14},{7,15},{8,0},{9,1},... | collective-permute-start | bytes 589832 | tf_op jit(solution)/shard_map/ppermute | solution.py:1033
  424.4 3.9 collective-permute-start.35
  428.4 6.3 %collective-permute-start.39 = (f32[2,32,14]{1,0,2:T(2,128)S(1)}, f32[2,32,14]{1,0,2:T(2,128)S(1)}, u32[]{:S(2)}, u32[]{:S(2)}) collective-permute-start(f32[2,32,14]{1,0,2:T(2,128)S(1)} %bitcast.266), channel_id=1, source_target_pairs={{0,1},{1,0},{2,3},{3,2},{4,5},{5,4},{6,7},{7,6},{8,9},{9,8},{10,11... | collective-permute-start | bytes 10760 | tf_op jit(solution)/shard_map/ppermute | solution.py:1033
  429.7 8.7 %collective-permute-start.38 = (bf16[2,32,3072]{2,1,0:T(8,128)(2,1)S(1)}, bf16[2,32,3072]{2,1,0:T(8,128)(2,1)S(1)}, u32[]{:S(2)}, u32[]{:S(2)}) collective-permute-start(bf16[2,32,3072]{2,1,0:T(8,128)(2,1)S(1)} %dynamic-slice_bitcast_fusion.16), channel_id=1, source_target_pairs={{0,1},{1,0},{2,3},{3,2},{4,5},{5,4},{6,7},{7,6},{8,9},{9,8},{10,11... | collective-permute-start | bytes 1179656 | tf_op jit(solution)/shard_map/ppermute | solution.py:1033
  438.5 6.7 %collective-permute-start.41 = (f32[32,14]{0,1:T(8,128)S(1)}, f32[32,14]{0,1:T(8,128)S(1)}, u32[]{:S(2)}, u32[]{:S(2)}) collective-permute-start(f32[32,14]{0,1:T(8,128)S(1)} %bitcast.269), channel_id=1, source_target_pairs={{0,2},{1,3},{2,0},{3,1},{4,6},{5,7},{6,4},{7,5},{8,10},{9,11},{10,... | collective-permute-start | bytes 5384 | tf_op jit(solution)/shard_map/ppermute | solution.py:1033
  443.6 10.9 %collective-permute-start.40 = (bf16[32,3072]{1,0:T(8,128)(2,1)S(1)}, bf16[32,3072]{1,0:T(8,128)(2,1)S(1)}, u32[]{:S(2)}, u32[]{:S(2)}) collective-permute-start(bf16[32,3072]{1,0:T(8,128)(2,1)S(1)} %dynamic-slice_bitcast_fusion.22), channel_id=1, source_target_pairs={{0,2},{1,3},{2,0},{3,1},{4,6},{5,7},{6,4},{7,5},{8,10},{9,11},{10,... | collective-permute-start | bytes 589832 | tf_op jit(solution)/shard_map/ppermute | solution.py:1033
  (32 other events, 118.7 us)
where the time goes:
time: 466 us; the launch traced here: 457 us
  Pallas kernels  241 us (52%)
  starting transfers between devices  63.4 us (14%)
  waiting for transfers between devices  57.7 us (12%)
  local copies, waits for them, and re-layouts  52.9 us (11%)
  other arithmetic  34.8 us (7%)
  between operations  6.92 us (1%)
    pallas_call x3, Pallas kernels, attn_bwd(): pl.pallas_call(functools.partial(bwd_kernel, bk, into is not None), input...  73.5 us
    ppermute x42, starting transfers between devices, send(): return lax.ppermute(value, AXES, self.perm(target))  63.4 us
    ppermute x42, waiting for transfers between devices, send(): return lax.ppermute(value, AXES, self.perm(target))  57.7 us
    pallas_call x1, Pallas kernels, middle(): pl.pallas_call(functools.partial(middle_kernel, fc), out_shape=(out(model...  54.9 us
    pallas_call x8, Pallas kernels, weight_grad(): pl.pallas_call(functools.partial(grad_kernel, count, extra), out_shape=ja...  46.2 us
    pallas_call x2, Pallas kernels, attn_fwd(): pl.pallas_call(functools.partial(fwd_kernel, bq), out_shape=(jax.ShapeDty...  35.6 us
    convert_element_type x16, other arithmetic, add(): self.terms = total.astype(self.terms.dtype) if self.axes else total  19.8 us
    unnamed x130, local copies, waits for them, and re-layouts  19.8 us
  transfers between devices with their start and end apart: 42, of which 12 were waited for; matrix products, arithmetic and copies ran while one was open for 13% of the time, Pallas kernels for 39%

commit v1 on v0

--- a/solution.py
+++ b/solution.py
@@ -1276,32 +1276,35 @@
             item.terms, other = tie(item.terms, other)
         return other
 
-    grads, b_sum0 = back(0, quads // 2)
-    got = away_rows(grads)
-    output_got, grads = tie(output_got, grads)
-    grads = settle([down, up, out], grads)
+    grads0, b_sum0 = back(0, quads // 2)
+    got0 = away_rows(grads0)
+    output_got, grads0 = tie(output_got, grads0)
+    cross0, keep0 = products(grads0)
+    cross0.terms, keep0.terms, grad_context = tie(cross0.terms, keep0.terms, grad_context)
+    down.got, up.got, keep0.terms = tie(down.got, up.got, keep0.terms)
+    down.add()
+    up.add()
+    down.terms, up.terms, grad_context = tie(down.terms, up.terms, grad_context)
     down.send("y")
     up.send("x")
-    out.send("y")
-    cross0, keep0 = products(grads)
-    got, cross0.terms, keep0.terms = tie(got, cross0.terms, keep0.terms)
-    (grad_start,) = add_start(core, grad_one, grads, got, w_own, w_oth, 0, False)
     keep0.send("x")
     cross0.send("y")
-    grad_context, grad_start = tie(grad_context, grad_start)
     grads, b_sum1 = back(quads // 2, quads // 4)
-    grads = settle([down, up, out, keep0, cross0], grads)
+    grads, grads0, got0 = tie(grads, grads0, got0)
+    (grad_start,) = add_start(core, grad_one, grads0, got0, w_own, w_oth, 0, False)
+    grad_start = settle([down, up, out], grad_start)
+    out.send("y")
     wide_rows = up.terms.shape[-2]
     slabs = [up.terms[..., i * model : (i + 1) * model] for i in range(up.terms.shape[-1] // model)]
-    ffn = jnp.concatenate([down.terms, *slabs, out.terms], axis=2)
-    ffn, grads = tie(ffn, grads)
+    ffn = jnp.concatenate([down.terms, *slabs], axis=2)
+    ffn, grads, grad_start = tie(ffn, grads, grad_start)
     ffn = Sum(plan, ffn, where, "hl").send("l")
+    grads, b_sum2 = back(quads // 2 + quads // 4, quads // 4, grads)
+    got = away_rows(grads)
+    grads = settle([ffn, keep0, cross0, out], grads)
+    ffn.send("h")
     keep0.send("y")
     cross0.send("x")
-    grads, b_sum2 = back(quads // 2 + quads // 4, quads // 4, grads)
-    got = away_rows(grads)
-    grads = settle([ffn], grads)
-    ffn.send("h")
     cross1, keep1 = products(grads)
     got, keep1.terms = tie(got, keep1.terms)
     keep1.send("x")
@@ -1333,7 +1336,7 @@
     keep1.add()
     cross1.add()
     small.add()
-    late = jnp.concatenate([i.terms for i in (keep0, cross0, keep1, cross1)], axis=3)
+    late = jnp.concatenate([i.terms for i in (keep0, cross0, keep1, cross1, out)], axis=3)
     late = Sum(plan, late, where, "hl").send("l")
     small.send("l")
     late.got, small.got = tie(late.got, small.got)
@@ -1348,8 +1351,8 @@
     keeps = [late[:, :wide], late[:, 2 * wide : 3 * wide]]
     crosses = [late[:, wide : 2 * wide], late[:, 3 * wide : 4 * wide]]
     ffn = ffn.add()
-    count = ffn.shape[0] - wide_rows * (len(slabs) + 1)
-    sum_w_down, sum_w_out = ffn[:count], ffn[count + wide_rows * len(slabs) :]
+    count = ffn.shape[0] - wide_rows * len(slabs)
+    sum_w_down, sum_w_out = ffn[:count], late[:, 4 * wide :]
     sum_w_up = jnp.concatenate(
         [ffn[count + i * wide_rows : count + (i + 1) * wide_rows] for i in range(len(slabs))], axis=1
     )

time: 466 us -> 463 us (level)
  waiting for transfers between devices: 57.7 us -> 40.6 us
  starting transfers between devices: 63.4 us -> 73.1 us
    ppermute x42, waiting for transfers between devices: 57.7 us -> 40.6 us  [send(): return lax.ppermute(value, AXES, self.perm(target))]
    ppermute x42, starting transfers between devices: 63.4 us -> 73.1 us  [send(): return lax.ppermute(value, AXES, self.perm(target))]
    unnamed x130 -> x153, local copies, waits for them, and re-layouts: 19.8 us -> 22.8 us
    squeeze x24 -> x23, local copies, waits for them, and re-layouts: 18.6 us -> 16.5 us  [pick(): return lax.dynamic_index_in_dim(array, index, axis, keepdims=False)]
    convert_element_type x16 -> x14, other arithmetic: 19.8 us -> 18.8 us  [add(): self.terms = total.astype(self.terms.dtype) if self.axes else total]
  transfers between devices with their start and end apart: 42 -> 42, of which waited for: 12 -> 11; matrix products, arithmetic and copies ran while one was open for 13% -> 13% of each run, Pallas kernels for 39% -> 40%
where the time goes in v1:
time: 463 us; the launch traced here: 454 us
  Pallas kernels  242 us (52%)
  starting transfers between devices  73.1 us (16%)
  local copies, waits for them, and re-layouts  56.3 us (12%)
  waiting for transfers between devices  40.6 us (9%)
  other arithmetic  34.6 us (7%)
  between operations  7.12 us (2%)
    pallas_call x3, Pallas kernels, attn_bwd(): pl.pallas_call(functools.partial(bwd_kernel, bk, into is not None), input...  73.9 us
    ppermute x42, starting transfers between devices, send(): return lax.ppermute(value, AXES, self.perm(target))  73.1 us
    pallas_call x1, Pallas kernels, middle(): pl.pallas_call(functools.partial(middle_kernel, fc), out_shape=(out(model...  54.9 us
    pallas_call x8, Pallas kernels, weight_grad(): pl.pallas_call(functools.partial(grad_kernel, count, extra), out_shape=ja...  46.4 us
    ppermute x42, waiting for transfers between devices, send(): return lax.ppermute(value, AXES, self.perm(target))  40.6 us
    pallas_call x2, Pallas kernels, attn_fwd(): pl.pallas_call(functools.partial(fwd_kernel, bq), out_shape=(jax.ShapeDty...  35.6 us
    unnamed x153, local copies, waits for them, and re-layouts  22.8 us
    convert_element_type x14, other arithmetic, add(): self.terms = total.astype(self.terms.dtype) if self.axes else total  18.8 us
  transfers between devices with their start and end apart: 42, of which 11 were waited for; matrix products, arithmetic and copies ran while one was open for 13% of the time, Pallas kernels for 40%

profile of v1, /device:TPU:0, one launch (start us, length us, event | category | flops | bytes accessed | tf_op | source)
XLA Modules:
  0.0 454.1 jit_solution(8697970060816704207)
XLA Ops:
  3.4 2.8 dynamic-slice_bitcast_fusion.12
  6.3 1.7 collective-permute-start.1
  8.0 3.0 collective-permute-start.2
  12.1 2.6 collective-permute-start
  16.4 2.8 copy-done.10
  19.2 3.7 split_columns.1
  22.9 1.7 copy-done.4
  28.2 3.2 collective-permute-done.2
  31.4 1.6 broadcast_select_fusion.3
  34.4 11.2 %collective-permute-start.3 = (bf16[864,1024]{1,0:T(8,128)(2,1)}, bf16[864,1024]{1,0:T(8,128)(2,1)}, u32[]{:S(2)}, u32[]{:S(2)}) collective-permute-start(bf16[864,1024]{1,0:T(8,128)(2,1)} %pad_maximum_fusion.own_ref.inp_ref), channel_id=1, source_target_pairs={{0,4},{1,5},{2,6},{3,7},{4,0},{5,1},{6,2},{7,3},{8,12},{9,13},{10,... | collective-permute-start | bytes 5308424 | tf_op jit(solution)/shard_map/ppermute | solution.py:1033
  46.8 2.4 collective-permute-done.3.oth_ref
  49.9 10.2 %collective-permute-start.7 = (bf16[432,1024]{1,0:T(8,128)(2,1)}, bf16[432,1024]{1,0:T(8,128)(2,1)S(1)}, u32[]{:S(2)}, u32[]{:S(2)}) collective-permute-start(bf16[432,1024]{1,0:T(8,128)(2,1)} %get-tuple-element.166), channel_id=1, source_target_pairs={{0,1},{1,0},{2,5},{3,4},{4,3},{5,2},{6,7},{7,6},{8,9},{9,8},{10,13... | collective-permute-start | bytes 2654216 | tf_op jit(solution)/shard_map/ppermute | solution.py:1033
  60.1 9.2 %project.1 = (bf16[1728,1536]{1,0:T(8,128)(2,1)}, bf16[1728,1024]{1,0:T(8,128)(2,1)S(1)}) custom-call(s32[1]{0:T(128)} %bitcast.1.sel_ref.refs_0_, f32[1]{0:T(128)} %bitcast.3.frac_ref, bf16[864,1024]{1,0:T(8,128)(2,1)} %pad_maximum_fusion.own_ref.inp_ref, bf16[864,1024]{1,0:T(8,128)(2,1)} %collective-permute-done.3.oth_ref, f32[8,1024]{1,0:T(8,128)S(1)} %stack.89.vec_ref, ...), custom_call_target="tpu_custom_call" | custom-call | flops 5435817984 | bytes 15532032 | tf_op jit(solution)/shard_map/project/pallas_call | solution.py:864
  69.3 1.8 copy-done
  71.1 17.7 %attn_forward.3 = (bf16[1728,256]{1,0:T(8,128)(2,1)S(1)}, bf16[1728,256]{1,0:T(8,128)(2,1)S(1)}, bf16[4,1728,128]{2,1,0:T(8,128)(2,1)S(1)}) custom-call(s32[27]{0:T(128)S(1)} %pad_add_fusion.1.info, bf16[1728,1536]{1,0:T(8,128)(2,1)} %get-tuple-element.162.q_ref.k_ref.v_ref, bf16[1728,1536]{1,0:T(8,128)(2,1)} %get-tuple-element.162.q_ref.k_ref.v_ref, ...), custom_call_target="tpu_custom_call" | custom-call | flops 12230590464 | bytes 4423680 | tf_op jit(solution)/shard_map/attn_forward/pallas_call | solution.py:117
  90.9 3.7 collective-permute-start.5
  94.6 17.9 %attn_forward.2 = (bf16[1728,256]{1,0:T(8,128)(2,1)S(1)}, bf16[1728,256]{1,0:T(8,128)(2,1)S(1)}, bf16[4,1728,128]{2,1,0:T(8,128)(2,1)S(1)}) custom-call(s32[27]{0:T(128)S(1)} %pad_add_fusion.1.info, bf16[1728,1536]{1,0:T(8,128)(2,1)} %get-tuple-element.162.q_ref.k_ref.v_ref, bf16[1728,1536]{1,0:T(8,128)(2,1)} %get-tuple-element.162.q_ref.k_ref.v_ref, ...), custom_call_target="tpu_custom_call" | custom-call | flops 12230590464 | bytes 4423680 | tf_op jit(solution)/shard_map/attn_forward/pallas_call | solution.py:117
  117.2 54.9 %middle.1 = (bf16[864,1024]{1,0:T(8,128)(2,1)}, bf16[864,1024]{1,0:T(8,128)(2,1)}, bf16[864,4096]{1,0:T(8,128)(2,1)}, bf16[864,1024]{1,0:T(8,128)(2,1)}, bf16[86...) custom-call(s32[1]{0:T(128)} %bitcast.1.sel_ref.refs_0_, ...), custom_call_target="tpu_custom_call" | custom-call | flops 30802968576 | bytes 45088768 | tf_op jit(solution)/shard_map/middle/pallas_call | solution.py:698
  172.1 1.5 copy-done.18
  173.6 7.8 %weight_grad.8 = bf16[2048,1024]{1,0:T(8,128)(2,1)} custom-call(s32[1]{0:T(128)S(6)} %sub.27.refs_0_, bf16[864,4096]{1,0:T(8,128)(2,1)} %get-tuple-element.176.refs_1_, bf16[864,1024]{1,0:T(8,128)(2,1)S(1)} %copy-done.18), custom_call_target="tpu_custom_call" | custom-call | flops 3623878656 | bytes 9502720 | tf_op jit(solution)/shard_map/weight_grad/pallas_call | solution.py:799
  181.4 8.5 %weight_grad.9 = bf16[512,4096]{1,0:T(8,128)(2,1)} custom-call(s32[1]{0:T(128)S(6)} %sub.27.refs_0_, bf16[864,1024]{1,0:T(8,128)(2,1)S(1)} %copy-done.1, bf16[864,1024]{1,0:T(8,128)(2,1)S(1)} %copy-done.1, bf16[864,1024]{1,0:T(8,128)(2,1)S(1)} %copy-done.1, bf16[864,1024]{1,0:T(8,128)(2,1)S(1)} %copy-done.1, bf16[864,4096]{1,0:T(8,128)(2,1)} %get-tuple-element.175.refs_5_), custom_call_target="tpu_custom_call" | custom-call | flops 3623878656 | bytes 12156928 | tf_op jit(solution)/shard_map/weight_grad/pallas_call | solution.py:799
  190.4 2.9 dynamic-slice_bitcast_fusion.7
  193.4 1.6 collective-permute-start.8
  195.0 7.0 %weight_grad.10 = bf16[2048,1024]{1,0:T(8,128)(2,1)S(1)} custom-call(s32[1]{0:T(128)} %bitcast.1.sel_ref.refs_0_, bf16[864,4096]{1,0:T(8,128)(2,1)} %get-tuple-element.176.refs_1_, bf16[864,1024]{1,0:T(8,128)(2,1)S(1)} %copy-done.19, bf16[2048,1024]{1,0:T(8,128)(2,1)} %collective-permute-done.11.refs_3_), custom_call_target="tpu_custom_call" | custom-call | flops 3623878656 | bytes 13697024 | tf_op jit(solution)/shard_map/weight_grad/pallas_call | solution.py:799
  202.1 7.9 %weight_grad.11 = bf16[512,4096]{1,0:T(8,128)(2,1)S(1)} custom-call(s32[1]{0:T(128)} %bitcast.1.sel_ref.refs_0_, bf16[864,1024]{1,0:T(8,128)(2,1)S(1)} %copy-done.1, bf16[864,1024]{1,0:T(8,128)(2,1)S(1)} %copy-done.1, bf16[864,1024]{1,0:T(8,128)(2,1)S(1)} %copy-done.1, bf16[864,1024]{1,0:T(8,128)(2,1)S(1)} %copy-done.1, ...), custom_call_target="tpu_custom_call" | custom-call | flops 3623878656 | bytes 16351232 | tf_op jit(solution)/shard_map/weight_grad/pallas_call | solution.py:799
  210.0 3.9 out_grad.1
  215.6 1.5 collective-permute-start.19
  217.6 1.6 copy.305
  219.2 1.5 collective-permute-start.14
  221.2 1.5 copy.306
  223.5 4.4 context_grad.1.g_ref
  229.2 35.0 %attn_backward.3 = (bf16[3,1728,256]{2,1,0:T(8,128)(2,1)}, f32[2,256]{1,0:T(2,128)}) custom-call(s32[27]{0:T(128)} %copy-done.22, bf16[4,1728,128]{2,1,0:T(8,128)(2,1)} %copy-done.24, bf16[1728,1536]{1,0:T(8,128)(2,1)} %get-tuple-element.162.q_ref.k_ref.v_ref, bf16[1728,1536]{1,0:T(8,128)(2,1)} %get-tuple-element.162.q_ref.k_ref.v_ref, ...), custom_call_target="tpu_custom_call" | custom-call | flops 30576476160 | bytes 7077888 | tf_op jit(solution)/shard_map/attn_backward/pallas_call | solution.py:216
  264.2 1.7 copy-done.6
  266.0 3.6 weight_grad.12
  271.8 4.0 weight_grad.13
  275.9 1.6 select_bitcast_fusion.3
  280.2 2.4 fusion
  282.6 3.3 fusion.1
  288.3 1.5 collective-permute-start.16
  289.9 19.7 %attn_backward.4 = (bf16[3,1728,256]{2,1,0:T(8,128)(2,1)}, f32[2,128]{1,0:T(2,128)}) custom-call(s32[27]{0:T(128)} %copy-done.22, bf16[4,1728,128]{2,1,0:T(8,128)(2,1)} %copy-done.23, bf16[1728,1536]{1,0:T(8,128)(2,1)} %get-tuple-element.162.q_ref.k_ref.v_ref, bf16[1728,1536]{1,0:T(8,128)(2,1)} %get-tuple-element.162.q_ref.k_ref.v_ref, ...), custom_call_target="tpu_custom_call" | custom-call | flops 15288238080 | bytes 3538944 | tf_op jit(solution)/shard_map/attn_backward/pallas_call | solution.py:216
  311.9 1.7 copy-done.8
  313.6 5.3 %add_start.2.base_ref = f32[864,1024]{1,0:T(8,128)S(1)} custom-call(s32[1]{0:T(128)} %bitcast.1.sel_ref.refs_0_, f32[864,1024]{1,0:T(8,128)} %get-tuple-element.202.base_ref, bf16[3,1728,256]{2,1,0:T(8,128)(2,1)S(1)} %copy-done.8, bf16[3,864,256]{2,1,0:T(8,128)(2,1)} %collective-permute-done.17.got_ref, bf16[1024,1536]{1,0:T(8,128)(2,1)S(1)} %copy-done.3, ...), custom_call_target="tpu_custom_call" | custom-call | flops 2717908992 | bytes 12877824 | tf_op jit(solution)/shard_map/add_start/pallas_call | solution.py:983
  319.0 2.6 fusion.4
  322.1 1.5 fusion.3
  327.5 19.2 %attn_backward.5 = (bf16[3,1728,256]{2,1,0:T(8,128)(2,1)}, f32[2,128]{1,0:T(2,128)}) custom-call(s32[27]{0:T(128)} %copy-done.22, bf16[4,1728,128]{2,1,0:T(8,128)(2,1)} %copy-done.23, bf16[1728,1536]{1,0:T(8,128)(2,1)} %get-tuple-element.162.q_ref.k_ref.v_ref, ...), custom_call_target="tpu_custom_call", output_to_operand_aliasing={{0}: (7, {})} | custom-call | flops 15288238080 | bytes 3538944 | tf_op jit(solution)/shard_map/attn_backward/pallas_call | solution.py:216
  347.3 1.4 dynamic-slice_bitcast_fusion
  349.0 3.1 collective-permute-done.24
  352.1 1.6 fusion.2
  356.9 3.9 weight_grad.14
  363.3 3.0 collective-permute-start.32
  366.3 3.6 weight_grad.15
  369.9 5.0 %add_start.3 = (bf16[864,1024]{1,0:T(8,128)(2,1)S(1)}, f32[1,1024]{1,0:T(1,128)S(1)}) custom-call(s32[1]{0:T(128)} %bitcast.1.sel_ref.refs_0_, f32[864,1024]{1,0:T(8,128)} %copy-done.11, bf16[3,1728,256]{2,1,0:T(8,128)(2,1)S(1)} %copy-done.9, bf16[3,864,256]{2,1,0:T(8,128)(2,1)S(1)} %collective-permute-done.20.got_ref, bf16[1024,1536]{1,0:T(8,128)(2,1)S(1)} %copy-done.3, ...), custom_call_target="tpu_custom_call" | custom-call | flops 2717908992 | bytes 12877824 | tf_op jit(solution)/shard_map/add_start/pallas_call | solution.py:983
  378.9 1.6 collective-permute-start.36
  382.0 1.6 collective-permute-start.30
  383.6 4.1 collective-permute-done.25
  388.7 1.6 collective-permute-start.28
  390.3 3.0 collective-permute-done.30
  406.3 1.6 collective-permute-start.35
  409.5 8.6 %collective-permute-done.37 = bf16[432,1024]{1,0:T(8,128)(2,1)} collective-permute-done((bf16[432,1024]{1,0:T(8,128)(2,1)}, bf16[432,1024]{1,0:T(8,128)(2,1)}, u32[]{:S(2)}, u32[]{:S(2)}) %collective-permute-start.37) | collective-permute-done | bytes 884768 | tf_op jit(solution)/shard_map/ppermute | solution.py:1033
  419.5 2.1 collective-permute-start.39
  424.2 4.5 collective-permute-done.39
  428.8 11.2 %collective-permute-start.41 = (f32[32,14]{0,1:T(8,128)S(1)}, f32[32,14]{0,1:T(8,128)S(1)}, u32[]{:S(2)}, u32[]{:S(2)}) collective-permute-start(f32[32,14]{0,1:T(8,128)S(1)} %bitcast.274), channel_id=1, source_target_pairs={{0,2},{1,3},{2,0},{3,1},{4,6},{5,7},{6,4},{7,5},{8,10},{9,11},{10,... | collective-permute-start | bytes 5384 | tf_op jit(solution)/shard_map/ppermute | solution.py:1033
  440.2 3.7 collective-permute-done.41
  445.2 5.9 %collective-permute-done.40 = bf16[32,4096]{1,0:T(8,128)(2,1)S(1)} collective-permute-done((bf16[32,4096]{1,0:T(8,128)(2,1)S(1)}, bf16[32,4096]{1,0:T(8,128)(2,1)S(1)}, u32[]{:S(2)}, u32[]{:S(2)}) %collective-permute-start.40) | collective-permute-done | bytes 262176 | tf_op jit(solution)/shard_map/ppermute | solution.py:1033
  (323 shorter events, 68.9 us)
Async XLA Ops:
  0.7 11.2 %copy-start.64 = (s32[2]{0:T(128)S(1)}, s32[2]{0:T(128)}, u32[]{:S(2)}) copy-start(s32[2]{0:T(128)} %param.20) | copy-start | bytes 28
  0.7 14.0 %copy-start.37 = (bf16[2,432,1024]{2,1,0:T(8,128)(2,1)S(1)}, bf16[2,432,1024]{2,1,0:T(8,128)(2,1)}, u32[]{:S(2)}) copy-start(bf16[2,432,1024]{2,1,0:T(8,128)(2,1)} %param.22) | copy-start | bytes 5308420
  6.2 10.0 %copy-start.56 = (bf16[1024]{0:T(1024)(128)(2,1)S(1)}, bf16[1024]{0:T(1024)(128)(2,1)}, u32[]{:S(2)}) copy-start(bf16[1024]{0:T(1024)(128)(2,1)} %param.29) | copy-start | bytes 6148
  6.2 10.0 %copy-start.57 = (bf16[1024]{0:T(1024)(128)(2,1)S(1)}, bf16[1024]{0:T(1024)(128)(2,1)}, u32[]{:S(2)}) copy-start(bf16[1024]{0:T(1024)(128)(2,1)} %param.33) | copy-start | bytes 6148
  6.2 10.0 %copy-start.58 = (bf16[1024]{0:T(1024)(128)(2,1)S(1)}, bf16[1024]{0:T(1024)(128)(2,1)}, u32[]{:S(2)}) copy-start(bf16[1024]{0:T(1024)(128)(2,1)} %param.34) | copy-start | bytes 6148
  6.3 10.0 %copy-start.59 = (bf16[1024]{0:T(1024)(128)(2,1)S(1)}, bf16[1024]{0:T(1024)(128)(2,1)}, u32[]{:S(2)}) copy-start(bf16[1024]{0:T(1024)(128)(2,1)} %param.35) | copy-start | bytes 6148
  6.3 21.9 %collective-permute-start.1 = (bf16[432,1024]{1,0:T(8,128)(2,1)}, bf16[432,1024]{1,0:T(8,128)(2,1)}, u32[]{:S(2)}, u32[]{:S(2)}) collective-permute-start(bf16[432,1024]{1,0:T(8,128)(2,1)} %get-tuple-element.307), channel_id=1, source_target_pairs={{2,4},{3,5},{4,2},{5,3},{10,12},{11,13},{12,10},{13,11},{18,20},{1... | collective-permute-start | bytes 2654216 | tf_op jit(solution)/shard_map/ppermute | solution.py:1033
  8.0 23.4 %collective-permute-start.2 = (bf16[432,1024]{1,0:T(8,128)(2,1)}, bf16[432,1024]{1,0:T(8,128)(2,1)}, u32[]{:S(2)}, u32[]{:S(2)}) collective-permute-start(bf16[432,1024]{1,0:T(8,128)(2,1)} %get-tuple-element.308), channel_id=1, source_target_pairs={{0,1},{1,0},{2,5},{3,4},{4,3},{5,2},{6,7},{7,6},{8,9},{9,8},{10,13... | collective-permute-start | bytes 2654216 | tf_op jit(solution)/shard_map/ppermute | solution.py:1033
  12.1 12.5 %collective-permute-start = (s32[2,16]{1,0:T(2,128)S(1)}, s32[2,16]{1,0:T(2,128)S(1)}, u32[]{:S(2)}, u32[]{:S(2)}) collective-permute-start(s32[2,16]{1,0:T(2,128)S(1)} %pad_add_fusion), channel_id=1, source_target_pairs={{0,4},{1,5},{2,6},{3,7},{4,0},{5,1},{6,2},{7,3},{8,12},{9,13},{10,... | collective-permute-start | bytes 392 | tf_op jit(solution)/shard_map/ppermute | solution.py:1033
  16.4 43.7 %copy-start.21 = (f32[8,1024]{1,0:T(8,128)}, f32[8,1024]{1,0:T(8,128)S(1)}, u32[]{:S(2)}) copy-start(f32[8,1024]{1,0:T(8,128)S(1)} %stack.89.vec_ref) | copy-start | bytes 98308
  24.6 35.5 %copy-start.2 = (bf16[1024,1536]{1,0:T(8,128)(2,1)}, bf16[1024,1536]{1,0:T(8,128)(2,1)S(1)}, u32[]{:S(2)}) copy-start(bf16[1024,1536]{1,0:T(8,128)(2,1)S(1)} %get-tuple-element.160.w_ref.wm0.wm1.wm2) | copy-start | bytes 9437188
  28.2 66.4 %copy-start.22 = (s32[27]{0:T(128)}, s32[27]{0:T(128)S(1)}, u32[]{:S(2)}) copy-start(s32[27]{0:T(128)S(1)} %pad_add_fusion.1.info) | copy-start | bytes 328
  33.0 12.5 %copy-start.49 = (bf16[4096]{0:T(1024)(128)(2,1)S(1)}, bf16[4096]{0:T(1024)(128)(2,1)}, u32[]{:S(2)}) copy-start(bf16[4096]{0:T(1024)(128)(2,1)} %param.31) | copy-start | bytes 24580
  34.4 14.8 %collective-permute-start.3 = (bf16[864,1024]{1,0:T(8,128)(2,1)}, bf16[864,1024]{1,0:T(8,128)(2,1)}, u32[]{:S(2)}, u32[]{:S(2)}) collective-permute-start(bf16[864,1024]{1,0:T(8,128)(2,1)} %pad_maximum_fusion.own_ref.inp_ref), channel_id=1, source_target_pairs={{0,4},{1,5},{2,6},{3,7},{4,0},{5,1},{6,2},{7,3},{8,12},{9,13},{10,... | collective-permute-start | bytes 5308424 | tf_op jit(solution)/shard_map/ppermute | solution.py:1033
  49.2 63.5 %collective-permute-start.6 = (bf16[432,1024]{1,0:T(8,128)(2,1)}, bf16[432,1024]{1,0:T(8,128)(2,1)S(1)}, u32[]{:S(2)}, u32[]{:S(2)}) collective-permute-start(bf16[432,1024]{1,0:T(8,128)(2,1)} %get-tuple-element.165), channel_id=1, source_target_pairs={{2,4},{3,5},{4,2},{5,3},{10,12},{11,13},{12,10},{13,11},{18,20},{1... | collective-permute-start | bytes 2654216 | tf_op jit(solution)/shard_map/ppermute | solution.py:1033
  49.9 62.8 %collective-permute-start.7 = (bf16[432,1024]{1,0:T(8,128)(2,1)}, bf16[432,1024]{1,0:T(8,128)(2,1)S(1)}, u32[]{:S(2)}, u32[]{:S(2)}) collective-permute-start(bf16[432,1024]{1,0:T(8,128)(2,1)} %get-tuple-element.166), channel_id=1, source_target_pairs={{0,1},{1,0},{2,5},{3,4},{4,3},{5,2},{6,7},{7,6},{8,9},{9,8},{10,13... | collective-permute-start | bytes 2654216 | tf_op jit(solution)/shard_map/ppermute | solution.py:1033
  90.9 21.7 %copy-start.13 = (bf16[1728,256]{1,0:T(8,128)(2,1)}, bf16[1728,256]{1,0:T(8,128)(2,1)S(1)}, u32[]{:S(2)}) copy-start(bf16[1728,256]{1,0:T(8,128)(2,1)S(1)} %get-tuple-element.164.ctx_a1_ref.a1.b1.o_ref) | copy-start | bytes 2654212
  90.9 21.8 %copy-start.33 = (bf16[432,1024]{1,0:T(8,128)(2,1)S(1)}, bf16[432,1024]{1,0:T(8,128)(2,1)}, u32[]{:S(2)}) copy-start(bf16[432,1024]{1,0:T(8,128)(2,1)} %get-tuple-element.165) | copy-start | bytes 2654212
  90.9 24.8 %collective-permute-start.5 = (bf16[864,256]{1,0:T(8,128)(2,1)S(1)}, bf16[864,256]{1,0:T(8,128)(2,1)S(1)}, u32[]{:S(2)}, u32[]{:S(2)}) collective-permute-start(bf16[864,256]{1,0:T(8,128)(2,1)S(1)} %dynamic-slice_bitcast_fusion.15), channel_id=1, source_target_pairs={{0,4},{1,5},{2,6},{3,7},{4,0},{5,1},{6,2},{7,3},{8,12},{9,13},{10,... | collective-permute-start | bytes 1327112 | tf_op jit(solution)/shard_map/ppermute | solution.py:1033
  112.6 3.1 collective-permute-start.4
  181.4 13.6 %collective-permute-start.11 = (bf16[2048,1024]{1,0:T(8,128)(2,1)}, bf16[2048,1024]{1,0:T(8,128)(2,1)}, u32[]{:S(2)}, u32[]{:S(2)}) collective-permute-start(bf16[2048,1024]{1,0:T(8,128)(2,1)} %weight_grad.8), channel_id=1, source_target_pairs={{0,4},{1,5},{2,6},{3,7},{4,0},{5,1},{6,2},{7,3},{8,12},{9,13},{10,... | collective-permute-start | bytes 12582920 | tf_op jit(solution)/shard_map/ppermute | solution.py:1033
  189.9 12.1 %collective-permute-start.12 = (bf16[512,4096]{1,0:T(8,128)(2,1)}, bf16[512,4096]{1,0:T(8,128)(2,1)}, u32[]{:S(2)}, u32[]{:S(2)}) collective-permute-start(bf16[512,4096]{1,0:T(8,128)(2,1)} %weight_grad.9), channel_id=1, source_target_pairs={{0,4},{1,5},{2,6},{3,7},{4,0},{5,1},{6,2},{7,3},{8,12},{9,13},{10,... | collective-permute-start | bytes 12582920 | tf_op jit(solution)/shard_map/ppermute | solution.py:1033
  190.4 19.5 %collective-permute-start.10 = (bf16[864,1024]{1,0:T(8,128)(2,1)S(1)}, bf16[864,1024]{1,0:T(8,128)(2,1)}, u32[]{:S(2)}, u32[]{:S(2)}) collective-permute-start(bf16[864,1024]{1,0:T(8,128)(2,1)S(1)} %copy-done.12), channel_id=1, source_target_pairs={{0,4},{1,5},{2,6},{3,7},{4,0},{5,1},{6,2},{7,3},{8,12},{9,13},{10,... | collective-permute-start | bytes 5308424 | tf_op jit(solution)/shard_map/ppermute | solution.py:1033
  193.4 70.8 %collective-permute-start.8 = (bf16[432,1024]{1,0:T(8,128)(2,1)}, bf16[432,1024]{1,0:T(8,128)(2,1)}, u32[]{:S(2)}, u32[]{:S(2)}) collective-permute-start(bf16[432,1024]{1,0:T(8,128)(2,1)} %get-tuple-element.185), channel_id=1, source_target_pairs={{2,4},{3,5},{4,2},{5,3},{10,12},{11,13},{12,10},{13,11},{18,20},{1... | collective-permute-start | bytes 2654216 | tf_op jit(solution)/shard_map/ppermute | solution.py:1033
  195.0 69.2 %collective-permute-start.9 = (bf16[432,1024]{1,0:T(8,128)(2,1)}, bf16[432,1024]{1,0:T(8,128)(2,1)}, u32[]{:S(2)}, u32[]{:S(2)}) collective-permute-start(bf16[432,1024]{1,0:T(8,128)(2,1)} %get-tuple-element.303), channel_id=1, source_target_pairs={{0,1},{1,0},{2,5},{3,4},{4,3},{5,2},{6,7},{7,6},{8,9},{9,8},{10,13... | collective-permute-start | bytes 2654216 | tf_op jit(solution)/shard_map/ppermute | solution.py:1033
  215.6 108.1 %collective-permute-start.19 = (bf16[2,2,2,32,1024]{4,3,1,2,0:T(8,128)(2,1)}, bf16[2,2,2,32,1024]{4,3,1,2,0:T(8,128)(2,1)}, u32[]{:S(2)}, u32[]{:S(2)}) collective-permute-start(bf16[2,2,2,32,1024]{4,3,1,2,0:T(8,128)(2,1)} %bitcast.233), channel_id=1, source_target_pairs={{0,8},{1,9},{2,10},{3,11},{4,12},{5,13},{6,14},{7,15},{8,0},{9,1},... | collective-permute-start | bytes 1572872 | tf_op jit(solution)/shard_map/ppermute | solution.py:1033
  219.2 61.0 %collective-permute-start.14 = (bf16[2,2,2,32,4096]{4,3,1,2,0:T(8,128)(2,1)}, bf16[2,2,2,32,4096]{4,3,1,2,0:T(8,128)(2,1)}, u32[]{:S(2)}, u32[]{:S(2)}) collective-permute-start(bf16[2,2,2,32,4096]{4,3,1,2,0:T(8,128)(2,1)} %bitcast.231), channel_id=1, source_target_pairs={{0,16},{1,17},{2,18},{3,19},{4,20},{5,21},{6,22},{7,23},{8,24},{9,... | collective-permute-start | bytes 6291464 | tf_op jit(solution)/shard_map/ppermute | solution.py:1033
  222.7 57.5 %collective-permute-start.13 = (bf16[2,2,2,128,1024]{4,3,1,2,0:T(8,128)(2,1)}, bf16[2,2,2,128,1024]{4,3,1,2,0:T(8,128)(2,1)}, u32[]{:S(2)}, u32[]{:S(2)}) collective-permute-start(bf16[2,2,2,128,1024]{4,3,1,2,0:T(8,128)(2,1)} %bitcast.232), channel_id=1, source_target_pairs={{0,8},{1,9},{2,10},{3,11},{4,12},{5,13},{6,14},{7,15},{8,0},{9,1},... | collective-permute-start | bytes 6291464 | tf_op jit(solution)/shard_map/ppermute | solution.py:1033
  269.6 9.2 %collective-permute-start.15 = (bf16[512,768]{1,0:T(8,128)(2,1)S(1)}, bf16[512,768]{1,0:T(8,128)(2,1)S(1)}, u32[]{:S(2)}, u32[]{:S(2)}) collective-permute-start(bf16[512,768]{1,0:T(8,128)(2,1)S(1)} %weight_grad.12), channel_id=1, source_target_pairs={{0,4},{1,5},{2,6},{3,7},{4,0},{5,1},{6,2},{7,3},{8,12},{9,13},{10,... | collective-permute-start | bytes 2359304 | tf_op jit(solution)/shard_map/ppermute | solution.py:1033
  271.2 38.4 %collective-permute-start.17 = (bf16[3,864,256]{2,1,0:T(8,128)(2,1)}, bf16[3,864,256]{2,1,0:T(8,128)(2,1)}, u32[]{:S(2)}, u32[]{:S(2)}) collective-permute-start(bf16[3,864,256]{2,1,0:T(8,128)(2,1)} %dynamic-slice_bitcast_fusion.1), channel_id=1, source_target_pairs={{0,4},{1,5},{2,6},{3,7},{4,0},{5,1},{6,2},{7,3},{8,12},{9,13},{10,... | collective-permute-start | bytes 3981320 | tf_op jit(solution)/shard_map/ppermute | solution.py:1033
  279.7 75.3 %collective-permute-start.22 = (bf16[2,2,2,32,768]{4,3,1,2,0:T(8,128)(2,1)}, bf16[2,2,2,32,768]{4,3,1,2,0:T(8,128)(2,1)}, u32[]{:S(2)}, u32[]{:S(2)}) collective-permute-start(bf16[2,2,2,32,768]{4,3,1,2,0:T(8,128)(2,1)} %copy_bitcast_fusion.10), channel_id=1, source_target_pairs={{0,16},{1,17},{2,18},{3,19},{4,20},{5,21},{6,22},{7,23},{8,24},{9,... | collective-permute-start | bytes 1179656 | tf_op jit(solution)/shard_map/ppermute | solution.py:1033
  286.0 35.6 %collective-permute-start.18 = (bf16[2,2,32,4096]{3,2,0,1:T(8,128)(2,1)S(1)}, bf16[2,2,32,4096]{3,2,0,1:T(8,128)(2,1)}, u32[]{:S(2)}, u32[]{:S(2)}) collective-permute-start(bf16[2,2,32,4096]{3,2,0,1:T(8,128)(2,1)S(1)} %dynamic-slice_bitcast_fusion.3), channel_id=1, source_target_pairs={{0,8},{1,9},{2,10},{3,11},{4,12},{5,13},{6,14},{7,15},{8,0},{9,1},... | collective-permute-start | bytes 3145736 | tf_op jit(solution)/shard_map/ppermute | solution.py:1033
  288.3 30.6 %collective-permute-start.16 = (bf16[2,2,128,1024]{3,2,0,1:T(8,128)(2,1)}, bf16[2,2,128,1024]{3,2,0,1:T(8,128)(2,1)}, u32[]{:S(2)}, u32[]{:S(2)}) collective-permute-start(bf16[2,2,128,1024]{3,2,0,1:T(8,128)(2,1)} %dynamic-slice_bitcast_fusion.4), channel_id=1, source_target_pairs={{0,16},{1,17},{2,18},{3,19},{4,20},{5,21},{6,22},{7,23},{8,24},{9,... | collective-permute-start | bytes 3145736 | tf_op jit(solution)/shard_map/ppermute | solution.py:1033
  289.9 22.0 %copy-start.3 = (bf16[1024,1536]{1,0:T(8,128)(2,1)S(1)}, bf16[1024,1536]{1,0:T(8,128)(2,1)}, u32[]{:S(2)}) copy-start(bf16[1024,1536]{1,0:T(8,128)(2,1)} %copy-done.2) | copy-start | bytes 9437188
  289.9 22.0 %copy-start.5 = (bf16[1024,1536]{1,0:T(8,128)(2,1)S(1)}, bf16[1024,1536]{1,0:T(8,128)(2,1)}, u32[]{:S(2)}) copy-start(bf16[1024,1536]{1,0:T(8,128)(2,1)} %copy-done.4) | copy-start | bytes 9437188
  310.4 43.4 %collective-permute-start.23 = (bf16[2,2,2,32,768]{4,3,1,2,0:T(8,128)(2,1)}, bf16[2,2,2,32,768]{4,3,1,2,0:T(8,128)(2,1)}, u32[]{:S(2)}, u32[]{:S(2)}) collective-permute-start(bf16[2,2,2,32,768]{4,3,1,2,0:T(8,128)(2,1)} %copy_bitcast_fusion.9), channel_id=1, source_target_pairs={{0,8},{1,9},{2,10},{3,11},{4,12},{5,13},{6,14},{7,15},{8,0},{9,1},... | collective-permute-start | bytes 1179656 | tf_op jit(solution)/shard_map/ppermute | solution.py:1033
  324.9 21.8 %copy-start.34 = (bf16[2,2,2,32,1024]{4,3,1,2,0:T(8,128)(2,1)}, bf16[2,2,2,32,1024]{4,3,1,2,0:T(8,128)(2,1)S(1)}, u32[]{:S(2)}) copy-start(bf16[2,2,2,32,1024]{4,3,1,2,0:T(8,128)(2,1)S(1)} %fusion.6) | copy-start | bytes 1572868
  327.5 24.6 %collective-permute-start.24 = (bf16[2,256,1024]{2,1,0:T(8,128)(2,1)}, bf16[2,256,1024]{2,1,0:T(8,128)(2,1)}, u32[]{:S(2)}, u32[]{:S(2)}) collective-permute-start(bf16[2,256,1024]{2,1,0:T(8,128)(2,1)} %dynamic-slice_bitcast_fusion.2), channel_id=1, source_target_pairs={{0,1},{1,0},{2,3},{3,2},{4,5},{5,4},{6,7},{7,6},{8,9},{9,8},{10,11... | collective-permute-start | bytes 3145736 | tf_op jit(solution)/shard_map/ppermute | solution.py:1033
  346.7 9.4 %collective-permute-start.21 = (bf16[2,2,32,1024]{3,2,0,1:T(8,128)(2,1)S(1)}, bf16[2,2,32,1024]{3,2,0,1:T(8,128)(2,1)S(1)}, u32[]{:S(2)}, u32[]{:S(2)}) collective-permute-start(bf16[2,2,32,1024]{3,2,0,1:T(8,128)(2,1)S(1)} %dynamic-slice_bitcast_fusion.18), channel_id=1, source_target_pairs={{0,16},{1,17},{2,18},{3,19},{4,20},{5,21},{6,22},{7,23},{8,24},{9,... | collective-permute-start | bytes 786440 | tf_op jit(solution)/shard_map/ppermute | solution.py:1033
  348.8 21.2 %collective-permute-start.20 = (bf16[3,864,256]{2,1,0:T(8,128)(2,1)S(1)}, bf16[3,864,256]{2,1,0:T(8,128)(2,1)S(1)}, u32[]{:S(2)}, u32[]{:S(2)}) collective-permute-start(bf16[3,864,256]{2,1,0:T(8,128)(2,1)S(1)} %dynamic-slice_bitcast_fusion), channel_id=1, source_target_pairs={{0,4},{1,5},{2,6},{3,7},{4,0},{5,1},{6,2},{7,3},{8,12},{9,13},{10,... | collective-permute-start | bytes 3981320 | tf_op jit(solution)/shard_map/ppermute | solution.py:1033
  360.8 20.0 %collective-permute-start.29 = (bf16[512,768]{1,0:T(8,128)(2,1)S(1)}, bf16[512,768]{1,0:T(8,128)(2,1)}, u32[]{:S(2)}, u32[]{:S(2)}) collective-permute-start(bf16[512,768]{1,0:T(8,128)(2,1)S(1)} %weight_grad.14), channel_id=1, source_target_pairs={{0,4},{1,5},{2,6},{3,7},{4,0},{5,1},{6,2},{7,3},{8,12},{9,13},{10,... | collective-permute-start | bytes 2359304 | tf_op jit(solution)/shard_map/ppermute | solution.py:1033
  360.9 15.1 %collective-permute-start.27 = (bf16[2,2,32,768]{3,2,0,1:T(8,128)(2,1)S(1)}, bf16[2,2,32,768]{3,2,0,1:T(8,128)(2,1)}, u32[]{:S(2)}, u32[]{:S(2)}) collective-permute-start(bf16[2,2,32,768]{3,2,0,1:T(8,128)(2,1)S(1)} %dynamic-slice_bitcast_fusion.21), channel_id=1, source_target_pairs={{0,16},{1,17},{2,18},{3,19},{4,20},{5,21},{6,22},{7,23},{8,24},{9,... | collective-permute-start | bytes 589832 | tf_op jit(solution)/shard_map/ppermute | solution.py:1033
  361.5 15.5 %collective-permute-start.26 = (bf16[2,2,32,768]{3,2,0,1:T(8,128)(2,1)S(1)}, bf16[2,2,32,768]{3,2,0,1:T(8,128)(2,1)}, u32[]{:S(2)}, u32[]{:S(2)}) collective-permute-start(bf16[2,2,32,768]{3,2,0,1:T(8,128)(2,1)S(1)} %dynamic-slice_bitcast_fusion.22), channel_id=1, source_target_pairs={{0,8},{1,9},{2,10},{3,11},{4,12},{5,13},{6,14},{7,15},{8,0},{9,1},... | collective-permute-start | bytes 589832 | tf_op jit(solution)/shard_map/ppermute | solution.py:1033
  363.3 31.6 %collective-permute-start.32 = (bf16[256,1024]{1,0:T(8,128)(2,1)}, bf16[256,1024]{1,0:T(8,128)(2,1)S(1)}, u32[]{:S(2)}, u32[]{:S(2)}) collective-permute-start(bf16[256,1024]{1,0:T(8,128)(2,1)} %dynamic-slice_bitcast_fusion.14), channel_id=1, source_target_pairs={{0,2},{1,3},{2,0},{3,1},{4,6},{5,7},{6,4},{7,5},{8,10},{9,11},{10,... | collective-permute-start | bytes 1572872 | tf_op jit(solution)/shard_map/ppermute | solution.py:1033
  377.0 10.7 %collective-permute-start.25 = (bf16[2,2,2,32,768]{4,3,1,2,0:T(8,128)(2,1)S(1)}, bf16[2,2,2,32,768]{4,3,1,2,0:T(8,128)(2,1)S(1)}, u32[]{:S(2)}, u32[]{:S(2)}) collective-permute-start(bf16[2,2,2,32,768]{4,3,1,2,0:T(8,128)(2,1)S(1)} %copy_bitcast_fusion.8), channel_id=1, source_target_pairs={{0,8},{1,9},{2,10},{3,11},{4,12},{5,13},{6,14},{7,15},{8,0},{9,1},... | collective-permute-start | bytes 1179656 | tf_op jit(solution)/shard_map/ppermute | solution.py:1033
  378.9 30.6 %collective-permute-start.36 = (bf16[432,1024]{1,0:T(8,128)(2,1)S(1)}, bf16[432,1024]{1,0:T(8,128)(2,1)}, u32[]{:S(2)}, u32[]{:S(2)}) collective-permute-start(bf16[432,1024]{1,0:T(8,128)(2,1)S(1)} %get-tuple-element.275), channel_id=1, source_target_pairs={{2,4},{3,5},{4,2},{5,3},{10,12},{11,13},{12,10},{13,11},{18,20},{1... | collective-permute-start | bytes 2654216 | tf_op jit(solution)/shard_map/ppermute | solution.py:1033
  380.5 37.6 %collective-permute-start.37 = (bf16[432,1024]{1,0:T(8,128)(2,1)}, bf16[432,1024]{1,0:T(8,128)(2,1)}, u32[]{:S(2)}, u32[]{:S(2)}) collective-permute-start(bf16[432,1024]{1,0:T(8,128)(2,1)} %get-tuple-element.274), channel_id=1, source_target_pairs={{0,1},{1,0},{2,5},{3,4},{4,3},{5,2},{6,7},{7,6},{8,9},{9,8},{10,13... | collective-permute-start | bytes 2654216 | tf_op jit(solution)/shard_map/ppermute | solution.py:1033
  382.0 13.7 %copy-start.47 = (f32[8,1024]{1,0:T(8,128)S(1)}, f32[8,1024]{1,0:T(8,128)}, u32[]{:S(2)}) copy-start(f32[8,1024]{1,0:T(8,128)} %get-tuple-element.267) | copy-start | bytes 98308
  382.0 14.4 %copy-start.48 = (f32[1,4096]{1,0:T(1,128)S(1)}, f32[1,4096]{1,0:T(1,128)}, u32[]{:S(2)}) copy-start(f32[1,4096]{1,0:T(1,128)} %get-tuple-element.272) | copy-start | bytes 49156
  382.0 11.2 %collective-permute-start.30 = (bf16[2,2,2,32,768]{4,3,1,2,0:T(8,128)(2,1)S(1)}, bf16[2,2,2,32,768]{4,3,1,2,0:T(8,128)(2,1)S(1)}, u32[]{:S(2)}, u32[]{:S(2)}) collective-permute-start(bf16[2,2,2,32,768]{4,3,1,2,0:T(8,128)(2,1)S(1)} %bitcast.258), channel_id=1, source_target_pairs={{0,16},{1,17},{2,18},{3,19},{4,20},{5,21},{6,22},{7,23},{8,24},{9,... | collective-permute-start | bytes 1179656 | tf_op jit(solution)/shard_map/ppermute | solution.py:1033
  383.6 10.5 %copy-start.41 = (bf16[2,2,32,4096]{3,2,0,1:T(8,128)(2,1)}, bf16[2,2,32,4096]{3,2,0,1:T(8,128)(2,1)S(1)}, u32[]{:S(2)}) copy-start(bf16[2,2,32,4096]{3,2,0,1:T(8,128)(2,1)S(1)} %constant_dynamic-update-slice_fusion.16) | copy-start | bytes 3145732
  388.7 20.9 %collective-permute-start.28 = (bf16[2,2,32,768]{3,2,0,1:T(8,128)(2,1)S(1)}, bf16[2,2,32,768]{3,2,0,1:T(8,128)(2,1)}, u32[]{:S(2)}, u32[]{:S(2)}) collective-permute-start(bf16[2,2,32,768]{3,2,0,1:T(8,128)(2,1)S(1)} %dynamic-slice_bitcast_fusion.20), channel_id=1, source_target_pairs={{0,16},{1,17},{2,18},{3,19},{4,20},{5,21},{6,22},{7,23},{8,24},{9,... | collective-permute-start | bytes 589832 | tf_op jit(solution)/shard_map/ppermute | solution.py:1033
  397.8 2.5 collective-permute-start.33
  400.3 17.9 %copy-start.39 = (bf16[2,2,2,32,768]{4,3,1,2,0:T(8,128)(2,1)S(1)}, bf16[2,2,2,32,768]{4,3,1,2,0:T(8,128)(2,1)}, u32[]{:S(2)}) copy-start(bf16[2,2,2,32,768]{4,3,1,2,0:T(8,128)(2,1)} %copy-done.38) | copy-start | bytes 1179652
  400.3 18.8 %copy-start.40 = (bf16[2,2,2,32,768]{4,3,1,2,0:T(8,128)(2,1)S(1)}, bf16[2,2,2,32,768]{4,3,1,2,0:T(8,128)(2,1)}, u32[]{:S(2)}) copy-start(bf16[2,2,2,32,768]{4,3,1,2,0:T(8,128)(2,1)} %fusion.7) | copy-start | bytes 1179652
  401.9 16.3 %copy-start.42 = (bf16[2,2,32,4096]{3,2,0,1:T(8,128)(2,1)S(1)}, bf16[2,2,32,4096]{3,2,0,1:T(8,128)(2,1)}, u32[]{:S(2)}) copy-start(bf16[2,2,32,4096]{3,2,0,1:T(8,128)(2,1)} %copy-done.41) | copy-start | bytes 3145732
  402.0 17.3 %copy-start.43 = (bf16[2,2,32,1024]{3,2,0,1:T(8,128)(2,1)S(1)}, bf16[2,2,32,1024]{3,2,0,1:T(8,128)(2,1)}, u32[]{:S(2)}) copy-start(bf16[2,2,32,1024]{3,2,0,1:T(8,128)(2,1)} %fusion.11) | copy-start | bytes 786436
  402.0 4.2 collective-permute-start.34
  404.2 13.9 %collective-permute-start.31 = (bf16[2,2,32,768]{3,2,0,1:T(8,128)(2,1)S(1)}, bf16[2,2,32,768]{3,2,0,1:T(8,128)(2,1)S(1)}, u32[]{:S(2)}, u32[]{:S(2)}) collective-permute-start(bf16[2,2,32,768]{3,2,0,1:T(8,128)(2,1)S(1)} %dynamic-slice_bitcast_fusion.19), channel_id=1, source_target_pairs={{0,8},{1,9},{2,10},{3,11},{4,12},{5,13},{6,14},{7,15},{8,0},{9,1},... | collective-permute-start | bytes 589832 | tf_op jit(solution)/shard_map/ppermute | solution.py:1033
  406.3 11.8 %collective-permute-start.35 = (f32[2,2,32,14]{2,1,3,0:T(2,128)S(1)}, f32[2,2,32,14]{2,1,3,0:T(2,128)S(1)}, u32[]{:S(2)}, u32[]{:S(2)}) collective-permute-start(f32[2,2,32,14]{2,1,3,0:T(2,128)S(1)} %dynamic-slice_bitcast_fusion.23), channel_id=1, source_target_pairs={{0,16},{1,17},{2,18},{3,19},{4,20},{5,21},{6,22},{7,23},{8,24},{9,... | collective-permute-start | bytes 21512 | tf_op jit(solution)/shard_map/ppermute | solution.py:1033
  419.3 9.4 %collective-permute-start.38 = (bf16[2,32,4096]{2,1,0:T(8,128)(2,1)S(1)}, bf16[2,32,4096]{2,1,0:T(8,128)(2,1)S(1)}, u32[]{:S(2)}, u32[]{:S(2)}) collective-permute-start(bf16[2,32,4096]{2,1,0:T(8,128)(2,1)S(1)} %dynamic-slice_bitcast_fusion.13), channel_id=1, source_target_pairs={{0,1},{1,0},{2,3},{3,2},{4,5},{5,4},{6,7},{7,6},{8,9},{9,8},{10,11... | collective-permute-start | bytes 1572872 | tf_op jit(solution)/shard_map/ppermute | solution.py:1033
  419.5 9.3 %collective-permute-start.39 = (f32[2,32,14]{1,0,2:T(2,128)S(1)}, f32[2,32,14]{1,0,2:T(2,128)S(1)}, u32[]{:S(2)}, u32[]{:S(2)}) collective-permute-start(f32[2,32,14]{1,0,2:T(2,128)S(1)} %bitcast.271), channel_id=1, source_target_pairs={{0,1},{1,0},{2,3},{3,2},{4,5},{5,4},{6,7},{7,6},{8,9},{9,8},{10,11... | collective-permute-start | bytes 10760 | tf_op jit(solution)/shard_map/ppermute | solution.py:1033
  428.8 15.2 %collective-permute-start.41 = (f32[32,14]{0,1:T(8,128)S(1)}, f32[32,14]{0,1:T(8,128)S(1)}, u32[]{:S(2)}, u32[]{:S(2)}) collective-permute-start(f32[32,14]{0,1:T(8,128)S(1)} %bitcast.274), channel_id=1, source_target_pairs={{0,2},{1,3},{2,0},{3,1},{4,6},{5,7},{6,4},{7,5},{8,10},{9,11},{10,... | collective-permute-start | bytes 5384 | tf_op jit(solution)/shard_map/ppermute | solution.py:1033
  440.1 11.0 %collective-permute-start.40 = (bf16[32,4096]{1,0:T(8,128)(2,1)S(1)}, bf16[32,4096]{1,0:T(8,128)(2,1)S(1)}, u32[]{:S(2)}, u32[]{:S(2)}) collective-permute-start(bf16[32,4096]{1,0:T(8,128)(2,1)S(1)} %dynamic-slice_bitcast_fusion.17), channel_id=1, source_target_pairs={{0,2},{1,3},{2,0},{3,1},{4,6},{5,7},{6,4},{7,5},{8,10},{9,11},{10,... | collective-permute-start | bytes 786440 | tf_op jit(solution)/shard_map/ppermute | solution.py:1033
  (43 other events, 175.3 us)

commit v2 on v0

--- a/solution.py
+++ b/solution.py
@@ -1276,32 +1276,34 @@
             item.terms, other = tie(item.terms, other)
         return other
 
-    grads, b_sum0 = back(0, quads // 2)
-    got = away_rows(grads)
-    output_got, grads = tie(output_got, grads)
-    grads = settle([down, up, out], grads)
+    grads0, b_sum0 = back(0, quads // 2)
+    got0 = away_rows(grads0)
+    output_got, grads0 = tie(output_got, grads0)
+    grads0 = settle([down, up, out], grads0)
+    grad_context, grads0 = tie(grad_context, grads0)
     down.send("y")
     up.send("x")
     out.send("y")
-    cross0, keep0 = products(grads)
-    got, cross0.terms, keep0.terms = tie(got, cross0.terms, keep0.terms)
-    (grad_start,) = add_start(core, grad_one, grads, got, w_own, w_oth, 0, False)
-    keep0.send("x")
-    cross0.send("y")
-    grad_context, grad_start = tie(grad_context, grad_start)
     grads, b_sum1 = back(quads // 2, quads // 4)
-    grads = settle([down, up, out, keep0, cross0], grads)
+    grads, grads0, got0 = tie(grads, grads0, got0)
+    grads0 = settle([down, up, out], grads0)
     wide_rows = up.terms.shape[-2]
     slabs = [up.terms[..., i * model : (i + 1) * model] for i in range(up.terms.shape[-1] // model)]
     ffn = jnp.concatenate([down.terms, *slabs, out.terms], axis=2)
-    ffn, grads = tie(ffn, grads)
+    ffn, grads0 = tie(ffn, grads0)
     ffn = Sum(plan, ffn, where, "hl").send("l")
+    cross0, keep0 = products(grads0)
+    got0, cross0.terms, keep0.terms = tie(got0, cross0.terms, keep0.terms)
+    keep0.send("x")
+    cross0.send("y")
+    (grad_start,) = add_start(core, grad_one, grads0, got0, w_own, w_oth, 0, False)
+    grads, grad_start = tie(grads, grad_start)
+    grads, b_sum2 = back(quads // 2 + quads // 4, quads // 4, grads)
+    got = away_rows(grads)
+    grads = settle([ffn, keep0, cross0], grads)
+    ffn.send("h")
     keep0.send("y")
     cross0.send("x")
-    grads, b_sum2 = back(quads // 2 + quads // 4, quads // 4, grads)
-    got = away_rows(grads)
-    grads = settle([ffn], grads)
-    ffn.send("h")
     cross1, keep1 = products(grads)
     got, keep1.terms = tie(got, keep1.terms)
     keep1.send("x")

time: 466 us -> 463 us (level)
    unnamed x130 -> x150, local copies, waits for them, and re-layouts: 19.8 us -> 20 us
  transfers between devices with their start and end apart: 42 -> 42, of which waited for: 12 -> 13; matrix products, arithmetic and copies ran while one was open for 13% -> 13% of each run, Pallas kernels for 39% -> 39%
where the time goes in v2:
time: 463 us; the launch traced here: 454 us
  Pallas kernels  242 us (52%)
  starting transfers between devices  59.5 us (13%)
  waiting for transfers between devices  58.3 us (13%)
  local copies, waits for them, and re-layouts  54.6 us (12%)
  other arithmetic  31.9 us (7%)
  between operations  6.95 us (2%)
    pallas_call x3, Pallas kernels, attn_bwd(): pl.pallas_call(functools.partial(bwd_kernel, bk, into is not None), input...  74.1 us
    ppermute x42, starting transfers between devices, send(): return lax.ppermute(value, AXES, self.perm(target))  59.5 us
    ppermute x42, waiting for transfers between devices, send(): return lax.ppermute(value, AXES, self.perm(target))  58.3 us
    pallas_call x1, Pallas kernels, middle(): pl.pallas_call(functools.partial(middle_kernel, fc), out_shape=(out(model...  54.9 us
    pallas_call x8, Pallas kernels, weight_grad(): pl.pallas_call(functools.partial(grad_kernel, count, extra), out_shape=ja...  46.6 us
    pallas_call x2, Pallas kernels, attn_fwd(): pl.pallas_call(functools.partial(fwd_kernel, bq), out_shape=(jax.ShapeDty...  35.8 us
    unnamed x150, local copies, waits for them, and re-layouts  20 us
    convert_element_type x16, other arithmetic, add(): self.terms = total.astype(self.terms.dtype) if self.axes else total  18.2 us
  transfers between devices with their start and end apart: 42, of which 13 were waited for; matrix products, arithmetic and copies ran while one was open for 13% of the time, Pallas kernels for 39%

profile of v2, /device:TPU:0, one launch (start us, length us, event | category | flops | bytes accessed | tf_op | source)
XLA Modules:
  0.0 453.7 jit_solution(16658593825228654775)
XLA Ops:
  3.4 2.8 dynamic-slice_bitcast_fusion.12
  6.3 1.7 collective-permute-start.1
  8.0 3.0 collective-permute-start.2
  12.1 2.6 collective-permute-start
  16.4 2.8 copy-done.9
  19.2 3.7 split_columns.1
  22.9 1.7 copy-done.4
  28.2 3.2 collective-permute-done.2
  31.4 1.6 broadcast_select_fusion.3
  34.4 11.1 %collective-permute-start.3 = (bf16[864,1024]{1,0:T(8,128)(2,1)}, bf16[864,1024]{1,0:T(8,128)(2,1)}, u32[]{:S(2)}, u32[]{:S(2)}) collective-permute-start(bf16[864,1024]{1,0:T(8,128)(2,1)} %pad_maximum_fusion.own_ref.inp_ref), channel_id=1, source_target_pairs={{0,4},{1,5},{2,6},{3,7},{4,0},{5,1},{6,2},{7,3},{8,12},{9,13},{10,... | collective-permute-start | bytes 5308424 | tf_op jit(solution)/shard_map/ppermute | solution.py:1033
  46.7 2.4 collective-permute-done.3.oth_ref
  49.8 10.2 %collective-permute-start.7 = (bf16[432,1024]{1,0:T(8,128)(2,1)}, bf16[432,1024]{1,0:T(8,128)(2,1)S(1)}, u32[]{:S(2)}, u32[]{:S(2)}) collective-permute-start(bf16[432,1024]{1,0:T(8,128)(2,1)} %get-tuple-element.171), channel_id=1, source_target_pairs={{0,1},{1,0},{2,5},{3,4},{4,3},{5,2},{6,7},{7,6},{8,9},{9,8},{10,13... | collective-permute-start | bytes 2654216 | tf_op jit(solution)/shard_map/ppermute | solution.py:1033
  60.1 9.2 %project.1 = (bf16[1728,1536]{1,0:T(8,128)(2,1)}, bf16[1728,1024]{1,0:T(8,128)(2,1)S(1)}) custom-call(s32[1]{0:T(128)} %bitcast.1.sel_ref.refs_0_, f32[1]{0:T(128)} %bitcast.3.frac_ref, bf16[864,1024]{1,0:T(8,128)(2,1)} %pad_maximum_fusion.own_ref.inp_ref, bf16[864,1024]{1,0:T(8,128)(2,1)} %collective-permute-done.3.oth_ref, f32[8,1024]{1,0:T(8,128)S(1)} %stack.89.vec_ref, ...), custom_call_target="tpu_custom_call" | custom-call | flops 5435817984 | bytes 15532032 | tf_op jit(solution)/shard_map/project/pallas_call | solution.py:864
  69.3 1.7 copy-done
  71.1 17.7 %attn_forward.3 = (bf16[1728,256]{1,0:T(8,128)(2,1)S(1)}, bf16[1728,256]{1,0:T(8,128)(2,1)S(1)}, bf16[4,1728,128]{2,1,0:T(8,128)(2,1)S(1)}) custom-call(s32[27]{0:T(128)S(1)} %pad_add_fusion.1.info, bf16[1728,1536]{1,0:T(8,128)(2,1)} %get-tuple-element.167.q_ref.k_ref.v_ref, bf16[1728,1536]{1,0:T(8,128)(2,1)} %get-tuple-element.167.q_ref.k_ref.v_ref, ...), custom_call_target="tpu_custom_call" | custom-call | flops 12230590464 | bytes 4423680 | tf_op jit(solution)/shard_map/attn_forward/pallas_call | solution.py:117
  90.9 3.7 collective-permute-start.5
  94.6 18.1 %attn_forward.2 = (bf16[1728,256]{1,0:T(8,128)(2,1)S(1)}, bf16[1728,256]{1,0:T(8,128)(2,1)S(1)}, bf16[4,1728,128]{2,1,0:T(8,128)(2,1)S(1)}) custom-call(s32[27]{0:T(128)S(1)} %pad_add_fusion.1.info, bf16[1728,1536]{1,0:T(8,128)(2,1)} %get-tuple-element.167.q_ref.k_ref.v_ref, bf16[1728,1536]{1,0:T(8,128)(2,1)} %get-tuple-element.167.q_ref.k_ref.v_ref, ...), custom_call_target="tpu_custom_call" | custom-call | flops 12230590464 | bytes 4423680 | tf_op jit(solution)/shard_map/attn_forward/pallas_call | solution.py:117
  116.9 54.9 %middle.1 = (bf16[864,1024]{1,0:T(8,128)(2,1)}, bf16[864,1024]{1,0:T(8,128)(2,1)}, bf16[864,4096]{1,0:T(8,128)(2,1)}, bf16[864,1024]{1,0:T(8,128)(2,1)}, bf16[86...) custom-call(s32[1]{0:T(128)} %bitcast.1.sel_ref.refs_0_, ...), custom_call_target="tpu_custom_call" | custom-call | flops 30802968576 | bytes 45088768 | tf_op jit(solution)/shard_map/middle/pallas_call | solution.py:698
  173.3 7.8 %weight_grad.8 = bf16[2048,1024]{1,0:T(8,128)(2,1)} custom-call(s32[1]{0:T(128)S(6)} %sub.27.refs_0_, bf16[864,4096]{1,0:T(8,128)(2,1)} %get-tuple-element.181.refs_1_, bf16[864,1024]{1,0:T(8,128)(2,1)S(1)} %copy-done.17), custom_call_target="tpu_custom_call" | custom-call | flops 3623878656 | bytes 9502720 | tf_op jit(solution)/shard_map/weight_grad/pallas_call | solution.py:799
  181.1 8.5 %weight_grad.9 = bf16[512,4096]{1,0:T(8,128)(2,1)} custom-call(s32[1]{0:T(128)S(6)} %sub.27.refs_0_, bf16[864,1024]{1,0:T(8,128)(2,1)S(1)} %copy-done.1, bf16[864,1024]{1,0:T(8,128)(2,1)S(1)} %copy-done.1, bf16[864,1024]{1,0:T(8,128)(2,1)S(1)} %copy-done.1, bf16[864,1024]{1,0:T(8,128)(2,1)S(1)} %copy-done.1, bf16[864,4096]{1,0:T(8,128)(2,1)} %get-tuple-element.180.refs_5_), custom_call_target="tpu_custom_call" | custom-call | flops 3623878656 | bytes 12156928 | tf_op jit(solution)/shard_map/weight_grad/pallas_call | solution.py:799
  190.1 2.9 dynamic-slice_bitcast_fusion.7
  193.0 1.6 collective-permute-start.8
  194.6 7.0 %weight_grad.10 = bf16[2048,1024]{1,0:T(8,128)(2,1)S(1)} custom-call(s32[1]{0:T(128)} %bitcast.1.sel_ref.refs_0_, bf16[864,4096]{1,0:T(8,128)(2,1)} %get-tuple-element.181.refs_1_, bf16[864,1024]{1,0:T(8,128)(2,1)S(1)} %copy-done.18, bf16[2048,1024]{1,0:T(8,128)(2,1)} %collective-permute-done.11.refs_3_), custom_call_target="tpu_custom_call" | custom-call | flops 3623878656 | bytes 13697024 | tf_op jit(solution)/shard_map/weight_grad/pallas_call | solution.py:799
  201.6 1.9 constant_dynamic-slice_fusion.7
  203.5 1.5 copy.237
  205.0 1.5 collective-permute-start.15
  206.5 7.8 %weight_grad.11 = bf16[512,4096]{1,0:T(8,128)(2,1)S(1)} custom-call(s32[1]{0:T(128)} %bitcast.1.sel_ref.refs_0_, bf16[864,1024]{1,0:T(8,128)(2,1)S(1)} %copy-done.1, bf16[864,1024]{1,0:T(8,128)(2,1)S(1)} %copy-done.1, bf16[864,1024]{1,0:T(8,128)(2,1)S(1)} %copy-done.1, bf16[864,1024]{1,0:T(8,128)(2,1)S(1)} %copy-done.1, ...), custom_call_target="tpu_custom_call" | custom-call | flops 3623878656 | bytes 16351232 | tf_op jit(solution)/shard_map/weight_grad/pallas_call | solution.py:799
  214.3 3.8 out_grad.1
  218.2 1.9 constant_dynamic-slice_fusion.9
  220.0 1.6 copy.238
  221.7 1.5 collective-permute-start.14
  223.2 4.4 context_grad.1.g_ref
  228.8 35.0 %attn_backward.3 = (bf16[3,1728,256]{2,1,0:T(8,128)(2,1)}, f32[2,256]{1,0:T(2,128)}) custom-call(s32[27]{0:T(128)} %copy-done.23, bf16[4,1728,128]{2,1,0:T(8,128)(2,1)} %copy-done.25, bf16[1728,1536]{1,0:T(8,128)(2,1)} %get-tuple-element.167.q_ref.k_ref.v_ref, bf16[1728,1536]{1,0:T(8,128)(2,1)} %get-tuple-element.167.q_ref.k_ref.v_ref, ...), custom_call_target="tpu_custom_call" | custom-call | flops 30576476160 | bytes 7077888 | tf_op jit(solution)/shard_map/attn_backward/pallas_call | solution.py:216
  267.1 2.7 fusion
  270.1 2.4 fusion.1
  272.5 5.8 %collective-permute-done.13 = bf16[2,2,2,32,1024]{4,3,1,2,0:T(8,128)(2,1)S(1)} collective-permute-done((bf16[2,2,2,32,1024]{4,3,1,2,0:T(8,128)(2,1)S(1)}, bf16[2,2,2,32,1024]{4,3,1,2,0:T(8,128)(2,1)S(1)}, u32[]{:S(2)}, u32[]{:S(2)}) %collective-permute-start.13) | collective-permute-done | bytes 524320 | tf_op jit(solution)/shard_map/ppermute | solution.py:1033
  284.8 19.4 %attn_backward.4 = (bf16[3,1728,256]{2,1,0:T(8,128)(2,1)}, f32[2,128]{1,0:T(2,128)}) custom-call(s32[27]{0:T(128)} %copy-done.23, bf16[4,1728,128]{2,1,0:T(8,128)(2,1)} %copy-done.24, bf16[1728,1536]{1,0:T(8,128)(2,1)} %get-tuple-element.167.q_ref.k_ref.v_ref, bf16[1728,1536]{1,0:T(8,128)(2,1)} %get-tuple-element.167.q_ref.k_ref.v_ref, ...), custom_call_target="tpu_custom_call" | custom-call | flops 15288238080 | bytes 3538944 | tf_op jit(solution)/shard_map/attn_backward/pallas_call | solution.py:216
  304.3 6.2 %collective-permute-done.17 = bf16[2,2,128,1024]{3,2,0,1:T(8,128)(2,1)} collective-permute-done((bf16[2,2,128,1024]{3,2,0,1:T(8,128)(2,1)}, bf16[2,2,128,1024]{3,2,0,1:T(8,128)(2,1)}, u32[]{:S(2)}, u32[]{:S(2)}) %collective-permute-start.17) | collective-permute-done | bytes 1048608 | tf_op jit(solution)/shard_map/ppermute | solution.py:1033
  310.5 1.6 fusion.4
  312.1 1.5 fusion.3
  314.9 4.5 weight_grad.12
  319.5 1.6 select_bitcast_fusion.3
  323.5 3.8 weight_grad.13
  328.2 4.9 %add_start.2.base_ref = f32[864,1024]{1,0:T(8,128)S(1)} custom-call(s32[1]{0:T(128)} %bitcast.1.sel_ref.refs_0_, f32[864,1024]{1,0:T(8,128)} %get-tuple-element.212.base_ref, bf16[3,1728,256]{2,1,0:T(8,128)(2,1)S(1)} %copy-done.7, bf16[3,864,256]{2,1,0:T(8,128)(2,1)S(1)} %copy-done.21, bf16[1024,1536]{1,0:T(8,128)(2,1)S(1)} %copy-done.3, ...), custom_call_target="tpu_custom_call" | custom-call | flops 2717908992 | bytes 12877824 | tf_op jit(solution)/shard_map/add_start/pallas_call | solution.py:983
  333.2 1.8 copy-done.10
  338.5 19.7 %attn_backward.5 = (bf16[3,1728,256]{2,1,0:T(8,128)(2,1)}, f32[2,128]{1,0:T(2,128)}) custom-call(s32[27]{0:T(128)} %copy-done.23, bf16[4,1728,128]{2,1,0:T(8,128)(2,1)} %copy-done.24, bf16[1728,1536]{1,0:T(8,128)(2,1)} %get-tuple-element.167.q_ref.k_ref.v_ref, ...), custom_call_target="tpu_custom_call", output_to_operand_aliasing={{0}: (7, {})} | custom-call | flops 15288238080 | bytes 3538944 | tf_op jit(solution)/shard_map/attn_backward/pallas_call | solution.py:216
  358.2 2.6 dynamic-slice_bitcast_fusion
  360.9 1.9 fusion.2
  365.0 3.7 weight_grad.14
  372.3 3.6 weight_grad.15
  377.4 5.0 %add_start.3 = (bf16[864,1024]{1,0:T(8,128)(2,1)S(1)}, f32[1,1024]{1,0:T(1,128)S(1)}) custom-call(s32[1]{0:T(128)} %bitcast.1.sel_ref.refs_0_, f32[864,1024]{1,0:T(8,128)} %copy-done.10, bf16[3,1728,256]{2,1,0:T(8,128)(2,1)S(1)} %copy-done.8, bf16[3,864,256]{2,1,0:T(8,128)(2,1)S(1)} %collective-permute-done.21.got_ref, bf16[1024,1536]{1,0:T(8,128)(2,1)S(1)} %copy-done.3, ...), custom_call_target="tpu_custom_call" | custom-call | flops 2717908992 | bytes 12877824 | tf_op jit(solution)/shard_map/add_start/pallas_call | solution.py:983
  384.1 1.6 fusion.15
  385.8 1.6 fusion.16
  387.4 1.6 collective-permute-start.36
  389.0 4.8 %collective-permute-done.25 = bf16[2,2,2,32,768]{4,3,2,1,0:T(8,128)(2,1)S(1)} collective-permute-done((bf16[2,2,2,32,768]{4,3,2,1,0:T(8,128)(2,1)S(1)}, bf16[2,2,2,32,768]{4,3,2,1,0:T(8,128)(2,1)S(1)}, u32[]{:S(2)}, u32[]{:S(2)}) %collective-permute-start.25) | collective-permute-done | bytes 393248 | tf_op jit(solution)/shard_map/ppermute | solution.py:1033
  394.0 7.8 %collective-permute-done.32 = bf16[288,1024]{1,0:T(8,128)(2,1)S(1)} collective-permute-done((bf16[288,1024]{1,0:T(8,128)(2,1)S(1)}, bf16[288,1024]{1,0:T(8,128)(2,1)S(1)}, u32[]{:S(2)}, u32[]{:S(2)}) %collective-permute-start.32) | collective-permute-done | bytes 589856 | tf_op jit(solution)/shard_map/ppermute | solution.py:1033
  407.2 1.5 collective-permute-start.31
  410.5 5.6 %collective-permute-done.34 = f32[2,2,2,32,14]{3,2,4,1,0:T(2,128)S(1)} collective-permute-done((f32[2,2,2,32,14]{3,2,4,1,0:T(2,128)S(1)}, f32[2,2,2,32,14]{3,2,4,1,0:T(2,128)S(1)}, u32[]{:S(2)}, u32[]{:S(2)}) %collective-permute-start.34) | collective-permute-done | bytes 14368 | tf_op jit(solution)/shard_map/ppermute | solution.py:1033
  420.0 5.6 %collective-permute-done.37 = bf16[432,1024]{1,0:T(8,128)(2,1)} collective-permute-done((bf16[432,1024]{1,0:T(8,128)(2,1)}, bf16[432,1024]{1,0:T(8,128)(2,1)}, u32[]{:S(2)}, u32[]{:S(2)}) %collective-permute-start.37) | collective-permute-done | bytes 884768 | tf_op jit(solution)/shard_map/ppermute | solution.py:1033
  427.0 2.1 collective-permute-start.38
  431.8 6.5 %collective-permute-done.38 = bf16[2,32,3072]{2,1,0:T(8,128)(2,1)S(1)} collective-permute-done((bf16[2,32,3072]{2,1,0:T(8,128)(2,1)S(1)}, bf16[2,32,3072]{2,1,0:T(8,128)(2,1)S(1)}, u32[]{:S(2)}, u32[]{:S(2)}) %collective-permute-start.38) | collective-permute-done | bytes 393248 | tf_op jit(solution)/shard_map/ppermute | solution.py:1033
  438.6 3.0 collective-permute-start.40
  441.5 1.5 collective-permute-done.41
  444.3 7.1 %collective-permute-done.40 = bf16[32,3072]{1,0:T(8,128)(2,1)S(1)} collective-permute-done((bf16[32,3072]{1,0:T(8,128)(2,1)S(1)}, bf16[32,3072]{1,0:T(8,128)(2,1)S(1)}, u32[]{:S(2)}, u32[]{:S(2)}) %collective-permute-start.40) | collective-permute-done | bytes 196640 | tf_op jit(solution)/shard_map/ppermute | solution.py:1033
  (317 shorter events, 62.9 us)
Async XLA Ops:
  0.7 11.2 %copy-start.63 = (s32[2]{0:T(128)S(1)}, s32[2]{0:T(128)}, u32[]{:S(2)}) copy-start(s32[2]{0:T(128)} %param.20) | copy-start | bytes 28
  0.7 14.0 %copy-start.35 = (bf16[2,432,1024]{2,1,0:T(8,128)(2,1)S(1)}, bf16[2,432,1024]{2,1,0:T(8,128)(2,1)}, u32[]{:S(2)}) copy-start(bf16[2,432,1024]{2,1,0:T(8,128)(2,1)} %param.22) | copy-start | bytes 5308420
  6.2 9.9 %copy-start.49 = (bf16[1024]{0:T(1024)(128)(2,1)S(1)}, bf16[1024]{0:T(1024)(128)(2,1)}, u32[]{:S(2)}) copy-start(bf16[1024]{0:T(1024)(128)(2,1)} %param.25) | copy-start | bytes 6148
  6.2 9.9 %copy-start.50 = (bf16[1024]{0:T(1024)(128)(2,1)S(1)}, bf16[1024]{0:T(1024)(128)(2,1)}, u32[]{:S(2)}) copy-start(bf16[1024]{0:T(1024)(128)(2,1)} %param.36) | copy-start | bytes 6148
  6.2 9.9 %copy-start.51 = (bf16[1024]{0:T(1024)(128)(2,1)S(1)}, bf16[1024]{0:T(1024)(128)(2,1)}, u32[]{:S(2)}) copy-start(bf16[1024]{0:T(1024)(128)(2,1)} %param.37) | copy-start | bytes 6148
  6.2 10.0 %copy-start.52 = (bf16[1024]{0:T(1024)(128)(2,1)S(1)}, bf16[1024]{0:T(1024)(128)(2,1)}, u32[]{:S(2)}) copy-start(bf16[1024]{0:T(1024)(128)(2,1)} %param.27) | copy-start | bytes 6148
  6.2 10.0 %copy-start.53 = (bf16[1024]{0:T(1024)(128)(2,1)S(1)}, bf16[1024]{0:T(1024)(128)(2,1)}, u32[]{:S(2)}) copy-start(bf16[1024]{0:T(1024)(128)(2,1)} %param.28) | copy-start | bytes 6148
  6.2 10.0 %copy-start.54 = (bf16[1024]{0:T(1024)(128)(2,1)S(1)}, bf16[1024]{0:T(1024)(128)(2,1)}, u32[]{:S(2)}) copy-start(bf16[1024]{0:T(1024)(128)(2,1)} %param.29) | copy-start | bytes 6148
  6.2 10.0 %copy-start.55 = (bf16[1024]{0:T(1024)(128)(2,1)S(1)}, bf16[1024]{0:T(1024)(128)(2,1)}, u32[]{:S(2)}) copy-start(bf16[1024]{0:T(1024)(128)(2,1)} %param.33) | copy-start | bytes 6148
  6.2 10.0 %copy-start.56 = (bf16[1024]{0:T(1024)(128)(2,1)S(1)}, bf16[1024]{0:T(1024)(128)(2,1)}, u32[]{:S(2)}) copy-start(bf16[1024]{0:T(1024)(128)(2,1)} %param.34) | copy-start | bytes 6148
  6.3 10.0 %copy-start.57 = (bf16[1024]{0:T(1024)(128)(2,1)S(1)}, bf16[1024]{0:T(1024)(128)(2,1)}, u32[]{:S(2)}) copy-start(bf16[1024]{0:T(1024)(128)(2,1)} %param.35) | copy-start | bytes 6148
  6.3 21.9 %collective-permute-start.1 = (bf16[432,1024]{1,0:T(8,128)(2,1)}, bf16[432,1024]{1,0:T(8,128)(2,1)}, u32[]{:S(2)}, u32[]{:S(2)}) collective-permute-start(bf16[432,1024]{1,0:T(8,128)(2,1)} %get-tuple-element.317), channel_id=1, source_target_pairs={{2,4},{3,5},{4,2},{5,3},{10,12},{11,13},{12,10},{13,11},{18,20},{1... | collective-permute-start | bytes 2654216 | tf_op jit(solution)/shard_map/ppermute | solution.py:1033
  8.0 23.4 %collective-permute-start.2 = (bf16[432,1024]{1,0:T(8,128)(2,1)}, bf16[432,1024]{1,0:T(8,128)(2,1)}, u32[]{:S(2)}, u32[]{:S(2)}) collective-permute-start(bf16[432,1024]{1,0:T(8,128)(2,1)} %get-tuple-element.318), channel_id=1, source_target_pairs={{0,1},{1,0},{2,5},{3,4},{4,3},{5,2},{6,7},{7,6},{8,9},{9,8},{10,13... | collective-permute-start | bytes 2654216 | tf_op jit(solution)/shard_map/ppermute | solution.py:1033
  12.1 12.4 %collective-permute-start = (s32[2,16]{1,0:T(2,128)S(1)}, s32[2,16]{1,0:T(2,128)S(1)}, u32[]{:S(2)}, u32[]{:S(2)}) collective-permute-start(s32[2,16]{1,0:T(2,128)S(1)} %pad_add_fusion), channel_id=1, source_target_pairs={{0,4},{1,5},{2,6},{3,7},{4,0},{5,1},{6,2},{7,3},{8,12},{9,13},{10,... | collective-permute-start | bytes 392 | tf_op jit(solution)/shard_map/ppermute | solution.py:1033
  16.4 43.7 %copy-start.22 = (f32[8,1024]{1,0:T(8,128)}, f32[8,1024]{1,0:T(8,128)S(1)}, u32[]{:S(2)}) copy-start(f32[8,1024]{1,0:T(8,128)S(1)} %stack.89.vec_ref) | copy-start | bytes 98308
  24.5 35.5 %copy-start.2 = (bf16[1024,1536]{1,0:T(8,128)(2,1)}, bf16[1024,1536]{1,0:T(8,128)(2,1)S(1)}, u32[]{:S(2)}) copy-start(bf16[1024,1536]{1,0:T(8,128)(2,1)S(1)} %get-tuple-element.165.w_ref.wm0.wm1.wm2) | copy-start | bytes 9437188
  28.2 66.4 %copy-start.23 = (s32[27]{0:T(128)}, s32[27]{0:T(128)S(1)}, u32[]{:S(2)}) copy-start(s32[27]{0:T(128)S(1)} %pad_add_fusion.1.info) | copy-start | bytes 328
  33.0 12.4 %copy-start.47 = (bf16[4096]{0:T(1024)(128)(2,1)S(1)}, bf16[4096]{0:T(1024)(128)(2,1)}, u32[]{:S(2)}) copy-start(bf16[4096]{0:T(1024)(128)(2,1)} %param.31) | copy-start | bytes 24580
  34.4 14.7 %collective-permute-start.3 = (bf16[864,1024]{1,0:T(8,128)(2,1)}, bf16[864,1024]{1,0:T(8,128)(2,1)}, u32[]{:S(2)}, u32[]{:S(2)}) collective-permute-start(bf16[864,1024]{1,0:T(8,128)(2,1)} %pad_maximum_fusion.own_ref.inp_ref), channel_id=1, source_target_pairs={{0,4},{1,5},{2,6},{3,7},{4,0},{5,1},{6,2},{7,3},{8,12},{9,13},{10,... | collective-permute-start | bytes 5308424 | tf_op jit(solution)/shard_map/ppermute | solution.py:1033
  49.1 63.8 %collective-permute-start.6 = (bf16[432,1024]{1,0:T(8,128)(2,1)}, bf16[432,1024]{1,0:T(8,128)(2,1)S(1)}, u32[]{:S(2)}, u32[]{:S(2)}) collective-permute-start(bf16[432,1024]{1,0:T(8,128)(2,1)} %get-tuple-element.170), channel_id=1, source_target_pairs={{2,4},{3,5},{4,2},{5,3},{10,12},{11,13},{12,10},{13,11},{18,20},{1... | collective-permute-start | bytes 2654216 | tf_op jit(solution)/shard_map/ppermute | solution.py:1033
  49.8 63.1 %collective-permute-start.7 = (bf16[432,1024]{1,0:T(8,128)(2,1)}, bf16[432,1024]{1,0:T(8,128)(2,1)S(1)}, u32[]{:S(2)}, u32[]{:S(2)}) collective-permute-start(bf16[432,1024]{1,0:T(8,128)(2,1)} %get-tuple-element.171), channel_id=1, source_target_pairs={{0,1},{1,0},{2,5},{3,4},{4,3},{5,2},{6,7},{7,6},{8,9},{9,8},{10,13... | collective-permute-start | bytes 2654216 | tf_op jit(solution)/shard_map/ppermute | solution.py:1033
  90.9 21.9 %copy-start.12 = (bf16[1728,256]{1,0:T(8,128)(2,1)}, bf16[1728,256]{1,0:T(8,128)(2,1)S(1)}, u32[]{:S(2)}) copy-start(bf16[1728,256]{1,0:T(8,128)(2,1)S(1)} %get-tuple-element.169.ctx_a1_ref.a1.b1.o_ref) | copy-start | bytes 2654212
  90.9 22.1 %copy-start.32 = (bf16[432,1024]{1,0:T(8,128)(2,1)S(1)}, bf16[432,1024]{1,0:T(8,128)(2,1)}, u32[]{:S(2)}) copy-start(bf16[432,1024]{1,0:T(8,128)(2,1)} %get-tuple-element.170) | copy-start | bytes 2654212
  90.9 25.1 %collective-permute-start.5 = (bf16[864,256]{1,0:T(8,128)(2,1)S(1)}, bf16[864,256]{1,0:T(8,128)(2,1)S(1)}, u32[]{:S(2)}, u32[]{:S(2)}) collective-permute-start(bf16[864,256]{1,0:T(8,128)(2,1)S(1)} %dynamic-slice_bitcast_fusion.14), channel_id=1, source_target_pairs={{0,4},{1,5},{2,6},{3,7},{4,0},{5,1},{6,2},{7,3},{8,12},{9,13},{10,... | collective-permute-start | bytes 1327112 | tf_op jit(solution)/shard_map/ppermute | solution.py:1033
  112.9 3.1 collective-permute-start.4
  181.0 13.6 %collective-permute-start.11 = (bf16[2048,1024]{1,0:T(8,128)(2,1)}, bf16[2048,1024]{1,0:T(8,128)(2,1)}, u32[]{:S(2)}, u32[]{:S(2)}) collective-permute-start(bf16[2048,1024]{1,0:T(8,128)(2,1)} %weight_grad.8), channel_id=1, source_target_pairs={{0,4},{1,5},{2,6},{3,7},{4,0},{5,1},{6,2},{7,3},{8,12},{9,13},{10,... | collective-permute-start | bytes 12582920 | tf_op jit(solution)/shard_map/ppermute | solution.py:1033
  189.6 16.9 %collective-permute-start.12 = (bf16[512,4096]{1,0:T(8,128)(2,1)}, bf16[512,4096]{1,0:T(8,128)(2,1)}, u32[]{:S(2)}, u32[]{:S(2)}) collective-permute-start(bf16[512,4096]{1,0:T(8,128)(2,1)} %weight_grad.9), channel_id=1, source_target_pairs={{0,4},{1,5},{2,6},{3,7},{4,0},{5,1},{6,2},{7,3},{8,12},{9,13},{10,... | collective-permute-start | bytes 12582920 | tf_op jit(solution)/shard_map/ppermute | solution.py:1033
  190.0 24.2 %collective-permute-start.10 = (bf16[864,1024]{1,0:T(8,128)(2,1)S(1)}, bf16[864,1024]{1,0:T(8,128)(2,1)}, u32[]{:S(2)}, u32[]{:S(2)}) collective-permute-start(bf16[864,1024]{1,0:T(8,128)(2,1)S(1)} %copy-done.11), channel_id=1, source_target_pairs={{0,4},{1,5},{2,6},{3,7},{4,0},{5,1},{6,2},{7,3},{8,12},{9,13},{10,... | collective-permute-start | bytes 5308424 | tf_op jit(solution)/shard_map/ppermute | solution.py:1033
  193.0 70.9 %collective-permute-start.8 = (bf16[432,1024]{1,0:T(8,128)(2,1)}, bf16[432,1024]{1,0:T(8,128)(2,1)}, u32[]{:S(2)}, u32[]{:S(2)}) collective-permute-start(bf16[432,1024]{1,0:T(8,128)(2,1)} %get-tuple-element.190), channel_id=1, source_target_pairs={{2,4},{3,5},{4,2},{5,3},{10,12},{11,13},{12,10},{13,11},{18,20},{1... | collective-permute-start | bytes 2654216 | tf_op jit(solution)/shard_map/ppermute | solution.py:1033
  194.6 69.3 %collective-permute-start.9 = (bf16[432,1024]{1,0:T(8,128)(2,1)}, bf16[432,1024]{1,0:T(8,128)(2,1)}, u32[]{:S(2)}, u32[]{:S(2)}) collective-permute-start(bf16[432,1024]{1,0:T(8,128)(2,1)} %get-tuple-element.313), channel_id=1, source_target_pairs={{0,1},{1,0},{2,5},{3,4},{4,3},{5,2},{6,7},{7,6},{8,9},{9,8},{10,13... | collective-permute-start | bytes 2654216 | tf_op jit(solution)/shard_map/ppermute | solution.py:1033
  205.0 62.1 %collective-permute-start.15 = (bf16[2,2,2,128,1024]{4,3,1,2,0:T(8,128)(2,1)}, bf16[2,2,2,128,1024]{4,3,1,2,0:T(8,128)(2,1)}, u32[]{:S(2)}, u32[]{:S(2)}) collective-permute-start(bf16[2,2,2,128,1024]{4,3,1,2,0:T(8,128)(2,1)} %bitcast.227), channel_id=1, source_target_pairs={{0,8},{1,9},{2,10},{3,11},{4,12},{5,13},{6,14},{7,15},{8,0},{9,1},... | collective-permute-start | bytes 6291464 | tf_op jit(solution)/shard_map/ppermute | solution.py:1033
  221.7 48.5 %collective-permute-start.14 = (bf16[2,2,2,32,4096]{4,3,1,2,0:T(8,128)(2,1)}, bf16[2,2,2,32,4096]{4,3,1,2,0:T(8,128)(2,1)}, u32[]{:S(2)}, u32[]{:S(2)}) collective-permute-start(bf16[2,2,2,32,4096]{4,3,1,2,0:T(8,128)(2,1)} %bitcast.228), channel_id=1, source_target_pairs={{0,16},{1,17},{2,18},{3,19},{4,20},{5,21},{6,22},{7,23},{8,24},{9,... | collective-permute-start | bytes 6291464 | tf_op jit(solution)/shard_map/ppermute | solution.py:1033
  264.0 14.2 %collective-permute-start.13 = (bf16[2,2,2,32,1024]{4,3,1,2,0:T(8,128)(2,1)S(1)}, bf16[2,2,2,32,1024]{4,3,1,2,0:T(8,128)(2,1)S(1)}, u32[]{:S(2)}, u32[]{:S(2)}) collective-permute-start(bf16[2,2,2,32,1024]{4,3,1,2,0:T(8,128)(2,1)S(1)} %bitcast.257), channel_id=1, source_target_pairs={{0,8},{1,9},{2,10},{3,11},{4,12},{5,13},{6,14},{7,15},{8,0},{9,1},... | collective-permute-start | bytes 1572872 | tf_op jit(solution)/shard_map/ppermute | solution.py:1033
  266.7 37.5 %collective-permute-start.16 = (bf16[3,864,256]{2,1,0:T(8,128)(2,1)}, bf16[3,864,256]{2,1,0:T(8,128)(2,1)S(1)}, u32[]{:S(2)}, u32[]{:S(2)}) collective-permute-start(bf16[3,864,256]{2,1,0:T(8,128)(2,1)} %dynamic-slice_bitcast_fusion.1), channel_id=1, source_target_pairs={{0,4},{1,5},{2,6},{3,7},{4,0},{5,1},{6,2},{7,3},{8,12},{9,13},{10,... | collective-permute-start | bytes 3981320 | tf_op jit(solution)/shard_map/ppermute | solution.py:1033
  280.0 33.7 %collective-permute-start.19 = (bf16[2,2,32,1024]{3,2,0,1:T(8,128)(2,1)}, bf16[2,2,32,1024]{3,2,0,1:T(8,128)(2,1)}, u32[]{:S(2)}, u32[]{:S(2)}) collective-permute-start(bf16[2,2,32,1024]{3,2,0,1:T(8,128)(2,1)} %dynamic-slice_bitcast_fusion.21), channel_id=1, source_target_pairs={{0,16},{1,17},{2,18},{3,19},{4,20},{5,21},{6,22},{7,23},{8,24},{9,... | collective-permute-start | bytes 786440 | tf_op jit(solution)/shard_map/ppermute | solution.py:1033
  282.1 30.0 %collective-permute-start.18 = (bf16[2,2,32,4096]{3,2,0,1:T(8,128)(2,1)}, bf16[2,2,32,4096]{3,2,0,1:T(8,128)(2,1)}, u32[]{:S(2)}, u32[]{:S(2)}) collective-permute-start(bf16[2,2,32,4096]{3,2,0,1:T(8,128)(2,1)} %dynamic-slice_bitcast_fusion.3), channel_id=1, source_target_pairs={{0,8},{1,9},{2,10},{3,11},{4,12},{5,13},{6,14},{7,15},{8,0},{9,1},... | collective-permute-start | bytes 3145736 | tf_op jit(solution)/shard_map/ppermute | solution.py:1033
  283.8 26.7 %collective-permute-start.17 = (bf16[2,2,128,1024]{3,2,0,1:T(8,128)(2,1)}, bf16[2,2,128,1024]{3,2,0,1:T(8,128)(2,1)}, u32[]{:S(2)}, u32[]{:S(2)}) collective-permute-start(bf16[2,2,128,1024]{3,2,0,1:T(8,128)(2,1)} %dynamic-slice_bitcast_fusion.4), channel_id=1, source_target_pairs={{0,16},{1,17},{2,18},{3,19},{4,20},{5,21},{6,22},{7,23},{8,24},{9,... | collective-permute-start | bytes 3145736 | tf_op jit(solution)/shard_map/ppermute | solution.py:1033
  319.4 7.9 %collective-permute-start.20 = (bf16[512,768]{1,0:T(8,128)(2,1)S(1)}, bf16[512,768]{1,0:T(8,128)(2,1)S(1)}, u32[]{:S(2)}, u32[]{:S(2)}) collective-permute-start(bf16[512,768]{1,0:T(8,128)(2,1)S(1)} %weight_grad.12), channel_id=1, source_target_pairs={{0,4},{1,5},{2,6},{3,7},{4,0},{5,1},{6,2},{7,3},{8,12},{9,13},{10,... | collective-permute-start | bytes 2359304 | tf_op jit(solution)/shard_map/ppermute | solution.py:1033
  322.6 38.2 %collective-permute-start.24 = (bf16[2,288,1024]{2,1,0:T(8,128)(2,1)S(1)}, bf16[2,288,1024]{2,1,0:T(8,128)(2,1)}, u32[]{:S(2)}, u32[]{:S(2)}) collective-permute-start(bf16[2,288,1024]{2,1,0:T(8,128)(2,1)S(1)} %dynamic-slice_bitcast_fusion.2), channel_id=1, source_target_pairs={{0,1},{1,0},{2,3},{3,2},{4,5},{5,4},{6,7},{7,6},{8,9},{9,8},{10,11... | collective-permute-start | bytes 3538952 | tf_op jit(solution)/shard_map/ppermute | solution.py:1033
  335.8 27.0 %collective-permute-start.23 = (bf16[2,2,2,32,768]{4,3,2,1,0:T(8,128)(2,1)}, bf16[2,2,2,32,768]{4,3,2,1,0:T(8,128)(2,1)}, u32[]{:S(2)}, u32[]{:S(2)}) collective-permute-start(bf16[2,2,2,32,768]{4,3,2,1,0:T(8,128)(2,1)} %dynamic-slice_bitcast_fusion.19), channel_id=1, source_target_pairs={{0,8},{1,9},{2,10},{3,11},{4,12},{5,13},{6,14},{7,15},{8,0},{9,1},... | collective-permute-start | bytes 1179656 | tf_op jit(solution)/shard_map/ppermute | solution.py:1033
  337.2 26.7 %collective-permute-start.22 = (bf16[2,2,2,32,768]{4,3,2,1,0:T(8,128)(2,1)}, bf16[2,2,2,32,768]{4,3,2,1,0:T(8,128)(2,1)}, u32[]{:S(2)}, u32[]{:S(2)}) collective-permute-start(bf16[2,2,2,32,768]{4,3,2,1,0:T(8,128)(2,1)} %dynamic-slice_bitcast_fusion.20), channel_id=1, source_target_pairs={{0,16},{1,17},{2,18},{3,19},{4,20},{5,21},{6,22},{7,23},{8,24},{9,... | collective-permute-start | bytes 1179656 | tf_op jit(solution)/shard_map/ppermute | solution.py:1033
  360.8 16.6 %collective-permute-start.21 = (bf16[3,864,256]{2,1,0:T(8,128)(2,1)}, bf16[3,864,256]{2,1,0:T(8,128)(2,1)S(1)}, u32[]{:S(2)}, u32[]{:S(2)}) collective-permute-start(bf16[3,864,256]{2,1,0:T(8,128)(2,1)} %dynamic-slice_bitcast_fusion), channel_id=1, source_target_pairs={{0,4},{1,5},{2,6},{3,7},{4,0},{5,1},{6,2},{7,3},{8,12},{9,13},{10,... | collective-permute-start | bytes 3981320 | tf_op jit(solution)/shard_map/ppermute | solution.py:1033
  368.7 7.3 %collective-permute-start.29 = (bf16[512,768]{1,0:T(8,128)(2,1)S(1)}, bf16[512,768]{1,0:T(8,128)(2,1)S(1)}, u32[]{:S(2)}, u32[]{:S(2)}) collective-permute-start(bf16[512,768]{1,0:T(8,128)(2,1)S(1)} %weight_grad.14), channel_id=1, source_target_pairs={{0,4},{1,5},{2,6},{3,7},{4,0},{5,1},{6,2},{7,3},{8,12},{9,13},{10,... | collective-permute-start | bytes 2359304 | tf_op jit(solution)/shard_map/ppermute | solution.py:1033
  369.3 32.5 %collective-permute-start.32 = (bf16[288,1024]{1,0:T(8,128)(2,1)S(1)}, bf16[288,1024]{1,0:T(8,128)(2,1)S(1)}, u32[]{:S(2)}, u32[]{:S(2)}) collective-permute-start(bf16[288,1024]{1,0:T(8,128)(2,1)S(1)} %dynamic-slice_bitcast_fusion.13), channel_id=1, source_target_pairs={{0,2},{1,3},{2,0},{3,1},{4,6},{5,7},{6,4},{7,5},{8,10},{9,11},{10,... | collective-permute-start | bytes 1769480 | tf_op jit(solution)/shard_map/ppermute | solution.py:1033
  370.1 13.3 %collective-permute-start.27 = (bf16[2,2,32,768]{3,2,1,0:T(8,128)(2,1)}, bf16[2,2,32,768]{3,2,1,0:T(8,128)(2,1)}, u32[]{:S(2)}, u32[]{:S(2)}) collective-permute-start(bf16[2,2,32,768]{3,2,1,0:T(8,128)(2,1)} %dynamic-slice_bitcast_fusion.25), channel_id=1, source_target_pairs={{0,16},{1,17},{2,18},{3,19},{4,20},{5,21},{6,22},{7,23},{8,24},{9,... | collective-permute-start | bytes 589832 | tf_op jit(solution)/shard_map/ppermute | solution.py:1033
  370.9 14.9 %collective-permute-start.26 = (bf16[2,2,32,768]{3,2,1,0:T(8,128)(2,1)S(1)}, bf16[2,2,32,768]{3,2,1,0:T(8,128)(2,1)}, u32[]{:S(2)}, u32[]{:S(2)}) collective-permute-start(bf16[2,2,32,768]{3,2,1,0:T(8,128)(2,1)S(1)} %dynamic-slice_bitcast_fusion.26), channel_id=1, source_target_pairs={{0,8},{1,9},{2,10},{3,11},{4,12},{5,13},{6,14},{7,15},{8,0},{9,1},... | collective-permute-start | bytes 589832 | tf_op jit(solution)/shard_map/ppermute | solution.py:1033
  376.0 17.9 %collective-permute-start.30 = (bf16[2,2,2,32,768]{4,3,2,1,0:T(8,128)(2,1)S(1)}, bf16[2,2,2,32,768]{4,3,2,1,0:T(8,128)(2,1)S(1)}, u32[]{:S(2)}, u32[]{:S(2)}) collective-permute-start(bf16[2,2,2,32,768]{4,3,2,1,0:T(8,128)(2,1)S(1)} %dynamic-slice_bitcast_fusion.17), channel_id=1, source_target_pairs={{0,16},{1,17},{2,18},{3,19},{4,20},{5,21},{6,22},{7,23},{8,24},{9,... | collective-permute-start | bytes 1179656 | tf_op jit(solution)/shard_map/ppermute | solution.py:1033
  383.5 10.3 %collective-permute-start.25 = (bf16[2,2,2,32,768]{4,3,2,1,0:T(8,128)(2,1)S(1)}, bf16[2,2,2,32,768]{4,3,2,1,0:T(8,128)(2,1)S(1)}, u32[]{:S(2)}, u32[]{:S(2)}) collective-permute-start(bf16[2,2,2,32,768]{4,3,2,1,0:T(8,128)(2,1)S(1)} %dynamic-slice_bitcast_fusion.18), channel_id=1, source_target_pairs={{0,8},{1,9},{2,10},{3,11},{4,12},{5,13},{6,14},{7,15},{8,0},{9,1},... | collective-permute-start | bytes 1179656 | tf_op jit(solution)/shard_map/ppermute | solution.py:1033
  387.4 32.6 %collective-permute-start.36 = (bf16[432,1024]{1,0:T(8,128)(2,1)S(1)}, bf16[432,1024]{1,0:T(8,128)(2,1)}, u32[]{:S(2)}, u32[]{:S(2)}) collective-permute-start(bf16[432,1024]{1,0:T(8,128)(2,1)S(1)} %get-tuple-element.286), channel_id=1, source_target_pairs={{2,4},{3,5},{4,2},{5,3},{10,12},{11,13},{12,10},{13,11},{18,20},{1... | collective-permute-start | bytes 2654216 | tf_op jit(solution)/shard_map/ppermute | solution.py:1033
  389.0 36.7 %collective-permute-start.37 = (bf16[432,1024]{1,0:T(8,128)(2,1)}, bf16[432,1024]{1,0:T(8,128)(2,1)}, u32[]{:S(2)}, u32[]{:S(2)}) collective-permute-start(bf16[432,1024]{1,0:T(8,128)(2,1)} %get-tuple-element.285), channel_id=1, source_target_pairs={{0,1},{1,0},{2,5},{3,4},{4,3},{5,2},{6,7},{7,6},{8,9},{9,8},{10,13... | collective-permute-start | bytes 2654216 | tf_op jit(solution)/shard_map/ppermute | solution.py:1033
  405.0 11.9 %copy-start.41 = (f32[32,1024]{1,0:T(8,128)S(1)}, f32[32,1024]{1,0:T(8,128)}, u32[]{:S(2)}) copy-start(f32[32,1024]{1,0:T(8,128)} %get-tuple-element.320) | copy-start | bytes 393220
  405.0 11.9 %copy-start.42 = (f32[32,1024]{1,0:T(8,128)S(1)}, f32[32,1024]{1,0:T(8,128)}, u32[]{:S(2)}) copy-start(f32[32,1024]{1,0:T(8,128)} %get-tuple-element.321) | copy-start | bytes 393220
  405.0 11.9 %copy-start.43 = (f32[32,1024]{1,0:T(8,128)S(1)}, f32[32,1024]{1,0:T(8,128)}, u32[]{:S(2)}) copy-start(f32[32,1024]{1,0:T(8,128)} %get-tuple-element.322) | copy-start | bytes 393220
  406.4 2.3 collective-permute-start.33
  407.2 12.8 %collective-permute-start.31 = (bf16[2,2,32,768]{3,2,1,0:T(8,128)(2,1)}, bf16[2,2,32,768]{3,2,1,0:T(8,128)(2,1)}, u32[]{:S(2)}, u32[]{:S(2)}) collective-permute-start(bf16[2,2,32,768]{3,2,1,0:T(8,128)(2,1)} %dynamic-slice_bitcast_fusion.23), channel_id=1, source_target_pairs={{0,8},{1,9},{2,10},{3,11},{4,12},{5,13},{6,14},{7,15},{8,0},{9,1},... | collective-permute-start | bytes 589832 | tf_op jit(solution)/shard_map/ppermute | solution.py:1033
  408.9 17.9 %copy-start.36 = (bf16[2,2,32,768]{3,2,1,0:T(8,128)(2,1)S(1)}, bf16[2,2,32,768]{3,2,1,0:T(8,128)(2,1)}, u32[]{:S(2)}) copy-start(bf16[2,2,32,768]{3,2,1,0:T(8,128)(2,1)} %fusion.15) | copy-start | bytes 589828
  408.9 17.9 %copy-start.37 = (bf16[2,2,32,768]{3,2,1,0:T(8,128)(2,1)S(1)}, bf16[2,2,32,768]{3,2,1,0:T(8,128)(2,1)}, u32[]{:S(2)}) copy-start(bf16[2,2,32,768]{3,2,1,0:T(8,128)(2,1)} %fusion.16) | copy-start | bytes 589828
  409.0 7.1 %collective-permute-start.34 = (f32[2,2,2,32,14]{3,2,4,1,0:T(2,128)S(1)}, f32[2,2,2,32,14]{3,2,4,1,0:T(2,128)S(1)}, u32[]{:S(2)}, u32[]{:S(2)}) collective-permute-start(f32[2,2,2,32,14]{3,2,4,1,0:T(2,128)S(1)} %bitcast.261), channel_id=1, source_target_pairs={{0,8},{1,9},{2,10},{3,11},{4,12},{5,13},{6,14},{7,15},{8,0},{9,1},... | collective-permute-start | bytes 43016 | tf_op jit(solution)/shard_map/ppermute | solution.py:1033
  409.7 10.4 %collective-permute-start.28 = (bf16[2,2,32,768]{3,2,1,0:T(8,128)(2,1)S(1)}, bf16[2,2,32,768]{3,2,1,0:T(8,128)(2,1)S(1)}, u32[]{:S(2)}, u32[]{:S(2)}) collective-permute-start(bf16[2,2,32,768]{3,2,1,0:T(8,128)(2,1)S(1)} %dynamic-slice_bitcast_fusion.24), channel_id=1, source_target_pairs={{0,16},{1,17},{2,18},{3,19},{4,20},{5,21},{6,22},{7,23},{8,24},{9,... | collective-permute-start | bytes 589832 | tf_op jit(solution)/shard_map/ppermute | solution.py:1033
  416.1 3.9 collective-permute-start.35
  425.7 6.0 %collective-permute-start.39 = (f32[2,32,14]{1,0,2:T(2,128)S(1)}, f32[2,32,14]{1,0,2:T(2,128)S(1)}, u32[]{:S(2)}, u32[]{:S(2)}) collective-permute-start(f32[2,32,14]{1,0,2:T(2,128)S(1)} %bitcast.270), channel_id=1, source_target_pairs={{0,1},{1,0},{2,3},{3,2},{4,5},{5,4},{6,7},{7,6},{8,9},{9,8},{10,11... | collective-permute-start | bytes 10760 | tf_op jit(solution)/shard_map/ppermute | solution.py:1033
  427.0 11.3 %collective-permute-start.38 = (bf16[2,32,3072]{2,1,0:T(8,128)(2,1)S(1)}, bf16[2,32,3072]{2,1,0:T(8,128)(2,1)S(1)}, u32[]{:S(2)}, u32[]{:S(2)}) collective-permute-start(bf16[2,32,3072]{2,1,0:T(8,128)(2,1)S(1)} %dynamic-slice_bitcast_fusion.16), channel_id=1, source_target_pairs={{0,1},{1,0},{2,3},{3,2},{4,5},{5,4},{6,7},{7,6},{8,9},{9,8},{10,11... | collective-permute-start | bytes 1179656 | tf_op jit(solution)/shard_map/ppermute | solution.py:1033
  438.3 4.7 %collective-permute-start.41 = (f32[32,14]{0,1:T(8,128)S(1)}, f32[32,14]{0,1:T(8,128)S(1)}, u32[]{:S(2)}, u32[]{:S(2)}) collective-permute-start(f32[32,14]{0,1:T(8,128)S(1)} %bitcast.273), channel_id=1, source_target_pairs={{0,2},{1,3},{2,0},{3,1},{4,6},{5,7},{6,4},{7,5},{8,10},{9,11},{10,... | collective-permute-start | bytes 5384 | tf_op jit(solution)/shard_map/ppermute | solution.py:1033
  438.6 12.8 %collective-permute-start.40 = (bf16[32,3072]{1,0:T(8,128)(2,1)S(1)}, bf16[32,3072]{1,0:T(8,128)(2,1)S(1)}, u32[]{:S(2)}, u32[]{:S(2)}) collective-permute-start(bf16[32,3072]{1,0:T(8,128)(2,1)S(1)} %dynamic-slice_bitcast_fusion.22), channel_id=1, source_target_pairs={{0,2},{1,3},{2,0},{3,1},{4,6},{5,7},{6,4},{7,5},{8,10},{9,11},{10,... | collective-permute-start | bytes 589832 | tf_op jit(solution)/shard_map/ppermute | solution.py:1033
  (42 other events, 161.6 us)
